TPU v7x, 128 devices: a whole 4x4x4 slice. The times are simulated.
128 devices in a mesh: dp: 64 (over z, x, y), fsdp: 2 (over core).
Axes of the slice: x: 4, y: 4, z: 4, core: 2. Of those that a mesh axis runs over, the one named last changes fastest.
Arguments:
- hidden: bfloat16 [128, 256, 768], P('dp', 'fsdp'), may hold values from -6 to 6
- cotangent: bfloat16 [128, 256, 768], P('dp', 'fsdp'), may hold values from -16 to 16
- remaining: int32 [128], P('dp'), may hold values from 1 to 256, 16384 in all
- order: int32 [128, 256], P('dp'), may hold values from 0 to 255, each once within a row
- norm1_gain: bfloat16 [2, 768], P(None, ('dp', 'fsdp')), may hold values from 0.5 to 1.5
- norm1_bias: bfloat16 [2, 768], P(None, ('dp', 'fsdp')), may hold values from -1 to 1
- w_qkv: bfloat16 [2, 768, 2304], P(None, ('dp', 'fsdp')), may hold values from -0.21875 to 0.21875
- bias_qv: bfloat16 [2, 1536], P(None, ('dp', 'fsdp')), may hold values from -1.5 to 1.5
- w_out: bfloat16 [2, 768, 768], P(None, ('dp', 'fsdp')), may hold values from -1.75 to 1.75
- bias_out: bfloat16 [2, 768], P(None, ('dp', 'fsdp')), may hold values from -1.5 to 1.5
- norm2_gain: bfloat16 [2, 768], P(None, ('dp', 'fsdp')), may hold values from 0.5 to 1.5
- norm2_bias: bfloat16 [2, 768], P(None, ('dp', 'fsdp')), may hold values from -1 to 1
- w_up: bfloat16 [2, 768, 3072], P(None, ('dp', 'fsdp')), may hold values from -0.21875 to 0.21875
- bias_up: bfloat16 [2, 3072], P(None, ('dp', 'fsdp')), may hold values from -1.5 to 1.5
- w_down: bfloat16 [2, 3072, 768], P(None, ('dp', 'fsdp')), may hold values from -0.21875 to 0.21875
- bias_down: bfloat16 [2, 768], P(None, ('dp', 'fsdp')), may hold values from -1.5 to 1.5
Outputs:
- output: bfloat16 [128, 256, 768], P('dp', 'fsdp')
- grad_hidden: float32 [128, 256, 768], P('dp', 'fsdp')
- grad_norm1_gain: float32 [2, 768], P(None, ('dp', 'fsdp'))
- grad_norm1_bias: float32 [2, 768], P(None, ('dp', 'fsdp'))
- grad_w_qkv: float32 [2, 768, 2304], P(None, ('dp', 'fsdp'))
- grad_bias_qv: float32 [2, 1536], P(None, ('dp', 'fsdp'))
- grad_w_out: float32 [2, 768, 768], P(None, ('dp', 'fsdp'))
- grad_bias_out: float32 [2, 768], P(None, ('dp', 'fsdp'))
- grad_norm2_gain: float32 [2, 768], P(None, ('dp', 'fsdp'))
- grad_norm2_bias: float32 [2, 768], P(None, ('dp', 'fsdp'))
- grad_w_up: float32 [2, 768, 3072], P(None, ('dp', 'fsdp'))
- grad_bias_up: float32 [2, 3072], P(None, ('dp', 'fsdp'))
- grad_w_down: float32 [2, 3072, 768], P(None, ('dp', 'fsdp'))
- grad_bias_down: float32 [2, 768], P(None, ('dp', 'fsdp'))
Inputs may be any that keep to these rules, and one draw needn't show every extreme that they name: `remaining`: the counts sum to 16384 and one of them is 256. `order`: each row is a permutation of the positions 0 .. 255.
All inputs are finite; a program needn't handle non-finite values. No bound on the sum of `remaining` on one device may be relied on, other than what follows from the above.
Results may differ from a plain program's by a relative error of at most 0.014.
Values may be sent and summed in bfloat16 or wider, within the bound.
A program may use at most 256 MiB of HBM per device.

v0:
```python
import jax
import jax.numpy as jnp
from jax import lax
from jax.sharding import PartitionSpec as P

HEAD = 64
LAYERS = 2


def norm_apply(stream, gain, offset):
    center = stream - jnp.mean(stream, axis=-1, keepdims=True)
    spread = jnp.mean(center * center, axis=-1, keepdims=True)
    return center * lax.rsqrt(spread + 1e-05) * gain + offset


def col_sums(values):
    return jnp.sum(values.astype(jnp.float32), axis=0)


def layer_forward(stream, weights, seq_count, tok_rows, model_width):
    (
        gain_one,
        offset_one,
        w_qkv,
        bias_qv,
        w_out,
        bias_out,
        gain_two,
        offset_two,
        w_up,
        bias_up,
        w_down,
        bias_down,
    ) = weights
    normed = norm_apply(
        stream, gain_one.astype(jnp.float32), offset_one.astype(jnp.float32)
    ).astype(jnp.bfloat16)
    qkv_bias = jnp.concatenate(
        [bias_qv[:model_width], jnp.zeros((model_width,), jnp.bfloat16), bias_qv[model_width:]]
    ).astype(jnp.float32)
    qkv = (jnp.dot(normed, w_qkv, preferred_element_type=jnp.float32) + qkv_bias).astype(
        jnp.bfloat16
    )
    qkv = qkv.reshape(seq_count, tok_rows, 3, model_width // HEAD, HEAD)
    query = qkv[:, :, 0]
    keys, values = (
        lax.all_gather(qkv[:, :, 1], "fsdp", axis=1, tiled=True),
        lax.all_gather(qkv[:, :, 2], "fsdp", axis=1, tiled=True),
    )
    scores = jnp.einsum("sqhe,skhe->shqk", query, keys, preferred_element_type=jnp.float32) * 0.125
    probs = jax.nn.softmax(scores, axis=-1)
    probs_low = probs.astype(jnp.bfloat16)
    attended = jnp.einsum("shqk,skhe->sqhe", probs_low, values, preferred_element_type=jnp.float32)
    attended = attended.astype(jnp.bfloat16).reshape(seq_count * tok_rows, model_width)
    middle = (
        stream
        + jnp.dot(attended, w_out, preferred_element_type=jnp.float32)
        + bias_out.astype(jnp.float32)
    )
    normed_two = norm_apply(
        middle, gain_two.astype(jnp.float32), offset_two.astype(jnp.float32)
    ).astype(jnp.bfloat16)
    hidden_pre = jnp.dot(normed_two, w_up, preferred_element_type=jnp.float32) + bias_up.astype(
        jnp.float32
    )
    active = jax.nn.gelu(hidden_pre, approximate=True).astype(jnp.bfloat16)
    result = (
        middle
        + jnp.dot(active, w_down, preferred_element_type=jnp.float32)
        + bias_down.astype(jnp.float32)
    )
    saved = (
        normed,
        query,
        keys,
        values,
        probs,
        probs_low,
        attended,
        middle,
        normed_two,
        hidden_pre,
        active,
    )
    return (result, saved)


def layer_backward(stream, weights, grad_top, seq_count, tok_rows, model_width):
    (
        gain_one,
        offset_one,
        w_qkv,
        bias_qv,
        w_out,
        bias_out,
        gain_two,
        offset_two,
        w_up,
        bias_up,
        w_down,
        bias_down,
    ) = weights
    unused, saved = layer_forward(stream, weights, seq_count, tok_rows, model_width)
    (
        normed,
        query,
        keys,
        values,
        probs,
        probs_low,
        attended,
        middle,
        normed_two,
        hidden_pre,
        active,
    ) = saved
    grad_z = grad_top.astype(jnp.bfloat16)
    grad_w_down = jnp.einsum("nf,nd->fd", active, grad_z, preferred_element_type=jnp.float32)
    grad_bias_down = col_sums(grad_z)
    grad_active = jnp.einsum("nd,fd->nf", grad_z, w_down, preferred_element_type=jnp.float32)
    gelu_pull = jax.vjp(lambda inner: jax.nn.gelu(inner, approximate=True), hidden_pre)[1]
    grad_pre = gelu_pull(grad_active)[0].astype(jnp.bfloat16)
    grad_w_up = jnp.einsum("nd,nf->df", normed_two, grad_pre, preferred_element_type=jnp.float32)
    grad_bias_up = col_sums(grad_pre)
    grad_normed_two = jnp.einsum("nf,df->nd", grad_pre, w_up, preferred_element_type=jnp.float32)
    norm_pull = jax.vjp(
        norm_apply, middle, gain_two.astype(jnp.float32), offset_two.astype(jnp.float32)
    )[1]
    grad_middle_norm, grad_gain_two, grad_offset_two = norm_pull(grad_normed_two)
    grad_middle = grad_top + grad_middle_norm
    grad_branch = grad_middle.astype(jnp.bfloat16)
    grad_w_out = jnp.einsum("nd,ne->de", attended, grad_branch, preferred_element_type=jnp.float32)
    grad_bias_out = col_sums(grad_branch)
    grad_attended = jnp.einsum("ne,de->nd", grad_branch, w_out, preferred_element_type=jnp.float32)
    grad_attended = grad_attended.astype(jnp.bfloat16).reshape(
        seq_count, tok_rows, model_width // HEAD, HEAD
    )
    grad_probs = jnp.einsum(
        "sqhe,skhe->shqk", grad_attended, values, preferred_element_type=jnp.float32
    )
    value_part = jnp.einsum(
        "shqk,sqhe->skhe", probs_low, grad_attended, preferred_element_type=jnp.float32
    )
    row_dot = jnp.sum(grad_probs * probs, axis=-1, keepdims=True)
    grad_scores = (probs * (grad_probs - row_dot)).astype(jnp.bfloat16)
    grad_query = (
        jnp.einsum("shqk,skhe->sqhe", grad_scores, keys, preferred_element_type=jnp.float32) * 0.125
    )
    key_part = (
        jnp.einsum("shqk,sqhe->skhe", grad_scores, query, preferred_element_type=jnp.float32)
        * 0.125
    )
    grad_keys, grad_values = (
        lax.psum_scatter(
            key_part.astype(jnp.bfloat16), "fsdp", scatter_dimension=1, tiled=True
        ).astype(jnp.float32),
        lax.psum_scatter(
            value_part.astype(jnp.bfloat16), "fsdp", scatter_dimension=1, tiled=True
        ).astype(jnp.float32),
    )
    grad_qkv = jnp.stack([grad_query, grad_keys, grad_values], axis=2).astype(jnp.bfloat16)
    grad_qkv = grad_qkv.reshape(seq_count * tok_rows, 3 * model_width)
    grad_w_qkv = jnp.einsum("nd,nk->dk", normed, grad_qkv, preferred_element_type=jnp.float32)
    qkv_sums = col_sums(grad_qkv)
    grad_bias_qv = jnp.concatenate([qkv_sums[:model_width], qkv_sums[2 * model_width :]])
    grad_normed = jnp.einsum("nk,dk->nd", grad_qkv, w_qkv, preferred_element_type=jnp.float32)
    norm_pull_one = jax.vjp(
        norm_apply, stream, gain_one.astype(jnp.float32), offset_one.astype(jnp.float32)
    )[1]
    grad_stream_norm, grad_gain_one, grad_offset_one = norm_pull_one(grad_normed)
    grad_stream = grad_middle + grad_stream_norm
    grads = (
        grad_gain_one,
        grad_offset_one,
        grad_w_qkv,
        grad_bias_qv,
        grad_w_out,
        grad_bias_out,
        grad_gain_two,
        grad_offset_two,
        grad_w_up,
        grad_bias_up,
        grad_w_down,
        grad_bias_down,
    )
    return (grad_stream, grads)


def shards(
    hidden,
    cotangent,
    remaining,
    order,
    norm1_gain,
    norm1_bias,
    w_qkv,
    bias_qv,
    w_out,
    bias_out,
    norm2_gain,
    norm2_bias,
    w_up,
    bias_up,
    w_down,
    bias_down,
):
    seq_total, half_rows, model_width = hidden.shape
    seq_len = order.shape[1]

    def fetch(layer_index):
        return (
            lax.all_gather(norm1_gain[layer_index], ("dp", "fsdp"), axis=0, tiled=True),
            lax.all_gather(norm1_bias[layer_index], ("dp", "fsdp"), axis=0, tiled=True),
            lax.all_gather(w_qkv[layer_index], ("dp", "fsdp"), axis=0, tiled=True),
            lax.all_gather(bias_qv[layer_index], ("dp", "fsdp"), axis=0, tiled=True),
            lax.all_gather(w_out[layer_index], ("dp", "fsdp"), axis=0, tiled=True),
            lax.all_gather(bias_out[layer_index], ("dp", "fsdp"), axis=0, tiled=True),
            lax.all_gather(norm2_gain[layer_index], ("dp", "fsdp"), axis=0, tiled=True),
            lax.all_gather(norm2_bias[layer_index], ("dp", "fsdp"), axis=0, tiled=True),
            lax.all_gather(w_up[layer_index], ("dp", "fsdp"), axis=0, tiled=True),
            lax.all_gather(bias_up[layer_index], ("dp", "fsdp"), axis=0, tiled=True),
            lax.all_gather(w_down[layer_index], ("dp", "fsdp"), axis=0, tiled=True),
            lax.all_gather(bias_down[layer_index], ("dp", "fsdp"), axis=0, tiled=True),
        )

    local_in, local_cot = (hidden, cotangent)
    places = lax.axis_index("fsdp") * half_rows + jnp.arange(half_rows, dtype=jnp.int32)
    live = jnp.arange(seq_len, dtype=jnp.int32)[None, :] >= (seq_len - remaining)[:, None]
    matched = (order[:, :, None] == places[None, None, :]) & live[:, :, None]
    mask = jnp.any(matched, axis=1).astype(jnp.float32)
    upstream = (local_cot.astype(jnp.float32) * mask[:, :, None]).reshape(
        seq_total * half_rows, model_width
    )
    stream = local_in.astype(jnp.float32).reshape(seq_total * half_rows, model_width)
    inputs = []
    for layer_index in range(LAYERS):
        weights = fetch(layer_index)
        inputs.append(stream)
        stream, unused = layer_forward(stream, weights, seq_total, half_rows, model_width)
    output = stream.astype(jnp.bfloat16).reshape(seq_total, half_rows, model_width)
    grad_stream = upstream
    shard_grads = [None] * LAYERS
    for layer_index in reversed(range(LAYERS)):
        weights = fetch(layer_index)
        grad_stream, grads = layer_backward(
            inputs[layer_index], weights, grad_stream, seq_total, half_rows, model_width
        )
        shard_grads[layer_index] = (
            lax.psum_scatter(grads[0], ("dp", "fsdp"), scatter_dimension=0, tiled=True),
            lax.psum_scatter(grads[1], ("dp", "fsdp"), scatter_dimension=0, tiled=True),
            lax.psum_scatter(grads[2], ("dp", "fsdp"), scatter_dimension=0, tiled=True),
            lax.psum_scatter(grads[3], ("dp", "fsdp"), scatter_dimension=0, tiled=True),
            lax.psum_scatter(grads[4], ("dp", "fsdp"), scatter_dimension=0, tiled=True),
            lax.psum_scatter(grads[5], ("dp", "fsdp"), scatter_dimension=0, tiled=True),
            lax.psum_scatter(grads[6], ("dp", "fsdp"), scatter_dimension=0, tiled=True),
            lax.psum_scatter(grads[7], ("dp", "fsdp"), scatter_dimension=0, tiled=True),
            lax.psum_scatter(grads[8], ("dp", "fsdp"), scatter_dimension=0, tiled=True),
            lax.psum_scatter(grads[9], ("dp", "fsdp"), scatter_dimension=0, tiled=True),
            lax.psum_scatter(grads[10], ("dp", "fsdp"), scatter_dimension=0, tiled=True),
            lax.psum_scatter(grads[11], ("dp", "fsdp"), scatter_dimension=0, tiled=True),
        )
    results = tuple(
        (
            jnp.stack([shard_grads[layer_index][member] for layer_index in range(LAYERS)])
            for member in range(12)
        )
    )
    grad_hidden = grad_stream.reshape(seq_total, half_rows, model_width)
    return (
        output,
        grad_hidden,
        results[0],
        results[1],
        results[2],
        results[3],
        results[4],
        results[5],
        results[6],
        results[7],
        results[8],
        results[9],
        results[10],
        results[11],
    )


def solution(mesh):
    placed = (
        P("dp", "fsdp", None),
        P("dp", "fsdp", None),
        P("dp"),
        P("dp", None),
        P(None, ("dp", "fsdp")),
        P(None, ("dp", "fsdp")),
        P(None, ("dp", "fsdp"), None),
        P(None, ("dp", "fsdp")),
        P(None, ("dp", "fsdp"), None),
        P(None, ("dp", "fsdp")),
        P(None, ("dp", "fsdp")),
        P(None, ("dp", "fsdp")),
        P(None, ("dp", "fsdp"), None),
        P(None, ("dp", "fsdp")),
        P(None, ("dp", "fsdp"), None),
        P(None, ("dp", "fsdp")),
    )
    return jax.shard_map(
        shards,
        mesh=mesh,
        in_specs=placed,
        out_specs=(
            P("dp", "fsdp", None),
            P("dp", "fsdp", None),
            P(None, ("dp", "fsdp")),
            P(None, ("dp", "fsdp")),
            P(None, ("dp", "fsdp"), None),
            P(None, ("dp", "fsdp")),
            P(None, ("dp", "fsdp"), None),
            P(None, ("dp", "fsdp")),
            P(None, ("dp", "fsdp")),
            P(None, ("dp", "fsdp")),
            P(None, ("dp", "fsdp"), None),
            P(None, ("dp", "fsdp")),
            P(None, ("dp", "fsdp"), None),
            P(None, ("dp", "fsdp")),
        ),
        check_vma=False,
    )
```

profile of v0, /device:TPU:1, one launch (start us, length us, event | category | flops | bytes accessed | tf_op | source)
XLA Modules:
  0.0 1893.1 jit_solution(10249592819128729319)
XLA Ops:
  25.7 69.7 %all-reduce.45 = (bf16[768]{0:T(1024)(128)(2,1)S(1)}, bf16[768]{0:T(1024)(128)(2,1)S(1)}, bf16[768]{0:T(1024)(128)(2,1)S(1)}, bf16[1536]{0:T(1024)(128)(2,1)S(1)...) all-reduce(bf16[768]{0:T(1024)(128)(2,1)S(1)} %dynamic-update-slice, ...), channel_id=9, replica_groups=mesh['dp'=64,'fsdp'=2] {'dp','fsdp'}, use_global_device_ids=true, to_apply=%add.3 | all-reduce | flops 18432 | bytes 73728
  106.0 4.1 fusion.30
  121.9 8.4 fusion.95
  130.8 19.4 %all-gather.39.cloned.1.call-done = bf16[1,768,768]{2,0,1:T(2,128)(2,1)} async-done(((bf16[1,6,768]{2,0,1:T(2,128)(2,1)}), bf16[1,768,768]{2,0,1:T(2,128)(2,1)}) %all-gather.39.cloned.1.call-update) | async-done | bytes 1179664 | tf_op jit(solution)/shard_map/all_gather | solution.py:216
  152.7 69.4 %all-gather.41.cloned.1.call-done = bf16[1,768,3072]{2,0,1:T(2,128)(2,1)} async-done(((bf16[1,6,3072]{2,0,1:T(2,128)(2,1)}), bf16[1,768,3072]{2,0,1:T(2,128)(2,1)}) %all-gather.41.cloned.1.call-update) | async-done | bytes 4718608 | tf_op jit(solution)/shard_map/all_gather | solution.py:220
  222.2 7.3 fusion.24
  229.5 60.3 %all-gather.43.cloned.1.call-done = bf16[1,3072,768]{2,1,0:T(8,128)(2,1)} async-done(((bf16[1,24,768]{2,1,0:T(8,128)(2,1)}), bf16[1,3072,768]{2,1,0:T(8,128)(2,1)}) %all-gather.43.cloned.1.call-update) | async-done | bytes 4718608 | tf_op jit(solution)/shard_map/all_gather | solution.py:222
  289.8 5.3 fusion.198
  295.4 64.3 %all-gather.45.cloned.1.call-done = bf16[1,768,2304]{2,0,1:T(2,128)(2,1)} async-done(((bf16[1,6,2304]{2,0,1:T(2,128)(2,1)}), bf16[1,768,2304]{2,0,1:T(2,128)(2,1)}) %all-gather.45.cloned.1.call-update) | async-done | bytes 3538960 | tf_op jit(solution)/shard_map/all_gather | solution.py:214
  359.6 5.2 fusion.31
  381.9 8.4 fusion.96
  390.7 34.6 %all-gather.47.cloned.1.call-done = bf16[1,768,768]{2,0,1:T(2,128)(2,1)} async-done(((bf16[1,6,768]{2,0,1:T(2,128)(2,1)}), bf16[1,768,768]{2,0,1:T(2,128)(2,1)}) %all-gather.47.cloned.1.call-update) | async-done | bytes 1179664 | tf_op jit(solution)/shard_map/all_gather | solution.py:216
  429.3 67.9 %all-gather.49.cloned.1.call-done = bf16[1,768,3072]{2,0,1:T(2,128)(2,1)} async-done(((bf16[1,6,3072]{2,0,1:T(2,128)(2,1)}), bf16[1,768,3072]{2,0,1:T(2,128)(2,1)}) %all-gather.49.cloned.1.call-update) | async-done | bytes 4718608 | tf_op jit(solution)/shard_map/all_gather | solution.py:220
  497.2 7.3 fusion.27
  504.5 61.1 %all-gather.51.cloned.1.call-done = bf16[1,3072,768]{2,1,0:T(8,128)(2,1)} async-done(((bf16[1,24,768]{2,1,0:T(8,128)(2,1)}), bf16[1,3072,768]{2,1,0:T(8,128)(2,1)}) %all-gather.51.cloned.1.call-update) | async-done | bytes 4718608 | tf_op jit(solution)/shard_map/all_gather | solution.py:222
  565.5 7.7 convert_reduce_fusion
  579.1 8.3 fusion.74
  591.2 4.0 reshape.448
  601.3 4.7 copy.112
  605.9 4.0 reshape.446
  625.4 5.4 multiply_reduce_fusion.6
  642.3 8.3 fusion.75
  650.7 3.8 copy.118
  654.5 4.0 reshape.452
  664.3 4.7 copy.116
  669.0 4.0 reshape.450
  691.9 5.3 fusion.182
  699.5 7.7 fusion.165
  708.2 7.6 fusion.164
  718.8 5.2 fusion.163
  726.0 4.1 fusion.100
  730.2 5.2 fusion.162
  735.4 4.0 fusion.97
  739.4 421.0 %fusion.183 = (f32[8,2304]{1,0:T(8,128)S(1)}, f32[8,2304]{1,0:T(8,128)S(1)}, f32[8,768]{1,0:T(8,128)S(1)}, f32[8,768]{1,0:T(8,128)}, f32[8,3072]{1,0:T(8,128)S(1)}, /*index=5*/f32[8,3072]{1,0:T(8,128)}) fusion(f32[768,2304]{1,0:T(8,128)} %fusion.100, f32[768,2304]{1,0:T(8,128)} %fusion.97, f32[768,768]{1,0:T(8,128)} %fusion.131, f32[768,768]{1,0:T(8,128)} %fusion.134, ...), kind=kCustom, calls=%all-reduce-scatter.6 | all-reduce-scatter fusion | flops 12582913 | bytes 38141952
  1165.0 3.8 collective-permute-start.95
  1177.2 12.0 collective-permute-start.118
  1189.2 7.7 collective-permute-start.117
  1216.2 4.7 collective-permute-start.108
  1295.6 4.4 collective-permute-start.74
  1299.9 6.0 fusion.92
  1335.3 13.8 concatenate.32
  1355.7 27.2 %concatenate.31 = f32[262,768]{1,0:T(8,128)S(1)} concatenate(f32[6,768]{1,0:T(8,128)S(1)} %copy-done.149, f32[8,768]{1,0:T(8,128)} %copy-done.194, f32[8,768]{1,0:T(8,128)} %copy-done.196, f32[8,768]{1,0:T(8,128)} %copy-done.198, f32[8,768]{1,0:T(8,128)} %copy-done.200, f32[8,768]{1,0:T(8,128)} %copy-done.202, f32[8,768]{1,0:T(8,128)} %copy-done.204, f32[8,768]{1,0:T(8,128)} %copy-done.206, ...), dimensions={0} | concatenate | bytes 1609728
  1395.6 3.8 collective-permute-start.53
  1426.3 4.2 collective-permute-start.42
  1505.6 5.5 collective-permute-start.10
  1520.3 4.3 collective-permute-start.5
  1529.9 4.1 collective-permute-start.2
  1552.1 6.0 collective-permute-start.186
  1580.3 4.2 collective-permute-start.176
  1598.0 4.1 collective-permute-start.170
  1604.2 11.1 collective-permute-start.168
  1618.0 4.0 collective-permute-start.165
  1625.1 4.6 collective-permute-start.163
  1655.5 5.5 collective-permute-start.149
  1664.2 3.9 collective-permute-start.147
  1679.1 31.7 %concatenate.30 = f32[262,2304]{1,0:T(8,128)S(1)} concatenate(f32[6,2304]{1,0:T(8,128)} %copy-done.108, f32[8,2304]{1,0:T(8,128)S(1)} %collective-permute-done.62, f32[8,2304]{1,0:T(8,128)} %copy-done.106, f32[8,2304]{1,0:T(8,128)} %copy-done.107, f32[8,2304]{1,0:T(8,128)} %copy-done.109, f32[8,2304]{1,0:T(8,128)} %copy-done.110, f32[8,2304]{1,0:T(8,128)} %copy-done.111, ...), dimensions={0} | concatenate | bytes 4829184
  1713.9 5.5 collective-permute-start.141
  1722.4 8.4 collective-permute-start.139
  1730.8 4.0 collective-permute-start.138
  1734.8 32.6 %concatenate.29 = f32[262,2304]{1,0:T(8,128)S(1)} concatenate(f32[6,2304]{1,0:T(8,128)} %copy-done.105, f32[8,2304]{1,0:T(8,128)} %collective-permute-done.30, f32[8,2304]{1,0:T(8,128)} %collective-permute-done.29, f32[8,2304]{1,0:T(8,128)} %collective-permute-done.28, f32[8,2304]{1,0:T(8,128)} %collective-permute-done.27, f32[8,2304]{1,0:T(8,128)} %collective-permute-done.26, ...), dimensions={0} | concatenate | bytes 4829184
  1777.8 5.8 collective-permute-start.132
  1785.5 4.6 collective-permute-start.130
  1795.3 32.4 %concatenate.34 = f32[262,3072]{1,0:T(8,128)S(1)} concatenate(f32[6,3072]{1,0:T(8,128)} %copy-done.62, f32[8,3072]{1,0:T(8,128)S(1)} %collective-permute-done.190, f32[8,3072]{1,0:T(8,128)} %copy-done.61, f32[8,3072]{1,0:T(8,128)} %copy-done.63, f32[8,3072]{1,0:T(8,128)} %copy-done.64, f32[8,3072]{1,0:T(8,128)} %copy-done.65, f32[8,3072]{1,0:T(8,128)} %copy-done.66, ...), dimensions={0} | concatenate | bytes 6438912
  1827.8 55.0 %concatenate.33 = f32[262,3072]{1,0:T(8,128)} concatenate(f32[6,3072]{1,0:T(8,128)S(1)} %collective-permute-done.159, f32[8,3072]{1,0:T(8,128)} %copy-done.90, f32[8,3072]{1,0:T(8,128)} %copy-done.92, f32[8,3072]{1,0:T(8,128)} %copy-done.94, f32[8,3072]{1,0:T(8,128)} %copy-done.95, f32[8,3072]{1,0:T(8,128)} %copy-done.96, f32[8,3072]{1,0:T(8,128)} %copy-done.97, ...), dimensions={0} | concatenate | bytes 6438912
  (1118 shorter events, 536.4 us)
Async XLA Ops:
  7.2 98.8 %all-gather.37.cloned.1.call-start = ((), (), s32[]{:S(2)}) async-start(), calls=%async_computation.8 | async-start | bytes 7133184 | tf_op jit(solution)/shard_map/all_gather | solution.py:214
  8.9 141.3 %all-gather.39.cloned.1.call-start = ((), (), s32[]{:S(2)}) async-start(), calls=%async_computation.9 | async-start | bytes 2377728 | tf_op jit(solution)/shard_map/all_gather | solution.py:216
  10.4 211.8 %all-gather.41.cloned.1.call-start = ((), (), s32[]{:S(2)}) async-start(), calls=%async_computation.10 | async-start | bytes 9510912 | tf_op jit(solution)/shard_map/all_gather | solution.py:220
  12.2 277.5 %all-gather.43.cloned.1.call-start = ((), (), s32[]{:S(2)}) async-start(), calls=%async_computation.11 | async-start | bytes 4755456 | tf_op jit(solution)/shard_map/all_gather | solution.py:222
  13.7 345.9 %all-gather.45.cloned.1.call-start = ((), (), s32[]{:S(2)}) async-start(), calls=%async_computation.12 | async-start | bytes 7133184 | tf_op jit(solution)/shard_map/all_gather | solution.py:214
  14.3 410.9 %all-gather.47.cloned.1.call-start = ((), (), s32[]{:S(2)}) async-start(), calls=%async_computation.13 | async-start | bytes 2377728 | tf_op jit(solution)/shard_map/all_gather | solution.py:216
  14.9 482.3 %all-gather.49.cloned.1.call-start = ((), (), s32[]{:S(2)}) async-start(), calls=%async_computation.14 | async-start | bytes 9510912 | tf_op jit(solution)/shard_map/all_gather | solution.py:220
  15.6 549.9 %all-gather.51.cloned.1.call-start = ((), (), s32[]{:S(2)}) async-start(), calls=%async_computation.15 | async-start | bytes 4755456 | tf_op jit(solution)/shard_map/all_gather | solution.py:222
  16.4 596.1 %reduce-scatter.33.cloned.1.call-start = ((), (), s32[]{:S(2)}) async-start(), calls=%async_computation.17 | async-start | bytes 1179648
  595.3 23.3 %reduce-scatter.31.cloned.1.call-start = ((), (), s32[]{:S(2)}) async-start(), calls=%async_computation.16 | async-start | bytes 1179648
  609.9 71.0 %reduce-scatter.37.cloned.1.call-start = ((), (), s32[]{:S(2)}) async-start(), calls=%async_computation.19 | async-start | bytes 1179648
  658.6 27.1 %reduce-scatter.35.cloned.1.call-start = ((), (), s32[]{:S(2)}) async-start(), calls=%async_computation.18 | async-start | bytes 1179648
  673.0 710.6 %all-reduce.49.cloned.1.call-start = ((), (), s32[]{:S(2)}) async-start(), calls=%async_computation.20 | async-start | bytes 180224
  699.0 1185.6 %reduce-scatter.29.cloned.1.call-start = ((), (), s32[]{:S(2)}) async-start(), calls=%async_computation.7 | async-start | bytes 9510912 | tf_op jit(solution)/shard_map/reduce_scatter | solution.py:259
  707.2 1177.3 %reduce-scatter.27.cloned.1.call-start = ((), (), s32[]{:S(2)}) async-start(), calls=%async_computation.6 | async-start | bytes 9510912 | tf_op jit(solution)/shard_map/reduce_scatter | solution.py:259
  1171.7 17.5 collective-permute-start.122
  1173.2 23.7 %collective-permute-start.121 = (f32[8,768]{1,0:T(8,128)S(1)}, f32[8,768]{1,0:T(8,128)S(1)}, u32[]{:S(2)}, u32[]{:S(2)}) collective-permute-start(f32[8,768]{1,0:T(8,128)S(1)} %get-tuple-element.127), channel_id=1, source_target_pairs={{0,26},{1,27},{2,28},{3,29},{4,30},{5,31},{6,32},{7,33},{8,34},{9,... | collective-permute-start | bytes 73736
  1174.5 25.2 %collective-permute-start.120 = (f32[8,768]{1,0:T(8,128)S(1)}, f32[8,768]{1,0:T(8,128)S(1)}, u32[]{:S(2)}, u32[]{:S(2)}) collective-permute-start(f32[8,768]{1,0:T(8,128)S(1)} %get-tuple-element.127), channel_id=1, source_target_pairs={{0,25},{1,26},{2,27},{3,28},{4,29},{5,30},{6,31},{7,32},{8,33},{9,... | collective-permute-start | bytes 73736
  1175.9 26.0 %collective-permute-start.119 = (f32[8,768]{1,0:T(8,128)S(1)}, f32[8,768]{1,0:T(8,128)S(1)}, u32[]{:S(2)}, u32[]{:S(2)}) collective-permute-start(f32[8,768]{1,0:T(8,128)S(1)} %get-tuple-element.127), channel_id=1, source_target_pairs={{0,24},{1,25},{2,26},{3,27},{4,28},{5,29},{6,30},{7,31},{8,32},{9,... | collective-permute-start | bytes 73736
  1177.2 26.9 %collective-permute-start.118 = (f32[8,768]{1,0:T(8,128)S(1)}, f32[8,768]{1,0:T(8,128)S(1)}, u32[]{:S(2)}, u32[]{:S(2)}) collective-permute-start(f32[8,768]{1,0:T(8,128)S(1)} %get-tuple-element.127), channel_id=1, source_target_pairs={{0,23},{1,24},{2,25},{3,26},{4,27},{5,28},{6,29},{7,30},{8,31},{9,... | collective-permute-start | bytes 73736
  1189.2 17.1 collective-permute-start.117
  1287.6 18.5 collective-permute-start.78
  1289.1 18.8 collective-permute-start.77
  1290.9 19.8 %collective-permute-start.76 = (f32[8,768]{1,0:T(8,128)}, f32[8,768]{1,0:T(8,128)S(1)}, u32[]{:S(2)}, u32[]{:S(2)}) collective-permute-start(f32[8,768]{1,0:T(8,128)} %get-tuple-element.128), channel_id=1, source_target_pairs={{0,13},{1,14},{2,15},{3,16},{4,17},{5,18},{6,19},{7,20},{8,21},{9,... | collective-permute-start | bytes 73736
  1292.7 19.3 %collective-permute-start.75 = (f32[8,768]{1,0:T(8,128)}, f32[8,768]{1,0:T(8,128)S(1)}, u32[]{:S(2)}, u32[]{:S(2)}) collective-permute-start(f32[8,768]{1,0:T(8,128)} %get-tuple-element.128), channel_id=1, source_target_pairs={{0,12},{1,13},{2,14},{3,15},{4,16},{5,17},{6,18},{7,19},{8,20},{9,... | collective-permute-start | bytes 73736
  1295.6 19.2 %collective-permute-start.74 = (f32[8,768]{1,0:T(8,128)}, f32[8,768]{1,0:T(8,128)S(1)}, u32[]{:S(2)}, u32[]{:S(2)}) collective-permute-start(f32[8,768]{1,0:T(8,128)} %get-tuple-element.128), channel_id=1, source_target_pairs={{0,11},{1,12},{2,13},{3,14},{4,15},{5,16},{6,17},{7,18},{8,19},{9,... | collective-permute-start | bytes 73736
  1318.2 30.8 %collective-permute-start.68 = (f32[8,768]{1,0:T(8,128)}, f32[8,768]{1,0:T(8,128)}, u32[]{:S(2)}, u32[]{:S(2)}) collective-permute-start(f32[8,768]{1,0:T(8,128)} %get-tuple-element.128), channel_id=1, source_target_pairs={{0,5},{1,6},{2,7},{3,8},{4,9},{5,10},{6,11},{7,12},{8,13},{9,14},{... | collective-permute-start | bytes 73736
  1321.9 28.5 %collective-permute-start.67 = (f32[8,768]{1,0:T(8,128)}, f32[8,768]{1,0:T(8,128)}, u32[]{:S(2)}, u32[]{:S(2)}) collective-permute-start(f32[8,768]{1,0:T(8,128)} %get-tuple-element.128), channel_id=1, source_target_pairs={{0,4},{1,5},{2,6},{3,7},{4,8},{5,9},{6,10},{7,11},{8,12},{9,13},{1... | collective-permute-start | bytes 73736
  1324.9 26.8 %collective-permute-start.66 = (f32[8,768]{1,0:T(8,128)}, f32[8,768]{1,0:T(8,128)}, u32[]{:S(2)}, u32[]{:S(2)}) collective-permute-start(f32[8,768]{1,0:T(8,128)} %get-tuple-element.128), channel_id=1, source_target_pairs={{0,3},{1,4},{2,5},{3,6},{4,7},{5,8},{6,9},{7,10},{8,11},{9,12},{10... | collective-permute-start | bytes 73736
  1328.4 24.6 %collective-permute-start.65 = (f32[8,768]{1,0:T(8,128)}, f32[8,768]{1,0:T(8,128)}, u32[]{:S(2)}, u32[]{:S(2)}) collective-permute-start(f32[8,768]{1,0:T(8,128)} %get-tuple-element.128), channel_id=1, source_target_pairs={{0,2},{1,3},{2,4},{3,5},{4,6},{5,7},{6,8},{7,9},{8,10},{9,11},{10,... | collective-permute-start | bytes 73736
  1330.4 23.9 %collective-permute-start.64 = (f32[8,768]{1,0:T(8,128)}, f32[8,768]{1,0:T(8,128)}, u32[]{:S(2)}, u32[]{:S(2)}) collective-permute-start(f32[8,768]{1,0:T(8,128)} %get-tuple-element.128), channel_id=1, source_target_pairs={{0,1},{1,2},{2,3},{3,4},{4,5},{5,6},{6,7},{7,8},{8,9},{9,10},{10,1... | collective-permute-start | bytes 73736
  1349.1 39.4 %collective-permute-start.62 = (f32[8,2304]{1,0:T(8,128)}, f32[8,2304]{1,0:T(8,128)S(1)}, u32[]{:S(2)}, u32[]{:S(2)}) collective-permute-start(f32[8,2304]{1,0:T(8,128)} %copy-done.45), channel_id=1, source_target_pairs={{0,31},{1,32},{2,33},{3,34},{4,35},{5,36},{6,37},{7,38},{8,39},{9,... | collective-permute-start | bytes 221192
  1350.4 40.1 %collective-permute-start.61 = (f32[8,2304]{1,0:T(8,128)}, f32[8,2304]{1,0:T(8,128)S(1)}, u32[]{:S(2)}, u32[]{:S(2)}) collective-permute-start(f32[8,2304]{1,0:T(8,128)} %copy-done.45), channel_id=1, source_target_pairs={{0,30},{1,31},{2,32},{3,33},{4,34},{5,35},{6,36},{7,37},{8,38},{9,... | collective-permute-start | bytes 221192
  1351.7 41.1 %collective-permute-start.60 = (f32[8,2304]{1,0:T(8,128)}, f32[8,2304]{1,0:T(8,128)S(1)}, u32[]{:S(2)}, u32[]{:S(2)}) collective-permute-start(f32[8,2304]{1,0:T(8,128)} %copy-done.45), channel_id=1, source_target_pairs={{0,29},{1,30},{2,31},{3,32},{4,33},{5,34},{6,35},{7,36},{8,37},{9,... | collective-permute-start | bytes 221192
  1353.0 32.0 %collective-permute-start.63 = (f32[6,2304]{1,0:T(8,128)S(1)}, f32[6,2304]{1,0:T(8,128)S(1)}, u32[]{:S(2)}, u32[]{:S(2)}) collective-permute-start(f32[6,2304]{1,0:T(8,128)S(1)} %slice.219), channel_id=1, source_target_pairs={{0,32},{1,33},{2,34},{3,35},{4,36},{5,37},{6,38},{7,39},{8,40},{9,... | collective-permute-start | bytes 165896
  1354.4 32.8 %collective-permute-start.31 = (f32[6,2304]{1,0:T(8,128)S(1)}, f32[6,2304]{1,0:T(8,128)S(1)}, u32[]{:S(2)}, u32[]{:S(2)}) collective-permute-start(f32[6,2304]{1,0:T(8,128)S(1)} %slice.218), channel_id=1, source_target_pairs={{0,32},{1,33},{2,34},{3,35},{4,36},{5,37},{6,38},{7,39},{8,40},{9,... | collective-permute-start | bytes 165896
  1520.3 16.8 collective-permute-start.5
  1539.8 18.3 collective-permute-start.190
  1541.1 18.3 collective-permute-start.189
  1591.0 24.3 %collective-permute-start.172 = (f32[8,3072]{1,0:T(8,128)S(1)}, f32[8,3072]{1,0:T(8,128)S(1)}, u32[]{:S(2)}, u32[]{:S(2)}) collective-permute-start(f32[8,3072]{1,0:T(8,128)S(1)} %get-tuple-element.129), channel_id=1, source_target_pairs={{0,13},{1,14},{2,15},{3,16},{4,17},{5,18},{6,19},{7,20},{8,21},{9,... | collective-permute-start | bytes 294920
  1594.4 22.3 %collective-permute-start.171 = (f32[8,3072]{1,0:T(8,128)S(1)}, f32[8,3072]{1,0:T(8,128)S(1)}, u32[]{:S(2)}, u32[]{:S(2)}) collective-permute-start(f32[8,3072]{1,0:T(8,128)S(1)} %get-tuple-element.129), channel_id=1, source_target_pairs={{0,12},{1,13},{2,14},{3,15},{4,16},{5,17},{6,18},{7,19},{8,20},{9,... | collective-permute-start | bytes 294920
  1598.0 19.9 %collective-permute-start.170 = (f32[8,3072]{1,0:T(8,128)S(1)}, f32[8,3072]{1,0:T(8,128)S(1)}, u32[]{:S(2)}, u32[]{:S(2)}) collective-permute-start(f32[8,3072]{1,0:T(8,128)S(1)} %get-tuple-element.129), channel_id=1, source_target_pairs={{0,11},{1,12},{2,13},{3,14},{4,15},{5,16},{6,17},{7,18},{8,19},{9,... | collective-permute-start | bytes 294920
  1602.2 19.9 %collective-permute-start.169 = (f32[8,3072]{1,0:T(8,128)S(1)}, f32[8,3072]{1,0:T(8,128)S(1)}, u32[]{:S(2)}, u32[]{:S(2)}) collective-permute-start(f32[8,3072]{1,0:T(8,128)S(1)} %get-tuple-element.129), channel_id=1, source_target_pairs={{0,10},{1,11},{2,12},{3,13},{4,14},{5,15},{6,16},{7,17},{8,18},{9,... | collective-permute-start | bytes 294920
  1604.2 20.8 %collective-permute-start.168 = (f32[8,3072]{1,0:T(8,128)S(1)}, f32[8,3072]{1,0:T(8,128)S(1)}, u32[]{:S(2)}, u32[]{:S(2)}) collective-permute-start(f32[8,3072]{1,0:T(8,128)S(1)} %get-tuple-element.129), channel_id=1, source_target_pairs={{0,9},{1,10},{2,11},{3,12},{4,13},{5,14},{6,15},{7,16},{8,17},{9,1... | collective-permute-start | bytes 294920
  1618.0 17.0 collective-permute-start.165
  1653.6 17.1 collective-permute-start.150
  1655.5 17.5 collective-permute-start.149
  1664.2 46.7 %collective-permute-start.147 = (f32[8,3072]{1,0:T(8,128)}, f32[8,3072]{1,0:T(8,128)}, u32[]{:S(2)}, u32[]{:S(2)}) collective-permute-start(f32[8,3072]{1,0:T(8,128)} %get-tuple-element.130), channel_id=1, source_target_pairs={{0,20},{1,21},{2,22},{3,23},{4,24},{5,25},{6,26},{7,27},{8,28},{9,... | collective-permute-start | bytes 294920
  1668.1 45.8 %collective-permute-start.146 = (f32[8,3072]{1,0:T(8,128)}, f32[8,3072]{1,0:T(8,128)}, u32[]{:S(2)}, u32[]{:S(2)}) collective-permute-start(f32[8,3072]{1,0:T(8,128)} %get-tuple-element.130), channel_id=1, source_target_pairs={{0,19},{1,20},{2,21},{3,22},{4,23},{5,24},{6,25},{7,26},{8,27},{9,... | collective-permute-start | bytes 294920
  1670.7 48.7 %collective-permute-start.145 = (f32[8,3072]{1,0:T(8,128)}, f32[8,3072]{1,0:T(8,128)}, u32[]{:S(2)}, u32[]{:S(2)}) collective-permute-start(f32[8,3072]{1,0:T(8,128)} %get-tuple-element.130), channel_id=1, source_target_pairs={{0,18},{1,19},{2,20},{3,21},{4,22},{5,23},{6,24},{7,25},{8,26},{9,... | collective-permute-start | bytes 294920
  1673.0 49.4 %collective-permute-start.144 = (f32[8,3072]{1,0:T(8,128)}, f32[8,3072]{1,0:T(8,128)}, u32[]{:S(2)}, u32[]{:S(2)}) collective-permute-start(f32[8,3072]{1,0:T(8,128)} %get-tuple-element.130), channel_id=1, source_target_pairs={{0,17},{1,18},{2,19},{3,20},{4,21},{5,22},{6,23},{7,24},{8,25},{9,... | collective-permute-start | bytes 294920
  1675.5 55.4 %collective-permute-start.143 = (f32[8,3072]{1,0:T(8,128)}, f32[8,3072]{1,0:T(8,128)}, u32[]{:S(2)}, u32[]{:S(2)}) collective-permute-start(f32[8,3072]{1,0:T(8,128)} %get-tuple-element.130), channel_id=1, source_target_pairs={{0,16},{1,17},{2,18},{3,19},{4,20},{5,21},{6,22},{7,23},{8,24},{9,... | collective-permute-start | bytes 294920
  1710.9 56.6 %collective-permute-start.142 = (f32[8,3072]{1,0:T(8,128)}, f32[8,3072]{1,0:T(8,128)}, u32[]{:S(2)}, u32[]{:S(2)}) collective-permute-start(f32[8,3072]{1,0:T(8,128)} %get-tuple-element.130), channel_id=1, source_target_pairs={{0,15},{1,16},{2,17},{3,18},{4,19},{5,20},{6,21},{7,22},{8,23},{9,... | collective-permute-start | bytes 294920
  1713.9 54.9 %collective-permute-start.141 = (f32[8,3072]{1,0:T(8,128)}, f32[8,3072]{1,0:T(8,128)}, u32[]{:S(2)}, u32[]{:S(2)}) collective-permute-start(f32[8,3072]{1,0:T(8,128)} %get-tuple-element.130), channel_id=1, source_target_pairs={{0,14},{1,15},{2,16},{3,17},{4,18},{5,19},{6,20},{7,21},{8,22},{9,... | collective-permute-start | bytes 294920
  1719.4 51.7 %collective-permute-start.140 = (f32[8,3072]{1,0:T(8,128)}, f32[8,3072]{1,0:T(8,128)}, u32[]{:S(2)}, u32[]{:S(2)}) collective-permute-start(f32[8,3072]{1,0:T(8,128)} %get-tuple-element.130), channel_id=1, source_target_pairs={{0,13},{1,14},{2,15},{3,16},{4,17},{5,18},{6,19},{7,20},{8,21},{9,... | collective-permute-start | bytes 294920
  1722.4 50.3 %collective-permute-start.139 = (f32[8,3072]{1,0:T(8,128)}, f32[8,3072]{1,0:T(8,128)}, u32[]{:S(2)}, u32[]{:S(2)}) collective-permute-start(f32[8,3072]{1,0:T(8,128)} %get-tuple-element.130), channel_id=1, source_target_pairs={{0,12},{1,13},{2,14},{3,15},{4,16},{5,17},{6,18},{7,19},{8,20},{9,... | collective-permute-start | bytes 294920
  1730.8 43.8 %collective-permute-start.138 = (f32[8,3072]{1,0:T(8,128)}, f32[8,3072]{1,0:T(8,128)}, u32[]{:S(2)}, u32[]{:S(2)}) collective-permute-start(f32[8,3072]{1,0:T(8,128)} %get-tuple-element.130), channel_id=1, source_target_pairs={{0,11},{1,12},{2,13},{3,14},{4,15},{5,16},{6,17},{7,18},{8,19},{9,... | collective-permute-start | bytes 294920
  1772.7 17.5 collective-permute-start.134
  1774.6 17.5 collective-permute-start.133
  1777.8 49.9 %collective-permute-start.132 = (f32[8,3072]{1,0:T(8,128)}, f32[8,3072]{1,0:T(8,128)}, u32[]{:S(2)}, u32[]{:S(2)}) collective-permute-start(f32[8,3072]{1,0:T(8,128)} %get-tuple-element.130), channel_id=1, source_target_pairs={{0,5},{1,6},{2,7},{3,8},{4,9},{5,10},{6,11},{7,12},{8,13},{9,14},{... | collective-permute-start | bytes 294920
  1783.6 44.1 %collective-permute-start.131 = (f32[8,3072]{1,0:T(8,128)}, f32[8,3072]{1,0:T(8,128)}, u32[]{:S(2)}, u32[]{:S(2)}) collective-permute-start(f32[8,3072]{1,0:T(8,128)} %get-tuple-element.130), channel_id=1, source_target_pairs={{0,4},{1,5},{2,6},{3,7},{4,8},{5,9},{6,10},{7,11},{8,12},{9,13},{1... | collective-permute-start | bytes 294920
  1785.5 42.2 %collective-permute-start.130 = (f32[8,3072]{1,0:T(8,128)}, f32[8,3072]{1,0:T(8,128)}, u32[]{:S(2)}, u32[]{:S(2)}) collective-permute-start(f32[8,3072]{1,0:T(8,128)} %get-tuple-element.130), channel_id=1, source_target_pairs={{0,3},{1,4},{2,5},{3,6},{4,7},{5,8},{6,9},{7,10},{8,11},{9,12},{10... | collective-permute-start | bytes 294920
  1790.2 37.5 %collective-permute-start.129 = (f32[8,3072]{1,0:T(8,128)}, f32[8,3072]{1,0:T(8,128)}, u32[]{:S(2)}, u32[]{:S(2)}) collective-permute-start(f32[8,3072]{1,0:T(8,128)} %get-tuple-element.130), channel_id=1, source_target_pairs={{0,2},{1,3},{2,4},{3,5},{4,6},{5,7},{6,8},{7,9},{8,10},{9,11},{10,... | collective-permute-start | bytes 294920
  1792.1 35.6 %collective-permute-start.128 = (f32[8,3072]{1,0:T(8,128)}, f32[8,3072]{1,0:T(8,128)}, u32[]{:S(2)}, u32[]{:S(2)}) collective-permute-start(f32[8,3072]{1,0:T(8,128)} %get-tuple-element.130), channel_id=1, source_target_pairs={{0,1},{1,2},{2,3},{3,4},{4,5},{5,6},{6,7},{7,8},{8,9},{9,10},{10,1... | collective-permute-start | bytes 294920
  (398 other events, 16563.2 us)
Sparse Core Ops, SparseCore 0:
  11.6 72.8 all-gather.36
  87.4 62.7 all-gather.38
  153.9 68.2 all-gather.40
  225.1 64.5 all-gather.42
  293.1 66.4 all-gather.44
  362.5 62.7 all-gather.46
  428.9 68.2 all-gather.48
  500.9 64.5 all-gather.50
  595.4 8.4 reduce-scatter.32
  610.0 8.4 reduce-scatter.30
  658.7 12.2 reduce-scatter.36
  673.3 12.2 reduce-scatter.34
  699.1 152.0 all-reduce.48
  856.9 227.6 reduce-scatter.28
  1090.3 216.8 reduce-scatter.26
where the time goes:
time: 1920 us; the launch traced here: 1890 us
  blocking collectives  501 us (26%)
  starting transfers between devices  495 us (26%)
  waiting for transfers between devices  388 us (20%)
  local copies, waits for them, and re-layouts  297 us (15%)
  matrix products  155 us (8%)
  other arithmetic  37.7 us (2%)
  between operations  19.9 us (1%)
    unnamed x197, starting transfers between devices  494 us
    unnamed x2, blocking collectives  491 us
    unnamed x588, local copies, waits for them, and re-layouts  259 us
    all_gather x2, waiting for transfers between devices, fetch(): lax.all_gather(w_up[layer_index], ('dp', 'fsdp'), axis=0, tiled=True)  137 us
    all_gather x2, waiting for transfers between devices, fetch(): lax.all_gather(w_down[layer_index], ('dp', 'fsdp'), axis=0, tiled=True)  121 us
    all_gather x2, waiting for transfers between devices, fetch(): lax.all_gather(w_qkv[layer_index], ('dp', 'fsdp'), axis=0, tiled=True)  64.3 us
    all_gather x2, waiting for transfers between devices, fetch(): lax.all_gather(w_out[layer_index], ('dp', 'fsdp'), axis=0, tiled=True)  54 us
  transfers between devices with their start and end apart: 207, of which 11 were waited for; matrix products, arithmetic and copies ran while one was open for 43% of the time, Pallas kernels for 0%

commit v1 on v0

v1 whole, which is shorter than its diff:
```python
import functools

import jax
import jax.numpy as jnp
from jax import lax
from jax.experimental import pallas as pl
from jax.experimental.pallas import tpu as pltpu
from jax.sharding import PartitionSpec as P

HEAD = 64
HEADS = 12
LAYERS = 2
D = 768
FF = 3072
VECTOR_WIDTHS = (6, 6, 12, 6, 6, 6, 24, 6)
VECTOR_ROWS = 2 * 72
MESH = pl.DeviceIdType.MESH
BF16, F32 = jnp.bfloat16, jnp.float32


def place():
    dp, core = lax.axis_index("dp"), lax.axis_index("fsdp")
    return {"z": dp // 16, "x": (dp // 4) % 4, "y": dp % 4, "c": core}


def device(at):
    return ((at["z"] * 4 + at["x"]) * 4 + at["y"], at["c"])


def moved(at, axis, step):
    size = 2 if axis == "c" else 4
    return {**at, axis: (at[axis] + step) % size}


class Links:
    def __init__(self, send_sems, recv_sems):
        self.send_sems, self.recv_sems, self.used, self.open = send_sems, recv_sems, 0, []

    def send(self, src, dst, target):
        copy = pltpu.make_async_remote_copy(
            src_ref=src,
            dst_ref=dst,
            send_sem=self.send_sems.at[self.used],
            recv_sem=self.recv_sems.at[self.used],
            device_id=device(target),
            device_id_type=MESH,
        )
        self.used += 1
        copy.start()
        self.open.append(copy)
        return copy

    def drain(self):
        for copy in self.open:
            copy.wait_send()
        self.open = []


def greet(me):
    partners = [moved(moved(me, "y", dy), "c", dc) for dy in range(4) for dc in range(2)][1:]
    partners += [moved(me, axis, step) for axis in "xz" for step in (1, 2, 3)]
    barrier = pltpu.get_barrier_semaphore()
    for partner in partners:
        pl.semaphore_signal(barrier, inc=1, device_id=device(partner), device_id_type=MESH)
    pl.semaphore_wait(barrier, len(partners))


def block_of(wide, deep, stream, layer, at):
    kind, part, _ = stream
    if kind == "wide":
        return wide.at[layer, at["y"], at["c"], at["z"], at["x"], :, part]
    return deep.at[layer, at["c"], at["z"], at["x"], at["y"], part, :]


ALL = slice(None)
STREAMS = (
    ("wide", slice(0, 384), "xyz"),
    ("wide", slice(384, 768), "xzy"),
    ("deep", slice(0, 16), "xyz"),
    ("deep", slice(16, 32), "xzy"),
    ("deep", slice(32, 48), "yzx"),
)


def gather_kernel(
    hidden, cot, w_qkv, w_out, w_up, w_down, vecs,
    seq_out, cot_out, wide, deep, vec_out,
    send_a, recv_a, send_d, recv_d, asm, piece_c, piece_d, vec_state, vec_recv,
    send_sems, recv_sems, local_sems,
):
    me = place()
    links = Links(send_sems, recv_sems)
    sibling = moved(me, "c", 1)
    mine = 2 * me["y"] + me["c"]
    for layer in range(LAYERS):
        rows = slice(8 * layer, 8 * layer + 6)
        for slab in range(8):
            if slab < 3:
                part = w_qkv[layer, :, slab * D : (slab + 1) * D]
            elif slab == 3:
                part = w_out[layer]
            else:
                part = w_up[layer, :, (slab - 4) * D : (slab - 3) * D]
            asm[slab, rows, :] = part.astype(F32)
    for slab in range(8):
        send_a[slab] = asm[slab, 0:16, :].astype(BF16)
    for half in range(2):
        for layer in range(LAYERS):
            asm[half, 16 + 24 * layer : 40 + 24 * layer, 0:384] = w_down[
                layer, :, half * 384 : (half + 1) * 384
            ].astype(F32)
        send_d[half] = asm[half, 16:64, 0:384].astype(BF16)

    greet(me)

    arrivals = []
    for dy in range(4):
        for dc in range(2):
            if dy == 0 and dc == 0:
                continue
            target = moved(moved(me, "y", dy), "c", dc)
            arrivals.append(
                links.send(send_a.at[2 * target["y"] + target["c"]], recv_a.at[mine], target)
            )
    arrivals.append(links.send(send_d.at[1 - me["c"]], recv_d.at[me["c"]], sibling))
    recv_a[mine] = send_a[mine]
    recv_d[me["c"]] = send_d[me["c"]]
    vec_state[0] = vecs[...]
    seq_links, locals_ = [], []
    for index, (src, dst) in enumerate(((hidden, seq_out), (cot, cot_out))):
        seq_links.append(links.send(src.at[1 - me["c"]], dst.at[me["c"]], sibling))
        copy = pltpu.make_async_copy(src.at[me["c"]], dst.at[me["c"]], local_sems.at[index])
        copy.start()
        locals_.append(copy)

    def vec_phase(number):
        axis = "xyzc"[number]
        return [
            links.send(vec_state.at[number], vec_recv.at[3 * number + step - 1], moved(me, axis, step))
            for step in range(1, 2 if axis == "c" else 4)
        ]

    def vec_sum(number, copies):
        total = vec_state[number].astype(F32)
        for copy in copies:
            copy.wait_recv()
        for step in range(len(copies)):
            total += vec_recv[3 * number + step].astype(F32)
        if number < 3:
            vec_state[number + 1] = total.astype(BF16)
        else:
            vec_out[...] = total.astype(BF16)

    vec_copies = vec_phase(0)
    for copy in arrivals:
        copy.wait_recv()
    own = []
    for layer in range(LAYERS):
        for source in range(8):
            asm[layer, 6 * source : 6 * source + 6, :] = recv_a[source].astype(F32)[
                8 * layer : 8 * layer + 6
            ]
        piece_c[layer] = asm[layer, 0:48, :].astype(BF16)
        for half in range(2):
            asm[2 + layer, 24 * half : 24 * half + 24, 0:384] = recv_d[half].astype(F32)[
                24 * layer : 24 * layer + 24
            ]
        piece_d[layer] = asm[2 + layer, 0:48, 0:384].astype(BF16)
        own.append(
            pltpu.make_async_copy(
                piece_c.at[layer],
                wide.at[layer, me["y"], me["c"], me["z"], me["x"]],
                local_sems.at[2 + 2 * layer],
            )
        )
        own.append(
            pltpu.make_async_copy(
                piece_d.at[layer],
                deep.at[layer, me["c"], me["z"], me["x"], me["y"]],
                local_sems.at[3 + 2 * layer],
            )
        )
        own[-2].start()
        own[-1].start()

    flows = [
        {"stream": stream, "layer": layer, "at": dict(me)}
        for layer in range(LAYERS)
        for stream in STREAMS
    ]

    def block(flow, at):
        return block_of(wide, deep, flow["stream"], flow["layer"], at)

    def begin(flow, phase):
        axis = flow["stream"][2][phase]
        src = block(flow, flow["at"])
        steps = (1, 3) if phase == 2 else (1, 3, 2)
        flow["copies"] = {step: links.send(src, src, moved(me, axis, step)) for step in steps}

    to_sibling = []

    def hand_over(flow, at):
        part = block(flow, at)
        to_sibling.append(links.send(part, part, sibling))

    def end(flow, phase):
        axis = flow["stream"][2][phase]
        if phase < 2:
            for step in (1, 3, 2):
                flow["copies"][step].wait_recv()
                if phase > 0:
                    hand_over(flow, moved(flow["at"], axis, -step))
            flow["at"] = {**flow["at"], axis: ALL}
            if phase == 0:
                hand_over(flow, flow["at"])
        else:
            split = flow["stream"][2][0]
            flow["halves"] = []
            for step, start in ((1, 0), (3, 2)):
                flow["copies"][step].wait_recv()
                came = moved(flow["at"], axis, -step)
                part = block(flow, {**came, split: pl.ds(start, 2)})
                flow["halves"].append(links.send(part, part, moved(me, axis, step)))
                hand_over(flow, came)

    def finish(flow):
        axis, split = flow["stream"][2][2], flow["stream"][2][0]
        for copy in flow["halves"]:
            copy.wait_recv()
        hand_over(flow, moved(flow["at"], axis, 2))

    for copy in own:
        copy.wait()
    for flow in flows:
        begin(flow, 0)
    vec_sum(0, vec_copies)
    vec_copies = vec_phase(1)
    for flow in flows:
        end(flow, 0)
        begin(flow, 1)
    vec_sum(1, vec_copies)
    vec_copies = vec_phase(2)
    for flow in flows:
        end(flow, 1)
        begin(flow, 2)
    vec_sum(2, vec_copies)
    vec_copies = vec_phase(3)
    for flow in flows:
        end(flow, 2)
    vec_sum(3, vec_copies)
    for flow in flows:
        finish(flow)
    for copy in to_sibling:
        copy.wait_recv()
    for copy in seq_links:
        copy.wait_recv()
    for copy in locals_:
        copy.wait()
    links.drain()


def gather(hidden, cot, w_qkv, w_out, w_up, w_down, vecs):
    vmem, hbm = pl.BlockSpec(memory_space=pltpu.VMEM), pl.BlockSpec(memory_space=pl.ANY)
    half = hidden.shape[1]
    return pl.pallas_call(
        gather_kernel,
        out_shape=(
            jax.ShapeDtypeStruct((2, half, D), BF16),
            jax.ShapeDtypeStruct((2, half, D), BF16),
            jax.ShapeDtypeStruct((LAYERS, 4, 2, 4, 4, 48, D), BF16),
            jax.ShapeDtypeStruct((LAYERS, 2, 4, 4, 4, 48, 384), BF16),
            jax.ShapeDtypeStruct((VECTOR_ROWS, 128), BF16),
        ),
        in_specs=[hbm, hbm, vmem, vmem, vmem, vmem, vmem],
        out_specs=(hbm, hbm, hbm, hbm, vmem),
        scratch_shapes=[
            pltpu.VMEM((8, 16, D), BF16),
            pltpu.VMEM((8, 16, D), BF16),
            pltpu.VMEM((2, 48, 384), BF16),
            pltpu.VMEM((2, 48, 384), BF16),
            pltpu.VMEM((8, 64, D), F32),
            pltpu.VMEM((LAYERS, 48, D), BF16),
            pltpu.VMEM((LAYERS, 48, 384), BF16),
            pltpu.VMEM((4, VECTOR_ROWS, 128), BF16),
            pltpu.VMEM((10, VECTOR_ROWS, 128), BF16),
            pltpu.SemaphoreType.DMA((240,)),
            pltpu.SemaphoreType.DMA((240,)),
            pltpu.SemaphoreType.DMA((8,)),
        ],
        compiler_params=pltpu.CompilerParams(
            collective_id=0, has_side_effects=True, vmem_limit_bytes=32 << 20
        ),
        name="gather",
    )(hidden, cot, w_qkv, w_out, w_up, w_down, vecs)


def spread(vectors, index):
    slot = (jnp.arange(128, dtype=jnp.int32) == index)[None, :, None]
    parts = [
        jnp.where(slot, vector[:, None, :], jnp.zeros((), BF16)).reshape(LAYERS, -1)
        for vector in vectors
    ]
    return jnp.concatenate(parts, axis=1).reshape(VECTOR_ROWS, 128)


WIDE_AXES, DEEP_AXES = "yzx", "zxy"
SUMS = (
    ("wide", slice(0, 48), slice(0, 384), "zyx"),
    ("wide", slice(0, 48), slice(384, 768), "yzx"),
    ("deep", slice(0, 16), slice(0, 384), "zyx"),
    ("deep", slice(16, 32), slice(0, 384), "yzx"),
    ("deep", slice(32, 48), slice(0, 384), "xzy"),
)


def extent(part):
    return part.stop - part.start


def scatter_kernel(layers, *refs):
    (wide_in, deep_in, vec_in, half_out, half_grad), refs = refs[:5], refs[5:]
    (g_qkv, g_out, g_up, g_down, vec_out, out, grad), refs = refs[:7], refs[7:]
    (own_wide, own_deep, got_wide, got_deep, vec_state, vec_recv), refs = refs[:6], refs[6:]
    first, second, third = refs[0:5], refs[5:10], refs[10:15]
    sum_wide, sum_deep, send_a, recv_a, send_d, recv_d, send_sems, recv_sems, local_sems = refs[15:]
    me = place()
    links = Links(send_sems, recv_sems)
    sibling = moved(me, "c", 1)
    mine = 2 * me["y"] + me["c"]

    def cut(wide, deep, flow, at):
        kind, rows, cols, _ = SUMS[flow["sum"]]
        axes = WIDE_AXES if kind == "wide" else DEEP_AXES
        index = tuple(at.get(axis, ALL) for axis in axes)
        return (wide if kind == "wide" else deep).at[(flow["layer"], *index, rows, cols)]

    def cut_in(flow, core, at):
        kind, rows, cols, _ = SUMS[flow["sum"]]
        if kind == "wide":
            index = (at.get("y", ALL), core, at.get("z", ALL), at.get("x", ALL))
            return wide_in.at[(flow["layer"], *index, rows, cols)]
        index = (core, at.get("z", ALL), at.get("x", ALL), at.get("y", ALL))
        return deep_in.at[(flow["layer"], *index, rows, cols)]

    greet(me)

    moves = []
    for index, (src, dst) in enumerate(((half_out, out), (half_grad, grad))):
        moves.append(links.send(src.at[1 - me["c"]], dst.at[me["c"]], sibling))
        copy = pltpu.make_async_copy(src.at[me["c"]], dst.at[me["c"]], local_sems.at[index])
        copy.start()
        moves.append(copy)
    used = 2

    vec_state[0] = vec_in[...]

    def vec_phase(number):
        axis = "xyzc"[number]
        return [
            links.send(vec_state.at[number], vec_recv.at[3 * number + step - 1], moved(me, axis, step))
            for step in range(1, 2 if axis == "c" else 4)
        ]

    def vec_sum(number, copies):
        total = vec_state[number]
        for copy in copies:
            copy.wait_recv()
        for step in range(len(copies)):
            total += vec_recv[3 * number + step]
        if number < 3:
            vec_state[number + 1] = total
        else:
            vec_out[...] = total

    vec_copies = vec_phase(0)
    flows = [{"sum": index, "layer": layer} for layer in layers for index in range(len(SUMS))]
    order = (1, 3, 2, 0)
    for step in order:
        for flow in flows:
            axis = SUMS[flow["sum"]][3][0]
            at = {axis: moved(me, axis, step)[axis]}
            core = me["c"]
            remote = links.send(
                cut_in(flow, 1 - core, at), cut(got_wide, got_deep, flow, at), sibling
            )
            copy = pltpu.make_async_copy(
                cut_in(flow, core, at), cut(own_wide, own_deep, flow, at), local_sems.at[used]
            )
            used += 1
            copy.start()
            flow.setdefault("pair", {})[step] = (remote, copy)
            flow.setdefault("at", {})[step] = at

    def rest(flow, at):
        kind = SUMS[flow["sum"]][0]
        return [axis for axis in (WIDE_AXES if kind == "wide" else DEEP_AXES) if axis not in at]

    def each(flow, at, body):
        axes = rest(flow, at)
        if len(axes) == 2:

            @pl.loop(0, 16)
            def _(index):
                body({**at, axes[0]: index // 4, axes[1]: index % 4}, (index // 4, index % 4))

        else:

            @pl.loop(0, 4)
            def _(index):
                body({**at, axes[0]: index}, (index,))

    for step in order:
        for flow in flows:
            at = flow["at"][step]
            for copy in flow["pair"][step]:
                copy.wait_recv() if copy is flow["pair"][step][0] else copy.wait()

            def add(spot, index):
                target = cut(own_wide, own_deep, flow, spot)
                target[...] += cut(got_wide, got_deep, flow, spot)[...]

            each(flow, at, add)
            if step:
                axis = SUMS[flow["sum"]][3][0]
                flow.setdefault("first", []).append(
                    links.send(
                        cut(own_wide, own_deep, flow, at),
                        first[flow["sum"]].at[flow["layer"], step - 1],
                        moved(me, axis, step),
                    )
                )

    vec_sum(0, vec_copies)
    vec_copies = vec_phase(1)

    def total_of(target, slots):
        total = target[...].astype(F32)
        for slot in slots:
            total += slot[...].astype(F32)
        return total

    for number, slots in ((0, first), (1, second)):
        for flow in flows:
            axes = SUMS[flow["sum"]][3]
            for copy in flow[("first", "second")[number]]:
                copy.wait_recv()
            at = {axis: me[axis] for axis in axes[: number + 1]}
            slot = slots[flow["sum"]]

            def add(spot, index):
                target = cut(own_wide, own_deep, flow, spot)
                target[...] = total_of(
                    target, [slot.at[(flow["layer"], s, *index)] for s in range(3)]
                ).astype(BF16)

            each(flow, at, add)
            axis = axes[number + 1]
            after = (second, third)[number][flow["sum"]]
            flow[("second", "third")[number]] = [
                links.send(
                    cut(own_wide, own_deep, flow, {**at, axis: moved(me, axis, step)[axis]}),
                    after.at[flow["layer"], step - 1],
                    moved(me, axis, step),
                )
                for step in (1, 3, 2)
            ]
        vec_sum(number + 1, vec_copies)
        vec_copies = vec_phase(number + 2)
    for flow in flows:
        kind, rows, cols, axes = SUMS[flow["sum"]]
        for copy in flow["third"]:
            copy.wait_recv()
        target = cut(own_wide, own_deep, flow, {axis: me[axis] for axis in axes})
        slot = third[flow["sum"]]
        total = total_of(target, [slot.at[flow["layer"], s] for s in range(3)])
        (sum_wide if kind == "wide" else sum_deep)[flow["layer"], rows, cols] = total
    vec_sum(3, vec_copies)

    for layer in layers:
        for owner in range(8):
            send_a[owner, 8 * layer : 8 * layer + 6, :] = sum_wide[
                layer, 6 * owner : 6 * owner + 6, :
            ]
        for owner in range(2):
            send_d[owner, 24 * layer : 24 * layer + 24, :] = sum_deep[
                layer, 24 * owner : 24 * owner + 24, :
            ]
    last = []
    for dy in range(4):
        for dc in range(2):
            if dy == 0 and dc == 0:
                continue
            target = moved(moved(me, "y", dy), "c", dc)
            last.append(
                links.send(send_a.at[2 * target["y"] + target["c"]], recv_a.at[mine], target)
            )
    last.append(links.send(send_d.at[1 - me["c"]], recv_d.at[me["c"]], sibling))
    recv_a[mine] = send_a[mine]
    recv_d[me["c"]] = send_d[me["c"]]
    for copy in last:
        copy.wait_recv()
    for layer in layers:
        rows = slice(8 * layer, 8 * layer + 6)
        for slab in range(8):
            value = recv_a[slab, rows, :]
            if slab < 3:
                g_qkv[layer, :, slab * D : (slab + 1) * D] = value
            elif slab == 3:
                g_out[layer] = value
            else:
                g_up[layer, :, (slab - 4) * D : (slab - 3) * D] = value
        for half in range(2):
            g_down[layer, :, half * 384 : (half + 1) * 384] = recv_d[
                half, 24 * layer : 24 * layer + 24, :
            ]
    moves[0].wait_recv()
    moves[1].wait()
    moves[2].wait_recv()
    moves[3].wait()
    links.drain()


def scatter(wide, deep, vecs, half_out, half_grad):
    vmem, hbm = pl.BlockSpec(memory_space=pltpu.VMEM), pl.BlockSpec(memory_space=pl.ANY)
    half = half_out.shape[1]
    sizes = [(extent(rows), extent(cols)) for _, rows, cols, _ in SUMS]
    return pl.pallas_call(
        functools.partial(scatter_kernel, (1, 0)),
        out_shape=(
            jax.ShapeDtypeStruct((LAYERS, 6, 3 * D), F32),
            jax.ShapeDtypeStruct((LAYERS, 6, D), F32),
            jax.ShapeDtypeStruct((LAYERS, 6, FF), F32),
            jax.ShapeDtypeStruct((LAYERS, 24, D), F32),
            jax.ShapeDtypeStruct((VECTOR_ROWS, 128), F32),
            jax.ShapeDtypeStruct((2, half, D), BF16),
            jax.ShapeDtypeStruct((2, half, D), F32),
        ),
        in_specs=[hbm, hbm, vmem, hbm, hbm],
        out_specs=(vmem, vmem, vmem, vmem, vmem, hbm, hbm),
        scratch_shapes=[
            pltpu.VMEM((LAYERS, 4, 4, 4, 48, D), BF16),
            pltpu.VMEM((LAYERS, 4, 4, 4, 48, 384), BF16),
            pltpu.VMEM((LAYERS, 4, 4, 4, 48, D), BF16),
            pltpu.VMEM((LAYERS, 4, 4, 4, 48, 384), BF16),
            pltpu.VMEM((4, VECTOR_ROWS, 128), F32),
            pltpu.VMEM((10, VECTOR_ROWS, 128), F32),
            *[pltpu.VMEM((LAYERS, 3, 4, 4, *size), BF16) for size in sizes],
            *[pltpu.VMEM((LAYERS, 3, 4, *size), BF16) for size in sizes],
            *[pltpu.VMEM((LAYERS, 3, *size), BF16) for size in sizes],
            pltpu.VMEM((LAYERS, 48, D), F32),
            pltpu.VMEM((LAYERS, 48, 384), F32),
            pltpu.VMEM((8, 16, D), F32),
            pltpu.VMEM((8, 16, D), F32),
            pltpu.VMEM((2, 48, 384), F32),
            pltpu.VMEM((2, 48, 384), F32),
            pltpu.SemaphoreType.DMA((200,)),
            pltpu.SemaphoreType.DMA((200,)),
            pltpu.SemaphoreType.DMA((64,)),
        ],
        compiler_params=pltpu.CompilerParams(
            collective_id=1, has_side_effects=True, vmem_limit_bytes=56 << 20
        ),
        name="scatter",
    )(wide, deep, vecs, half_out, half_grad)


def norm_apply(stream, gain, offset):
    center = stream - jnp.mean(stream, axis=-1, keepdims=True)
    spread = jnp.mean(center * center, axis=-1, keepdims=True)
    return center * lax.rsqrt(spread + 1e-05) * gain + offset


def col_sums(values):
    return jnp.sum(values.astype(F32), axis=0)


def dot(a, b):
    return jnp.dot(a, b, preferred_element_type=F32)


def dot_nt(a, b):
    return lax.dot_general(a, b, (((1,), (1,)), ((), ())), preferred_element_type=F32)


def dot_tn(a, b):
    return lax.dot_general(a, b, (((0,), (0,)), ((), ())), preferred_element_type=F32)


def split_vectors(row):
    parts, start = [], 0
    for width in VECTOR_WIDTHS:
        parts.append(row[start : start + 128 * width].astype(F32))
        start += 128 * width
    return parts


def layer_forward(stream, wide, deep, vectors):
    gain_one, offset_one, bias_qv, bias_out, gain_two, offset_two, bias_up, bias_down = vectors
    normed = norm_apply(stream, gain_one, offset_one).astype(BF16)
    length = stream.shape[0]
    query, keys, values = (
        (dot(normed, wide[slab]) + bias).astype(BF16).reshape(length, HEADS, HEAD)
        for slab, bias in ((0, bias_qv[:D]), (1, 0.0), (2, bias_qv[D:]))
    )
    scores = jnp.einsum("qhe,khe->hqk", query, keys, preferred_element_type=F32) * 0.125
    probs = jax.nn.softmax(scores, axis=-1)
    attended = jnp.einsum("hqk,khe->qhe", probs.astype(BF16), values, preferred_element_type=F32)
    attended = attended.astype(BF16).reshape(length, D)
    middle = stream + dot(attended, wide[3]) + bias_out
    normed_two = norm_apply(middle, gain_two, offset_two).astype(BF16)
    pre = [dot(normed_two, wide[4 + i]) + bias_up[i * D : (i + 1) * D] for i in range(4)]
    active = [jax.nn.gelu(part, approximate=True).astype(BF16) for part in pre]
    active = jnp.concatenate(active, axis=1)
    result = middle + jnp.concatenate([dot(active, deep[i]) for i in range(2)], axis=1) + bias_down
    return result, (normed, query, keys, values, probs, attended, middle, normed_two, pre, active)


def layer_backward(stream, wide, deep, vectors, saved, grad_top):
    gain_one, offset_one, bias_qv, bias_out, gain_two, offset_two, bias_up, bias_down = vectors
    normed, query, keys, values, probs, attended, middle, normed_two, pre, active = saved
    length = stream.shape[0]
    grad_z = grad_top.astype(BF16)
    grad_deep = jnp.stack([dot_tn(active, grad_z[:, i * 384 : (i + 1) * 384]) for i in range(2)])
    grad_bias_down = col_sums(grad_z)
    grad_active = dot_nt(grad_z[:, :384], deep[0]) + dot_nt(grad_z[:, 384:], deep[1])
    pre = jnp.concatenate(pre, axis=1)
    pull = jax.vjp(lambda inner: jax.nn.gelu(inner, approximate=True), pre)[1]
    grad_pre = pull(grad_active)[0].astype(BF16)
    grad_bias_up = col_sums(grad_pre)
    grad_up = [dot_tn(normed_two, grad_pre[:, i * D : (i + 1) * D]) for i in range(4)]
    grad_normed_two = sum(dot_nt(grad_pre[:, i * D : (i + 1) * D], wide[4 + i]) for i in range(4))
    pull = jax.vjp(norm_apply, middle, gain_two, offset_two)[1]
    grad_norm, grad_gain_two, grad_offset_two = pull(grad_normed_two)
    grad_middle = grad_top + grad_norm
    grad_branch = grad_middle.astype(BF16)
    grad_out = dot_tn(attended, grad_branch)
    grad_bias_out = col_sums(grad_branch)
    grad_attended = dot_nt(grad_branch, wide[3]).astype(BF16).reshape(length, HEADS, HEAD)
    grad_probs = jnp.einsum("qhe,khe->hqk", grad_attended, values, preferred_element_type=F32)
    grad_values = jnp.einsum(
        "hqk,qhe->khe", probs.astype(BF16), grad_attended, preferred_element_type=F32
    )
    row_dot = jnp.sum(grad_probs * probs, axis=-1, keepdims=True)
    grad_scores = (probs * (grad_probs - row_dot)).astype(BF16)
    grad_query = jnp.einsum("hqk,khe->qhe", grad_scores, keys, preferred_element_type=F32) * 0.125
    grad_keys = jnp.einsum("hqk,qhe->khe", grad_scores, query, preferred_element_type=F32) * 0.125
    grad_qkv = [part.astype(BF16).reshape(length, D) for part in (grad_query, grad_keys, grad_values)]
    grad_w_qkv = [dot_tn(normed, part) for part in grad_qkv]
    grad_bias_qv = jnp.concatenate([col_sums(grad_qkv[0]), col_sums(grad_qkv[2])])
    grad_normed = sum(dot_nt(part, wide[slab]) for slab, part in enumerate(grad_qkv))
    pull = jax.vjp(norm_apply, stream, gain_one, offset_one)[1]
    grad_norm, grad_gain_one, grad_offset_one = pull(grad_normed)
    grad_wide = jnp.stack(
        [part.astype(BF16) for part in (*grad_w_qkv, grad_out, *grad_up)]
    )
    vecs = jnp.concatenate(
        [
            grad_gain_one, grad_offset_one, grad_bias_qv, grad_bias_out,
            grad_gain_two, grad_offset_two, grad_bias_up, grad_bias_down,
        ]
    )
    return grad_middle + grad_norm, grad_wide, grad_deep.astype(BF16), vecs


def shards(
    hidden, cotangent, remaining, order,
    norm1_gain, norm1_bias, w_qkv, bias_qv, w_out, bias_out,
    norm2_gain, norm2_bias, w_up, bias_up, w_down, bias_down,
):
    half_rows = hidden.shape[1]
    length = 2 * half_rows
    core = lax.axis_index("fsdp")
    index = lax.axis_index("dp") * 2 + core
    vectors = (
        norm1_gain, norm1_bias, bias_qv, bias_out, norm2_gain, norm2_bias, bias_up, bias_down
    )
    own_hidden, own_cot, wide, deep, vecs = gather(
        hidden, cotangent, w_qkv, w_out, w_up, w_down, spread(vectors, index)
    )
    wide = wide.reshape(LAYERS, 8, D, D)
    deep = deep.reshape(LAYERS, 2, FF, 384)
    vecs = vecs.reshape(LAYERS, -1)
    own_order, own_remaining = order[core], remaining[core]
    positions = jnp.arange(length, dtype=jnp.int32)
    live = positions >= length - own_remaining
    mask = jnp.any((own_order[:, None] == positions[None, :]) & live[:, None], axis=0)
    grad = own_cot.reshape(length, D).astype(F32) * mask.astype(F32)[:, None]
    stream = own_hidden.reshape(length, D).astype(F32)
    inputs, saved = [], []
    for layer in range(LAYERS):
        inputs.append(stream)
        stream, kept = layer_forward(stream, wide[layer], deep[layer], split_vectors(vecs[layer]))
        saved.append(kept)
    grads = [None] * LAYERS
    for layer in reversed(range(LAYERS)):
        grad, *grads[layer] = layer_backward(
            inputs[layer], wide[layer], deep[layer], split_vectors(vecs[layer]), saved[layer], grad
        )
    grad_wide, grad_deep, grad_vecs = (jnp.stack(parts) for parts in zip(*grads))
    g_qkv, g_out, g_up, g_down, vec_sums, out, grad_hidden = scatter(
        grad_wide.reshape(LAYERS, 4, 2, 4, 4, 48, D),
        grad_deep.reshape(LAYERS, 2, 4, 4, 4, 48, 384),
        grad_vecs.reshape(VECTOR_ROWS, 128),
        stream.astype(BF16).reshape(2, half_rows, D),
        grad.reshape(2, half_rows, D),
    )
    vec_sums, parts, start = vec_sums.reshape(LAYERS, -1), [], 0
    for width in VECTOR_WIDTHS:
        parts.append(lax.dynamic_slice_in_dim(vec_sums, start + width * index, width, 1))
        start += 128 * width
    gain_one, offset_one, qv, out_bias, gain_two, offset_two, up, down = parts
    return (
        out, grad_hidden, gain_one, offset_one, g_qkv, qv, g_out, out_bias,
        gain_two, offset_two, g_up, up, g_down, down,
    )


def solution(mesh):
    tokens, rows = P("dp", "fsdp", None), P(None, ("dp", "fsdp"), None)
    vector = P(None, ("dp", "fsdp"))
    weights = (
        vector, vector, rows, vector, rows, vector, vector, vector, rows, vector, rows, vector
    )
    return jax.shard_map(
        shards,
        mesh=mesh,
        in_specs=(tokens, tokens, P("dp"), P("dp", None), *weights),
        out_specs=(tokens, tokens, *weights),
        check_vma=False,
    )
```

time: 1920 us -> 427 us (0.22); the launches traced: 1890 us -> 423 us
  blocking collectives: 501 us -> 0 us
  starting transfers between devices: 495 us -> 0 us
  waiting for transfers between devices: 388 us -> 0 us
  local copies, waits for them, and re-layouts: 297 us -> 66.2 us
  Pallas kernels: 0 us -> 219 us
  matrix products: 155 us -> 110 us
    unnamed x197 -> x0, starting transfers between devices: 494 us -> none
    unnamed x2 -> x0, blocking collectives: 491 us -> none
    all_gather x8 -> x0, waiting for transfers between devices: 377 us -> none  [the longest x2 137 us: fetch(): lax.all_gather(w_up[layer_index], ('dp', 'fsdp'), axis=0, tiled=True)]
    unnamed x588 -> x301, local copies, waits for them, and re-layouts: 259 us -> 25.2 us
    pallas_call x0 -> x2, Pallas kernels: none -> 219 us  [the longest x1 118 us: scatter(): pl.pallas_call(functools.partial(scatter_kernel, (1, 0)), out_shape=(jax....]
    dot_general x36 -> x70, matrix products: 155 us -> 104 us  [the longest x20 36.5 us: dot(): return jnp.dot(a, b, preferred_element_type=F32)]
  transfers between devices with their start and end apart: 207 -> 0, of which waited for: 11 -> 0; matrix products, arithmetic and copies ran while one was open for 43% -> 0% of each run, Pallas kernels for 0% -> 0%
where the time goes in v1:
time: 427 us; the launch traced here: 423 us
  Pallas kernels  219 us (51%)
  matrix products  110 us (26%)
  local copies, waits for them, and re-layouts  66.2 us (16%)
  other arithmetic  23.4 us (5%)
    pallas_call x1, Pallas kernels, scatter(): pl.pallas_call(functools.partial(scatter_kernel, (1, 0)), out_shape=(jax....  118 us
    pallas_call x1, Pallas kernels, gather(): pl.pallas_call(gather_kernel, out_shape=(jax.ShapeDtypeStruct((2, half, D...  102 us
    dot_general x20, matrix products, dot(): return jnp.dot(a, b, preferred_element_type=F32)  36.5 us
    dot_general x20, matrix products, dot_nt(): lax.dot_general(a, b, (((1,), (1,)), ((), ())), preferred_element_type=F32)  32 us
    unnamed x301, local copies, waits for them, and re-layouts  25.2 us
    dot_general x20, matrix products, dot_tn(): lax.dot_general(a, b, (((0,), (0,)), ((), ())), preferred_element_type=F32)  18 us
    slice x1, local copies, waits for them, and re-layouts, shards(): wide[layer]  13.4 us
    another operation x3, other arithmetic, shards(): jnp.stack(parts)  13 us

profile of v1, /device:TPU:1, one launch (start us, length us, event | category | flops | bytes accessed | tf_op | source)
XLA Modules:
  0.0 423.2 jit_solution(3956957578296117711)
XLA Ops:
  0.7 1.2 dynamic_slice.31
  15.5 101.7 %gather.1 = (bf16[2,128,768]{2,1,0:T(8,128)(2,1)S(1)}, bf16[2,128,768]{2,1,0:T(8,128)(2,1)S(1)}, bf16[2,4,2,4,4,48,768]{6,5,4,3,2,1,0:T(8,128)(2,1)}, bf16[2,2,4...) custom-call(bf16[2,128,768]{2,1,0:T(8,128)(2,1)S(1)} %copy-done.3, bf16[2,128,768]{2,1,0:T(8,128)(2,1)S(1)} %copy-done.4, ...), custom_call_target="tpu_custom_call" | custom-call | tf_op jit(solution)/shard_map/gather/pallas_call | solution.py:266
  117.2 13.4 %fusion.195 = (bf16[1,4,2,4,4,48,768]{6,5,4,3,2,1,0:T(8,128)(2,1)}, bf16[1,4,2,4,4,48,768]{6,5,4,3,2,1,0:T(8,128)(2,1)S(1)}) fusion(bf16[2,4,2,4,4,48,768]{6,5,4,3,2,1,0:T(8,128)(2,1)} %get-tuple-element.28), kind=kLoop, calls=%fused_computation.422 | loop fusion | bytes 37748736 | tf_op jit(solution)/shard_map/slice | solution.py:693
  131.8 1.0 slice_bitcast_fusion.52
  132.8 1.3 slice_bitcast_fusion.51
  136.4 1.9 fusion.58
  138.5 1.9 convolution_convert_fusion.27
  140.5 2.9 fusion.197
  143.5 2.3 convolution_convert_fusion.26
  145.8 2.0 fusion.198
  148.3 2.9 fusion.101
  151.3 2.9 fusion.93
  154.2 2.9 fusion.85
  157.1 2.9 fusion.77
  160.0 3.0 fusion.196
  163.0 1.0 fusion.186
  165.1 1.0 fusion.187
  167.4 2.7 fusion.61
  170.1 1.2 copy.90
  171.3 2.7 fusion.60
  174.0 1.9 copy.89
  175.9 2.5 convolution_convert_fusion.25
  178.4 1.2 copy.91
  179.6 4.5 %fusion.173 = f32[256,3072]{1,0:T(8,128)} fusion(bf16[3072,384]{1,0:T(8,128)(2,1)} %bitcast.428, bf16[256,768]{1,0:T(8,128)(2,1)S(1)} %fusion.141), kind=kOutput, calls=%fused_computation.310 | convolution fusion | flops 603979776 | bytes 5701632 | tf_op jit(solution)/shard_map/dot_general | solution.py:583
  184.1 3.4 fusion.199
  187.5 2.5 convolution_convert_fusion.24
  190.1 2.8 fusion.200
  193.3 2.0 fusion.133
  197.3 1.3 copy-done.9
  198.6 1.0 fusion.185
  201.2 3.7 convert_reduce_fusion
  205.0 1.0 fusion.184
  207.6 1.3 multiply_reduce_fusion.5
  208.9 1.1 fusion.192
  211.6 1.3 convolution_convert_fusion.23
  212.8 1.9 copy.93
  214.8 3.9 convert_reduce_fusion.4
  218.7 1.4 reduce_sum.406
  220.0 3.9 convolution_convert_fusion
  224.0 2.4 convolution_convert_fusion.1
  228.7 1.8 convert_reduce_fusion.5
  230.5 1.4 reduce_sum.401
  231.9 2.0 fusion.68
  234.0 1.8 convolution_add_fusion.8
  235.8 2.1 multiply_reduce_fusion.6
  239.6 1.0 fusion.168
  241.6 3.9 convert_reduce_fusion.1
  247.2 1.3 multiply_reduce_fusion.7
  250.5 3.3 convert_reduce_fusion.8
  253.9 2.5 convolution_convert_fusion.2
  256.4 1.0 convolution_convert_fusion.3
  258.8 4.6 %maximum_maximum_fusion.refs_1_ = bf16[2,2,4,4,4,48,384]{6,5,4,3,2,1,0:T(8,128)(2,1)} fusion(bf16[1,1,4,4,4,48,384]{6,5,4,3,2,1,0:T(8,128)(2,1)S(1)} %bitcast.445, bf16[1,1,4,4,4,48,384]{6,5,4,3,2,1,0:T(8,128)(2,1)S(1)} %bitcast.446, bf16[1,1,4,4,4,48,384]{6,5,4,3,2,1,0:T(8,128)(2,1)S(1)} %bitcast.449, bf16[1,1,4,4,4,48,384]{6,5,4,3,2,1,0:T(8,128)(2,1)S(1)} %bitcast.450), kind=kLoop, calls=%fused_computation.3 | loop fusion | flops 14155776 | bytes 18874368 | tf_op jit(solution)/shard_map/stack | solution.py:700
  265.8 1.2 convert_reduce_fusion.9
  267.6 1.9 fusion.66
  269.6 1.8 convolution_add_fusion.3
  271.4 2.0 multiply_reduce_fusion.4
  274.0 1.2 add_add_fusion.4
  284.7 8.3 %pad_maximum_fusion.refs_0_ = bf16[2,4,2,4,4,48,768]{6,5,4,3,2,1,0:T(8,128)(2,1)} fusion(bf16[1,4,2,4,4,48,768]{6,5,4,3,2,1,0:T(8,128)(2,1)S(1)} %bitcast.431, bf16[1,4,2,4,4,48,768]{6,5,4,3,2,1,0:T(8,128)(2,1)S(1)} %bitcast.430), kind=kLoop, calls=%fused_computation.2 | loop fusion | flops 9437184 | bytes 37748736 | tf_op jit(solution)/shard_map/stack | solution.py:700
  293.0 117.8 %scatter.1 = (f32[2,6,2304]{2,1,0:T(8,128)}, f32[2,6,768]{2,1,0:T(8,128)}, f32[2,6,3072]{2,1,0:T(8,128)}, f32[2,24,768]{2,1,0:T(8,128)}, f32[144,128]{1,0:T(8,12...) custom-call(bf16[2,4,2,4,4,48,768]{6,5,4,3,2,1,0:T(8,128)(2,1)} %pad_maximum_fusion.refs_0_, ...), custom_call_target="tpu_custom_call" | custom-call | tf_op jit(solution)/shard_map/scatter/pallas_call | solution.py:528
  410.8 1.5 copy.102
  415.2 1.6 copy.101
  416.8 1.7 copy.103
  418.5 1.8 copy.154
  420.2 2.1 copy.155
  (419 shorter events, 52.2 us)
Async XLA Ops:
  2.8 132.0 %copy-start.62 = (f32[256]{0:T(256)}, f32[256]{0:T(256)S(1)}, u32[]{:S(2)}) copy-start(f32[256]{0:T(256)S(1)} %get-tuple-element.153) | copy-start | bytes 3076
  117.2 13.4 %copy-start.2 = (bf16[2,2,4,4,4,48,384]{6,5,4,3,2,1,0:T(8,128)(2,1)}, bf16[2,2,4,4,4,48,384]{6,5,4,3,2,1,0:T(8,128)(2,1)S(1)}, u32[]{:S(2)}) copy-start(bf16[2,2,4,4,4,48,384]{6,5,4,3,2,1,0:T(8,128)(2,1)S(1)} %get-tuple-element.30) | copy-start | bytes 28311556
  130.7 5.0 %copy-start.6 = (bf16[1,4,2,4,4,48,768]{6,5,4,3,2,1,0:T(8,128)(2,1)}, bf16[1,4,2,4,4,48,768]{6,5,4,3,2,1,0:T(8,128)(2,1)S(1)}, u32[]{:S(2)}) copy-start(bf16[1,4,2,4,4,48,768]{6,5,4,3,2,1,0:T(8,128)(2,1)S(1)} %get-tuple-element.108) | copy-start | bytes 28311556
  131.7 3.0 copy-start.96
  135.7 2.8 copy-start.10
  136.4 7.1 %copy-start.45 = (bf16[256,768]{0,1:T(8,128)(2,1)}, bf16[256,768]{0,1:T(8,128)(2,1)S(1)}, u32[]{:S(2)}) copy-start(bf16[256,768]{0,1:T(8,128)(2,1)S(1)} %copy.87) | copy-start | bytes 1179652
  138.4 5.0 %copy-start.26 = (bf16[256,768]{0,1:T(8,128)(2,1)}, bf16[256,768]{0,1:T(8,128)(2,1)S(1)}, u32[]{:S(2)}) copy-start(bf16[256,768]{0,1:T(8,128)(2,1)S(1)} %copy.86) | copy-start | bytes 1179652
  140.5 5.2 %copy-start.24 = (bf16[256,768]{0,1:T(8,128)(2,1)}, bf16[256,768]{0,1:T(8,128)(2,1)S(1)}, u32[]{:S(2)}) copy-start(bf16[256,768]{0,1:T(8,128)(2,1)S(1)} %copy.85) | copy-start | bytes 1179652
  145.8 5.5 %copy-start.53 = (bf16[12,64,256]{2,1,0:T(8,128)(2,1)}, bf16[12,64,256]{2,1,0:T(8,128)(2,1)S(1)}, u32[]{:S(2)}) copy-start(bf16[12,64,256]{2,1,0:T(8,128)(2,1)S(1)} %convolution_convert_fusion.26) | copy-start | bytes 1179652
  145.8 14.2 %slice-start = ((s8[9437184]{0:T(1024)(128)(4,1)}), s8[4194304]{0:T(1024)(128)(4,1)S(1)}, s32[]{:S(2)}) async-start(s8[9437184]{0:T(1024)(128)(4,1)} %bitcast.388), calls=%async_computation | async-start | bytes 8388608
  147.8 6.3 %copy-start.69 = (f32[256]{0:T(256)}, f32[256]{0:T(256)S(1)}, u32[]{:S(2)}) copy-start(f32[256]{0:T(256)S(1)} %broadcast_multiply_fusion.2) | copy-start | bytes 3076
  148.1 6.1 %copy-start.92 = (f32[256]{0:T(256)}, f32[256]{0:T(256)S(1)}, u32[]{:S(2)}) copy-start(f32[256]{0:T(256)S(1)} %multiply_reduce_fusion.14) | copy-start | bytes 3076
  148.1 6.0 %copy-start.88 = (f32[256]{0:T(256)}, f32[256]{0:T(256)S(1)}, u32[]{:S(2)}) copy-start(f32[256]{0:T(256)S(1)} %fusion.176) | copy-start | bytes 3076
  148.3 8.8 %copy-start.49 = (bf16[256,768]{1,0:T(8,128)(2,1)}, bf16[256,768]{1,0:T(8,128)(2,1)S(1)}, u32[]{:S(2)}) copy-start(bf16[256,768]{1,0:T(8,128)(2,1)S(1)} %add_convert_fusion.2) | copy-start | bytes 1179652
  148.3 11.7 %slice-start.1 = ((s8[9437184]{0:T(1024)(128)(4,1)}), s8[4194304]{0:T(1024)(128)(4,1)S(1)}, s32[]{:S(2)}) async-start(s8[9437184]{0:T(1024)(128)(4,1)} %bitcast.388), calls=%async_computation.1 | async-start | bytes 8388608
  151.3 12.8 %copy-start.113 = (bf16[256,768]{1,0:T(8,128)(2,1)}, bf16[256,768]{1,0:T(8,128)(2,1)S(1)}, u32[]{:S(2)}) copy-start(bf16[256,768]{1,0:T(8,128)(2,1)S(1)} %get-tuple-element.158) | copy-start | bytes 1179652
  154.2 9.9 %copy-start.115 = (bf16[256,768]{1,0:T(8,128)(2,1)}, bf16[256,768]{1,0:T(8,128)(2,1)S(1)}, u32[]{:S(2)}) copy-start(bf16[256,768]{1,0:T(8,128)(2,1)S(1)} %get-tuple-element.160) | copy-start | bytes 1179652
  154.2 5.8 %slice-start.2 = ((s8[9437184]{0:T(1024)(128)(4,1)}), s8[1048576]{0:T(1024)(128)(4,1)S(1)}, s32[]{:S(2)}) async-start(s8[9437184]{0:T(1024)(128)(4,1)} %bitcast.388), calls=%async_computation.2 | async-start | bytes 2097152
  157.1 7.0 %copy-start.117 = (bf16[256,768]{1,0:T(8,128)(2,1)}, bf16[256,768]{1,0:T(8,128)(2,1)S(1)}, u32[]{:S(2)}) copy-start(bf16[256,768]{1,0:T(8,128)(2,1)S(1)} %get-tuple-element.162) | copy-start | bytes 1179652
  160.0 4.1 copy-start.119
  167.4 8.5 %copy-start.12 = (bf16[256,768]{1,0:T(8,128)(2,1)}, bf16[256,768]{1,0:T(8,128)(2,1)S(1)}, u32[]{:S(2)}) copy-start(bf16[256,768]{1,0:T(8,128)(2,1)S(1)} %add_convert_fusion.1) | copy-start | bytes 1179652
  171.3 12.8 %copy-start.28 = (bf16[256,768]{0,1:T(8,128)(2,1)}, bf16[256,768]{0,1:T(8,128)(2,1)S(1)}, u32[]{:S(2)}) copy-start(bf16[256,768]{0,1:T(8,128)(2,1)S(1)} %copy.90) | copy-start | bytes 1179652
  179.6 7.9 %copy-start.30 = (bf16[256,768]{0,1:T(8,128)(2,1)}, bf16[256,768]{0,1:T(8,128)(2,1)S(1)}, u32[]{:S(2)}) copy-start(bf16[256,768]{0,1:T(8,128)(2,1)S(1)} %copy.91) | copy-start | bytes 1179652
  187.5 7.9 %slice-start.6 = ((s8[9437184]{0:T(1024)(128)(4,1)}), s8[4194304]{0:T(1024)(128)(4,1)S(1)}, s32[]{:S(2)}) async-start(s8[9437184]{0:T(1024)(128)(4,1)} %bitcast.416), calls=%async_computation.6 | async-start | bytes 8388608
  187.5 7.9 %slice-start.7 = ((s8[9437184]{0:T(1024)(128)(4,1)}), s8[4194304]{0:T(1024)(128)(4,1)S(1)}, s32[]{:S(2)}) async-start(s8[9437184]{0:T(1024)(128)(4,1)} %bitcast.416), calls=%async_computation.7 | async-start | bytes 8388608
  190.0 5.3 %copy-start.36 = (bf16[12,64,256]{2,1,0:T(8,128)(2,1)}, bf16[12,64,256]{2,1,0:T(8,128)(2,1)S(1)}, u32[]{:S(2)}) copy-start(bf16[12,64,256]{2,1,0:T(8,128)(2,1)S(1)} %convolution_convert_fusion.24) | copy-start | bytes 1179652
  190.0 3.1 copy-start.73
  190.0 3.3 copy-start.103
  190.0 5.3 %slice-start.8 = ((s8[9437184]{0:T(1024)(128)(4,1)}), s8[1048576]{0:T(1024)(128)(4,1)S(1)}, s32[]{:S(2)}) async-start(s8[9437184]{0:T(1024)(128)(4,1)} %bitcast.416), calls=%async_computation.8 | async-start | bytes 2097152
  193.3 3.4 copy-start.51
  195.3 9.6 %copy-start.121 = (bf16[256,768]{1,0:T(8,128)(2,1)}, bf16[256,768]{1,0:T(8,128)(2,1)S(1)}, u32[]{:S(2)}) copy-start(bf16[256,768]{1,0:T(8,128)(2,1)S(1)} %get-tuple-element.171) | copy-start | bytes 1179652
  196.0 9.0 %copy-start.123 = (bf16[256,768]{1,0:T(8,128)(2,1)}, bf16[256,768]{1,0:T(8,128)(2,1)S(1)}, u32[]{:S(2)}) copy-start(bf16[256,768]{1,0:T(8,128)(2,1)S(1)} %get-tuple-element.173) | copy-start | bytes 1179652
  196.7 8.3 %copy-start.125 = (bf16[256,768]{1,0:T(8,128)(2,1)}, bf16[256,768]{1,0:T(8,128)(2,1)S(1)}, u32[]{:S(2)}) copy-start(bf16[256,768]{1,0:T(8,128)(2,1)S(1)} %get-tuple-element.175) | copy-start | bytes 1179652
  197.3 7.7 %copy-start.127 = (bf16[256,768]{1,0:T(8,128)(2,1)}, bf16[256,768]{1,0:T(8,128)(2,1)S(1)}, u32[]{:S(2)}) copy-start(bf16[256,768]{1,0:T(8,128)(2,1)S(1)} %get-tuple-element.177) | copy-start | bytes 1179652
  220.0 3.9 copy-start.122
  220.0 3.9 copy-start.124
  220.0 3.9 copy-start.126
  220.0 3.9 copy-start.128
  230.5 5.3 %copy-start.72 = (f32[256]{0:T(256)S(1)}, f32[256]{0:T(256)}, u32[]{:S(2)}) copy-start(f32[256]{0:T(256)} %copy-done.71) | copy-start | bytes 3076
  231.9 3.9 copy-start.55
  233.9 4.0 copy-start.59
  233.9 4.1 copy-start.81
  233.9 4.1 copy-start.79
  233.9 4.1 copy-start.78
  233.9 4.1 copy-start.107
  233.9 4.1 copy-start.106
  233.9 4.1 copy-start.85
  233.9 4.1 copy-start.77
  233.9 4.2 copy-start.95
  233.9 4.2 copy-start.91
  238.8 6.7 %copy-start.39 = (bf16[256,768]{1,0:T(8,128)(2,1)}, bf16[256,768]{1,0:T(8,128)(2,1)S(1)}, u32[]{:S(2)}) copy-start(bf16[256,768]{1,0:T(8,128)(2,1)S(1)} %get-tuple-element.93) | copy-start | bytes 1179652
  238.8 2.8 copy-start.112
  239.6 6.0 %slice-start.3 = ((s8[9437184]{0:T(1024)(128)(4,1)}), s8[4194304]{0:T(1024)(128)(4,1)S(1)}, s32[]{:S(2)}) async-start(s8[9437184]{0:T(1024)(128)(4,1)} %bitcast.401), calls=%async_computation.3 | async-start | bytes 8388608
  241.6 3.9 slice-start.4
  241.6 3.9 slice-start.5
  248.8 5.0 %copy-start.98 = (f32[256]{0:T(256)}, f32[256]{0:T(256)S(1)}, u32[]{:S(2)}) copy-start(f32[256]{0:T(256)S(1)} %negate_multiply_fusion.1) | copy-start | bytes 3076
  250.5 3.4 copy-start.40
  258.8 4.6 %copy-start.14 = (f32[12,256,256]{1,2,0:T(8,128)S(1)}, f32[12,256,256]{1,2,0:T(8,128)}, u32[]{:S(2)}) copy-start(f32[12,256,256]{1,2,0:T(8,128)} %get-tuple-element.155) | copy-start | bytes 9437188
  258.8 4.7 %copy-start.46 = (bf16[256,768]{0,1:T(8,128)(2,1)S(1)}, bf16[256,768]{0,1:T(8,128)(2,1)}, u32[]{:S(2)}) copy-start(bf16[256,768]{0,1:T(8,128)(2,1)} %copy-done.45) | copy-start | bytes 1179652
  269.5 3.9 copy-start.97
  269.6 3.9 copy-start.83
  273.4 2.7 copy-start.11
  293.0 130.0 %copy-start.1 = (s32[2,256]{1,0:T(2,128)S(1)}, s32[2,256]{1,0:T(2,128)}, u32[]{:S(2)}) copy-start(s32[2,256]{1,0:T(2,128)} %param.19) | copy-start | bytes 6148
  410.8 11.5 %copy-start.57 = (f32[2,24,768]{2,1,0:T(8,128)S(1)}, f32[2,24,768]{2,1,0:T(8,128)}, u32[]{:S(2)}) copy-start(f32[2,24,768]{2,1,0:T(8,128)} %get-tuple-element.233) | copy-start | bytes 442372
  (74 other events, 128.2 us)

commit v2 on v0

v2 whole, which is shorter than its diff:
```python
import types

import jax
import jax.numpy as jnp
from jax import lax
from jax.experimental import pallas as pl
from jax.experimental.pallas import tpu as pltpu
from jax.sharding import PartitionSpec as P

HEAD = 64
HEADS = 12
LAYERS = 2
D = 768
FF = 3072
MESH = pl.DeviceIdType.MESH
BF16, F32 = jnp.bfloat16, jnp.float32

AXES = {"q": "yczx", "u": "yczx", "d": "czxy"}
STREAMS = {
    "q": ((slice(0, 32), "xyz"), (slice(32, 48), "xzy")),
    "u": ((slice(0, 32), "xyz"), (slice(32, 48), "xzy")),
    "d": ((slice(0, 32), "xzy"), (slice(32, 48), "yzx")),
}
FIRST = {
    "q": ((slice(0, 48), "x"),),
    "u": ((slice(0, 48), "x"),),
    "d": ((slice(0, 32), "x"), (slice(32, 48), "y")),
}
KINDS = "qud"
ALL = slice(None)
STEPS = (1, 3, 2)


def place():
    dp, core = lax.axis_index("dp"), lax.axis_index("fsdp")
    return {"z": dp // 16, "x": (dp // 4) % 4, "y": dp % 4, "c": core}


def device(at):
    return ((at["z"] * 4 + at["x"]) * 4 + at["y"], at["c"])


def moved(at, axis, step):
    size = 2 if axis == "c" else 4
    return {**at, axis: (at[axis] + step) % size}


class Links:
    def __init__(self, send_sems, recv_sems):
        self.send_sems, self.recv_sems, self.used, self.open = send_sems, recv_sems, 0, []

    def copy(self, src, dst, target, number):
        return pltpu.make_async_remote_copy(
            src_ref=src,
            dst_ref=dst,
            send_sem=self.send_sems.at[number],
            recv_sem=self.recv_sems.at[number],
            device_id=device(target),
            device_id_type=MESH,
        )

    def take(self, count):
        self.used += count
        return self.used - count

    def send(self, src, dst, target):
        copy = self.copy(src, dst, target, self.take(1))
        copy.start()
        self.open.append(copy)
        return copy

    def drain(self):
        for copy in self.open:
            copy.wait_send()
        self.open = []


def greet(me):
    partners = [moved(moved(me, "y", dy), "c", dc) for dy in range(4) for dc in range(2)][1:]
    partners += [moved(me, axis, step) for axis in "xz" for step in (1, 2, 3)]
    barrier = pltpu.get_barrier_semaphore()
    for partner in partners:
        pl.semaphore_signal(barrier, inc=1, device_id=device(partner), device_id_type=MESH)
    pl.semaphore_wait(barrier, len(partners))


T = 256
ROWS = 128
GAIN1, OFF1, BIAS_Q, BIAS_OUT, GAIN2, OFF2, BIAS_UP, BIAS_DOWN = 0, 1, 2, 5, 6, 7, 8, 12


def dot(a, b):
    return jnp.dot(a, b, preferred_element_type=F32)


def dot_nt(a, b):
    return lax.dot_general(a, b, (((1,), (1,)), ((), ())), preferred_element_type=F32)


def dot_tn(a, b):
    return lax.dot_general(a, b, (((0,), (0,)), ((), ())), preferred_element_type=F32)


def slab(ref, layer, index):
    return jnp.concatenate([ref[layer, index, core].reshape(D, 384) for core in range(2)], axis=1)


def chunk(ref, layer, index):
    return jnp.concatenate([ref[layer, core, index].reshape(D, 384) for core in range(2)], axis=1)


def put_slab(ref, layer, index, value):
    for core in range(2):
        ref[layer, index, core] = value[:, core * 384 : (core + 1) * 384].reshape(4, 4, 48, 384)


def put_chunk(ref, layer, index, value):
    for core in range(2):
        ref[layer, core, index] = value[:, core * 384 : (core + 1) * 384].reshape(4, 4, 48, 384)


def rows_of(index):
    return pl.ds(pl.multiple_of(index * ROWS, ROWS), ROWS)


def normal(x):
    center = x - jnp.mean(x, axis=-1, keepdims=True)
    scale = lax.rsqrt(jnp.mean(center * center, axis=-1, keepdims=True) + 1e-05)
    return center * scale, scale


def norm_into(x_ref, vec, gain, offset, out_ref):
    @pl.loop(0, T // ROWS)
    def _(index):
        rows = rows_of(index)
        hat, _ = normal(x_ref[rows, :].astype(F32))
        out_ref[rows, :] = (hat * vec[gain : gain + 1, :] + vec[offset : offset + 1, :]).astype(BF16)


def fold(value):
    return jnp.sum(value.reshape(ROWS // 8, 8, value.shape[1]), axis=0)


def total(value):
    return jnp.sum(value, axis=0, keepdims=True)


def norm_back(x_ref, grad_ref, vec, sums, gain, offset, top_ref, out_ref, bias=None, low_ref=None):
    zero = jnp.zeros((8, D), F32)

    def body(index, carry):
        sum_gain, sum_offset, sum_bias = carry
        rows = rows_of(index)
        hat, scale = normal(x_ref[rows, :].astype(F32))
        grad = grad_ref[rows, :]
        scaled = grad * vec[gain : gain + 1, :]
        inner = scaled - jnp.mean(scaled, axis=-1, keepdims=True)
        inner -= hat * jnp.mean(scaled * hat, axis=-1, keepdims=True)
        result = top_ref[rows, :] + scale * inner
        out_ref[rows, :] = result
        low = result.astype(BF16)
        if low_ref is not None:
            low_ref[rows, :] = low
        return sum_gain + fold(grad * hat), sum_offset + fold(grad), sum_bias + fold(low.astype(F32))

    sum_gain, sum_offset, sum_bias = lax.fori_loop(0, T // ROWS, body, (zero, zero, zero))
    sums[gain : gain + 1, :] = total(sum_gain)
    sums[offset : offset + 1, :] = total(sum_offset)
    if bias is not None:
        sums[bias : bias + 1, :] = total(sum_bias)


def gelu_parts(u):
    inner = 0.7978845608028654 * (u + 0.044715 * u * u * u)
    t = jnp.tanh(inner)
    slope = 0.7978845608028654 * (1.0 + 0.134145 * u * u)
    half = 0.5 * (1.0 + t)
    return u * half, half + 0.5 * u * (1.0 - t * t) * slope


def gelu(u):
    return 0.5 * u * (1.0 + jnp.tanh(0.7978845608028654 * (u + 0.044715 * u * u * u)))


def head_mask(which, scale=1.0):
    lane = lax.broadcasted_iota(jnp.int32, (1, 128), 1)
    return jnp.where(lane // HEAD == which, scale, 0.0).astype(BF16)


def lanes_of(pair):
    return pl.ds(pl.multiple_of(pair * 128, 128), 128)


def forward_qkv(layer, m):
    norm_into(m.x[layer], m.vec.at[layer], GAIN1, OFF1, m.h.at[layer])

    @pl.loop(0, 3)
    def _(part):
        bias = m.vec[layer, pl.ds(BIAS_Q + part, 1), :]
        m.qkv[layer, part] = (dot(m.h[layer], slab(m.wq, layer, part)) + bias).astype(BF16)


def forward_attention(layer, m):
    @pl.loop(0, HEADS // 2)
    def _(pair):
        lanes = lanes_of(pair)
        query, keys, values = (m.qkv[layer, part, :, lanes] for part in range(3))
        attended = jnp.zeros((T, 128), F32)
        for which in range(2):
            scores = dot_nt(query * head_mask(which, 0.125), keys)
            grown = jnp.exp(scores - jnp.max(scores, axis=-1, keepdims=True))
            probs = grown * (1.0 / jnp.sum(grown, axis=-1, keepdims=True))
            probs = probs.astype(BF16)
            m.probs[layer, 2 * pair + which] = probs
            attended += dot(probs, values * head_mask(which))
        m.o[layer, :, lanes] = attended.astype(BF16)


def forward_out(layer, m):
    m.mid[layer] = (
        m.x[layer][...].astype(F32)
        + dot(m.o[layer], slab(m.wq, layer, 3))
        + m.vec[layer, BIAS_OUT : BIAS_OUT + 1, :]
    )
    norm_into(m.mid.at[layer], m.vec.at[layer], GAIN2, OFF2, m.h2.at[layer])


def forward_up(layer, m):
    @pl.loop(0, 4)
    def _(index):
        bias = m.vec[layer, pl.ds(BIAS_UP + index, 1), :]
        u = dot(m.h2[layer], slab(m.wu, layer, index)) + bias
        m.u[layer, index] = u.astype(BF16)
        m.a[index] = gelu(u).astype(BF16)


def forward_down(layer, m):
    out = m.x[layer + 1]
    out[...] = m.mid[layer] + m.vec[layer, BIAS_DOWN : BIAS_DOWN + 1, :]

    @pl.loop(0, 4)
    def _(index):
        out[...] += dot(m.a[index], chunk(m.wd, layer, index))


def backward_ffn(layer, m, index):
    grad_active = dot_nt(m.gz[...], chunk(m.wd, layer, index))
    active, slope = gelu_parts(m.u[layer, index].astype(F32))
    pre = (grad_active * slope).astype(BF16)
    m.gu[...] = pre
    m.a[0] = active.astype(BF16)
    m.sums[layer, pl.ds(BIAS_UP + index, 1), :] = total(pre.astype(F32))
    m.gh[...] += dot_nt(m.gu[...], slab(m.wu, layer, index))
    put_chunk(m.wd, layer, index, dot_tn(m.a[0], m.gz[...]).astype(BF16))
    put_slab(m.wu, layer, index, dot_tn(m.h2[layer], m.gu[...]).astype(BF16))


def backward_mid(layer, m):
    norm_back(
        m.mid.at[layer], m.gh, m.vec.at[layer], m.sums.at[layer], GAIN2, OFF2, m.g, m.g, BIAS_OUT, m.gz
    )
    m.go[...] = dot_nt(m.gz[...], slab(m.wq, layer, 3)).astype(BF16)
    put_slab(m.wq, layer, 3, dot_tn(m.o[layer], m.gz[...]).astype(BF16))


def backward_attention(layer, m):
    @pl.loop(0, HEADS // 2)
    def _(pair):
        lanes = lanes_of(pair)
        query, keys, values = (m.qkv[layer, part, :, lanes] for part in range(3))
        grad = m.go[:, lanes]
        zero = jnp.zeros((T, 128), F32)
        grad_query, grad_keys, grad_values = zero, zero, zero
        for which in range(2):
            low = m.probs[layer, 2 * pair + which]
            probs = low.astype(F32)
            part = grad * head_mask(which)
            grad_probs = dot_nt(part, values)
            grad_values += dot_tn(low, part)
            row_dot = jnp.sum(grad_probs * probs, axis=-1, keepdims=True)
            grad_scores = (probs * (grad_probs - row_dot)).astype(BF16)
            grad_query += dot(grad_scores, keys * head_mask(which, 0.125))
            grad_keys += dot_tn(grad_scores, query * head_mask(which, 0.125))
        for part, value in enumerate((grad_query, grad_keys, grad_values)):
            m.gqkv[part, :, lanes] = value.astype(BF16)


def backward_qkv(layer, m, part):
    m.sums[layer, pl.ds(BIAS_Q + part, 1), :] = total(m.gqkv[part].astype(F32))
    m.gh[...] += dot_nt(m.gqkv[part], slab(m.wq, layer, part))
    put_slab(m.wq, layer, part, dot_tn(m.h[layer], m.gqkv[part]).astype(BF16))


def backward_in(layer, m, out_ref):
    norm_back(m.x[layer], m.gh, m.vec.at[layer], m.sums.at[layer], GAIN1, OFF1, m.g, out_ref)


def upstream(order_ref, remaining_ref, cot_ref, m):
    live = lax.broadcasted_iota(jnp.int32, (1, T), 1) >= T - remaining_ref

    def body(index, carry):
        rows = rows_of(index)
        spot = index * ROWS + lax.broadcasted_iota(jnp.int32, (ROWS, 1), 0)
        hit = jnp.where((order_ref == spot) & live, 1.0, 0.0)
        mask = jnp.max(hit, axis=-1, keepdims=True)
        grad = cot_ref[rows, :].astype(F32) * mask
        m.g[rows, :] = grad
        return carry

    lax.fori_loop(0, T // ROWS, body, 0)


def top(layer, m):
    def body(index, carry):
        rows = rows_of(index)
        low = m.g[rows, :].astype(BF16)
        m.gz[rows, :] = low
        return carry + fold(low.astype(F32))

    sums = lax.fori_loop(0, T // ROWS, body, jnp.zeros((8, D), F32))
    m.sums[layer, BIAS_DOWN : BIAS_DOWN + 1, :] = total(sums)
    m.gh[...] = jnp.zeros((T, D), F32)


class Gather:
    def __init__(self, kind, layer, m):
        self.kind, self.layer, self.m = kind, layer, m
        self.streams, self.handed = STREAMS[kind], []

    def part(self, rows, at):
        index = tuple(at[axis] for axis in AXES[self.kind])
        return self.m.weights[self.kind].at[(self.layer, *index, rows, ALL)]

    def hand_over(self, rows, at):
        part = self.part(rows, at)
        self.handed.append(self.m.links.send(part, part, moved(self.m.me, "c", 1)))

    def out(self, rows, at, axis, steps):
        part, me = self.part(rows, at), self.m.me
        return {step: self.m.links.send(part, part, moved(me, axis, step)) for step in steps}

    def first(self):
        me = self.m.me
        self.copies = [self.out(rows, me, axis, STEPS) for rows, axis in FIRST[self.kind]]

    def second(self):
        me = self.m.me
        for (rows, axis), copies in zip(FIRST[self.kind], self.copies):
            for step in STEPS:
                copies[step].wait_recv()
            self.hand_over(rows, {**me, axis: ALL})
        self.copies = [
            self.out(rows, {**me, axes[0]: ALL}, axes[1], STEPS) for rows, axes in self.streams
        ]

    def third(self):
        me = self.m.me
        for (rows, axes), copies in zip(self.streams, self.copies):
            for step in STEPS:
                copies[step].wait_recv()
                self.hand_over(rows, {**moved(me, axes[1], -step), axes[0]: ALL})
        self.copies = [
            self.out(rows, {**me, axes[0]: ALL, axes[1]: ALL}, axes[2], (1, 3))
            for rows, axes in self.streams
        ]

    def relay(self):
        me, self.halves = self.m.me, []
        for (rows, axes), copies in zip(self.streams, self.copies):
            for step, start in ((1, 0), (3, 2)):
                copies[step].wait_recv()
                came = {**moved(me, axes[2], -step), axes[1]: ALL}
                half = self.part(rows, {**came, axes[0]: pl.ds(start, 2)})
                self.halves.append(self.m.links.send(half, half, moved(me, axes[2], step)))
                self.hand_over(rows, {**came, axes[0]: ALL})

    def finish(self):
        for copy in self.halves:
            copy.wait_recv()
        for rows, axes in self.streams:
            self.hand_over(rows, {**moved(self.m.me, axes[2], 2), axes[0]: ALL, axes[1]: ALL})

    def arrive(self):
        for copy in self.handed:
            copy.wait_recv()


class Scatter:
    def __init__(self, kind, layer, m):
        self.kind, self.layer, self.m = kind, layer, m
        self.streams = [(rows, axes[::-1]) for rows, axes in STREAMS[kind]]
        self.base = m.links.take(4)
        self.slots = [m.first[kind, number] for number in range(2)]
        self.later = [m.second[kind, number].at[layer] for number in range(2)]
        self.last = [m.third[kind, number].at[layer] for number in range(2)]
        self.free = [m.free.at[2 * KINDS.index(kind) + number] for number in range(2)]
        self.room, self.got = (m.free.at[6], m.got_d) if kind == "d" else (m.free.at[7], m.got_qu)

    def part(self, rows, at):
        index = tuple(at.get(axis, ALL) for axis in AXES[self.kind])
        return self.m.weights[self.kind].at[(self.layer, *index, rows, ALL)]

    def between(self, index):
        axis, sibling = ("z" if self.kind == "d" else "y"), moved(self.m.me, "c", 1)
        src = self.part(ALL, {axis: index, "c": sibling["c"]})
        return self.m.links.copy(src, self.got.at[index], sibling, self.base + index)

    def wait_room(self):
        pl.semaphore_wait(self.room, 1)

    def join(self, more):
        m, me = self.m, self.m.me
        axis, others = ("z", "xy") if self.kind == "d" else ("y", "zx")
        for index in range(4):
            copy = self.between(index)
            copy.wait_recv()
            m.links.open.append(copy)

        @pl.loop(0, 16)
        def _(spot):
            for third in range(4):
                at = {axis: spot // 4, others[0]: spot % 4, others[1]: third, "c": me["c"]}
                own = self.part(ALL, at)
                own[...] += self.got[spot // 4, spot % 4, third]

        if more:
            pl.semaphore_signal(
                self.room, inc=1, device_id=device(moved(me, "c", 1)), device_id_type=MESH
            )
        self.copies = []
        for (rows, axes), slots, free in zip(self.streams, self.slots, self.free):
            if self.layer == 0:
                pl.semaphore_wait(free, 3)
            for step in STEPS:
                target = moved(me, axes[0], step)
                src = self.part(rows, {"c": me["c"], axes[0]: target[axes[0]]})
                self.copies.append(m.links.send(src, slots.at[step - 1], target))

    def rest(self, done):
        return [axis for axis in AXES[self.kind] if axis != "c" and axis not in done]

    def add(self, target, slots):
        value = target[...].astype(F32)
        for slot in slots:
            value += slot[...].astype(F32)
        return value

    def second(self):
        m, me = self.m, self.m.me
        for copy in self.copies:
            copy.wait_recv()
        self.copies = []
        for (rows, axes), slots, later, free in zip(
            self.streams, self.slots, self.later, self.free
        ):
            here = {"c": me["c"], axes[0]: me[axes[0]]}
            others = self.rest(here)

            @pl.loop(0, 4)
            def _(one):
                for two in range(4):
                    target = self.part(rows, {**here, others[0]: one, others[1]: two})
                    total = self.add(target, [slots.at[step, one, two] for step in range(3)])
                    target[...] = total.astype(BF16)

            if self.layer == 1:
                for step in STEPS:
                    peer = device(moved(me, axes[0], step))
                    pl.semaphore_signal(free, inc=1, device_id=peer, device_id_type=MESH)
            for step in STEPS:
                target = moved(me, axes[1], step)
                src = self.part(rows, {**here, axes[1]: target[axes[1]]})
                self.copies.append(m.links.send(src, later.at[step - 1], target))

    def third(self):
        m, me = self.m, self.m.me
        for copy in self.copies:
            copy.wait_recv()
        self.copies = []
        for (rows, axes), later, last in zip(self.streams, self.later, self.last):
            here = {"c": me["c"], axes[0]: me[axes[0]], axes[1]: me[axes[1]]}
            for one in range(4):
                target = self.part(rows, {**here, axes[2]: one})
                target[...] = self.add(target, [later.at[step, one] for step in range(3)]).astype(BF16)
            for step in STEPS:
                target = moved(me, axes[2], step)
                src = self.part(rows, {**here, axes[2]: target[axes[2]]})
                self.copies.append(m.links.send(src, last.at[step - 1], target))

    def finish(self):
        for copy in self.copies:
            copy.wait_recv()
        for (rows, _), last in zip(self.streams, self.last):
            total = self.add(self.part(rows, self.m.me), [last.at[step] for step in range(3)])
            self.m.totals[self.kind][self.layer, rows, :] = total


def spot_matrix(base, width):
    row = lax.broadcasted_iota(jnp.int32, (128, D), 0)
    lane = lax.broadcasted_iota(jnp.int32, (128, D), 1)
    return jnp.where((lane == base + row) & (row < width), 1.0, 0.0).astype(BF16)


def flag(condition):
    return jnp.where(condition, 1.0, 0.0).astype(F32)


NARROW_ROWS = (GAIN1, OFF1, BIAS_OUT, GAIN2, OFF2, BIAS_DOWN)


def spread_vectors(index, narrow, wide_qv, wide_up, stage, out):
    stage[...] = jnp.zeros(stage.shape, F32)
    for layer in range(LAYERS):
        rows = slice(layer, layer + 1)
        for row, vector in zip(NARROW_ROWS, narrow):
            stage[0, layer, row : row + 1, 0:6] = vector[rows, :].astype(F32)
        pair = wide_qv[rows, :].astype(F32)
        stage[1, layer, BIAS_Q : BIAS_Q + 1, 0:12] = pair * flag(index < 64)
        stage[1, layer, BIAS_Q + 2 : BIAS_Q + 3, 0:12] = pair * flag(index >= 64)
        for row in range(4):
            up = wide_up[rows, :].astype(F32) * flag(index // 32 == row)
            stage[2, layer, BIAS_UP + row : BIAS_UP + row + 1, 0:24] = up
    for layer in range(LAYERS):
        total = jnp.zeros((16, D), F32)
        for number, matrix in enumerate(spot_matrices(index)):
            total += dot(stage[number, layer].astype(BF16), matrix)
        out[layer] = total


def spot_matrices(index):
    return (
        spot_matrix(6 * index, 6), spot_matrix(12 * (index % 64), 12), spot_matrix(24 * (index % 32), 24)
    )


def own_entries(index, total, out):
    for layer in range(LAYERS):
        value = total[layer]
        high = value.astype(BF16)
        middle = (value - high.astype(F32)).astype(BF16)
        low = (value - high.astype(F32) - middle.astype(F32)).astype(BF16)
        found = []
        for matrix in spot_matrices(index):
            found.append(dot_nt(high, matrix) + (dot_nt(middle, matrix) + dot_nt(low, matrix)))
        for place_out, row in enumerate(NARROW_ROWS):
            out[layer, place_out : place_out + 1, :] = found[0][row : row + 1]
        out[layer, 6:7, :] = found[1][BIAS_Q : BIAS_Q + 1] * flag(index < 64) + found[1][
            BIAS_Q + 2 : BIAS_Q + 3
        ] * flag(index >= 64)
        up = jnp.zeros((1, 128), F32)
        for row in range(4):
            up += found[2][BIAS_UP + row : BIAS_UP + row + 1] * flag(index // 32 == row)
        out[layer, 7:8, :] = up


class VectorSum:
    ORDER = "xyzc"

    def __init__(self, m):
        self.m, self.number = m, 0

    def begin(self):
        m, axis = self.m, self.ORDER[self.number]
        self.copies = [
            m.links.send(
                m.vec_state.at[self.number],
                m.vec_recv.at[3 * self.number + step - 1],
                moved(m.me, axis, step),
            )
            for step in range(1, 2 if axis == "c" else 4)
        ]

    def end(self):
        m, total = self.m, self.m.vec_state[self.number]
        for copy in self.copies:
            copy.wait_recv()
        for step in range(len(self.copies)):
            total += m.vec_recv[3 * self.number + step]
        self.number += 1
        if self.number < 4:
            m.vec_state[self.number] = total
        return total

    def turn(self):
        self.end()
        self.begin()


def kernel(
    hidden, cot, order, remaining, w_qkv, w_out, w_up, w_down,
    gain1, off1, bias_qv, bias_out, gain2, off2, bias_up, bias_down,
    out, grad, g_qkv, g_out, g_up, g_down, vec_out,
    wq, wu, wd, got_qu, got_d, q_a, q_b, u_a, u_b, d_a, d_b, q_a2, q_b2, u_a2, u_b2, d_a2, d_b2,
    q_a3, q_b3, u_a3, u_b3, d_a3, d_b3, sum_q, sum_u, sum_d,
    x0, x1, h, qkv, probs, o, mid, h2, u, tmp, g, gh, gz, cots, outs, vec, sums,
    vec_state, vec_recv, stage, send_a, recv_a, send_d, recv_d, asm, send_f, recv_f, send_df, recv_df,
    send_sems, recv_sems, local_sems, free,
):
    me = place()
    sibling = moved(me, "c", 1)
    mine = 2 * me["y"] + me["c"]
    index = ((me["z"] * 4 + me["x"]) * 4 + me["y"]) * 2 + me["c"]
    links = Links(send_sems, recv_sems)
    m = types.SimpleNamespace(
        me=me, links=links, weights={"q": wq, "u": wu, "d": wd}, wq=wq, wu=wu, wd=wd,
        got_qu=got_qu, got_d=got_d, free=free, totals={"q": sum_q, "u": sum_u, "d": sum_d},
        first={("q", 0): q_a, ("q", 1): q_b, ("u", 0): u_a, ("u", 1): u_b, ("d", 0): d_a, ("d", 1): d_b},
        second={
            ("q", 0): q_a2, ("q", 1): q_b2, ("u", 0): u_a2, ("u", 1): u_b2, ("d", 0): d_a2, ("d", 1): d_b2
        },
        third={
            ("q", 0): q_a3, ("q", 1): q_b3, ("u", 0): u_a3, ("u", 1): u_b3, ("d", 0): d_a3, ("d", 1): d_b3
        },
        x=[x0, x1, g], h=h, qkv=qkv, probs=probs, o=o, mid=mid, h2=h2, u=u, a=tmp, g=g, gh=gh, gz=gz,
        gu=tmp.at[1], go=tmp.at[3], gqkv=tmp, vec=vec, sums=sums, vec_state=vec_state, vec_recv=vec_recv,
    )

    asm[...] = jnp.zeros(asm.shape, F32)
    send_f[...] = jnp.zeros(send_f.shape, F32)
    for owner in range(8):
        columns = slice(384 * (owner % 2), 384 * (owner % 2) + 384)
        for layer in range(LAYERS):
            for row in range(6):
                if owner < 6:
                    part = w_qkv[row, layer : layer + 1, 384 * owner : 384 * owner + 384]
                else:
                    part = w_out[row, layer : layer + 1, columns]
                asm[owner, 8 * layer + row : 8 * layer + row + 1, :] = part.astype(F32)
                part = w_up[row, layer : layer + 1, 384 * owner : 384 * owner + 384]
                asm[owner, 16 + 8 * layer + row : 17 + 8 * layer + row, :] = part.astype(F32)
    for owner in range(8):
        send_a[owner] = asm[owner, 0:32, :].astype(BF16)
    for half in range(2):
        for layer in range(LAYERS):
            part = w_down[layer, :, 384 * half : 384 * half + 384]
            send_df[half, 24 * layer : 24 * layer + 24, :] = part.astype(F32)
        send_d[half] = send_df[half].astype(BF16)
    narrow = (gain1, off1, bias_out, gain2, off2, bias_down)
    spread_vectors(index, narrow, bias_qv, bias_up, stage, vec_state.at[0])

    greet(me)

    def group_sends(src, dst):
        copies = []
        for dy in range(4):
            for dc in range(2):
                if dy or dc:
                    target = moved(moved(me, "y", dy), "c", dc)
                    spot = src.at[2 * target["y"] + target["c"]]
                    copies.append(links.send(spot, dst.at[mine], target))
        return copies

    arrivals = group_sends(send_a, recv_a)
    arrivals.append(links.send(send_d.at[1 - me["c"]], recv_d.at[me["c"]], sibling))
    recv_a[mine] = send_a[mine]
    recv_d[me["c"]] = send_d[me["c"]]
    here = pl.ds(pl.multiple_of(128 * me["c"], 128), 128)
    there = pl.ds(pl.multiple_of(128 * (1 - me["c"]), 128), 128)
    halves = []
    for number, (src, dst) in enumerate(((hidden, x0), (cot, cots))):
        halves.append(links.send(src.at[1 - me["c"]], dst.at[here, :], sibling))
        copy = pltpu.make_async_copy(src.at[me["c"]], dst.at[here, :], local_sems.at[number])
        copy.start()
        halves.append(copy)
    vectors = VectorSum(m)
    vectors.begin()
    for copy in arrivals:
        copy.wait_recv()
    gathers = [Gather(kind, layer, m) for layer in range(LAYERS) for kind in KINDS]
    own = (me["y"], me["c"], me["z"], me["x"])
    for layer in range(LAYERS):
        for group, target in enumerate((wq, wu)):
            for source in range(8):
                rows = slice(16 * group + 8 * layer, 16 * group + 8 * layer + 6)
                asm[group, 6 * source : 6 * source + 6, :] = recv_a[source].astype(F32)[rows]
            target[(layer, *own)] = asm[group].astype(BF16)
        for half in range(2):
            asm[2, 24 * half : 24 * half + 24, :] = recv_d[half].astype(F32)[
                24 * layer : 24 * layer + 24
            ]
        wd[layer, me["c"], me["z"], me["x"], me["y"]] = asm[2].astype(BF16)
        for gather in gathers[3 * layer : 3 * layer + 3]:
            gather.first()
    vectors.turn()
    gathers[0].second()
    vectors.turn()
    gathers[1].second()
    gathers[0].third()
    gathers[2].second()
    gathers[1].third()
    for gather in gathers[3:]:
        gather.second()
    vectors.turn()
    gathers[0].relay()
    gathers[2].third()
    gathers[0].finish()
    gathers[1].relay()
    gathers[3].third()
    vec[...] = vectors.end()
    halves[0].wait_recv()
    halves[1].wait()
    gathers[0].arrive()

    forward_qkv(0, m)
    gathers[1].finish()
    gathers[2].relay()
    gathers[4].third()
    forward_attention(0, m)
    forward_out(0, m)
    gathers[2].finish()
    gathers[3].relay()
    gathers[5].third()
    gathers[1].arrive()
    forward_up(0, m)
    gathers[3].finish()
    gathers[4].relay()
    gathers[2].arrive()
    forward_down(0, m)
    gathers[4].finish()
    gathers[5].relay()
    gathers[3].arrive()
    forward_qkv(1, m)
    gathers[5].finish()
    forward_attention(1, m)
    forward_out(1, m)
    gathers[4].arrive()
    forward_up(1, m)
    gathers[5].arrive()
    forward_down(1, m)
    outs[...] = g[...].astype(BF16)
    links.drain()
    halves[2].wait_recv()
    halves[3].wait()

    def swap(src, dst, number):
        remote = links.send(src.at[there, :], dst.at[me["c"]], sibling)
        copy = pltpu.make_async_copy(src.at[here, :], dst.at[me["c"]], local_sems.at[number])
        copy.start()
        return remote, copy

    results = [swap(outs, out, 2)]
    upstream(order[me["c"]], remaining[me["c"]], cots, m)
    sums[...] = jnp.zeros(sums.shape, F32)
    scatters = {(kind, layer): Scatter(kind, layer, m) for layer in (1, 0) for kind in KINDS}

    def ffn(layer):
        ups, downs = scatters["u", layer], scatters["d", layer]
        if layer == 0:
            ups.wait_room()
            downs.wait_room()

        @pl.loop(0, 4)
        def _(part):
            backward_ffn(layer, m, part)
            ups.between(part).start()
            downs.between(part).start()

    def attention_grads(layer):
        scatter = scatters["q", layer]
        scatter.wait_room()
        scatter.between(3).start()
        m.gh[...] = jnp.zeros((T, D), F32)

        @pl.loop(0, 3)
        def _(part):
            backward_qkv(layer, m, part)
            scatter.between(part).start()

    top(1, m)
    ffn(1)
    backward_mid(1, m)
    scatters["u", 1].join(True)
    scatters["d", 1].join(True)
    backward_attention(1, m)
    attention_grads(1)
    backward_in(1, m, g)
    top(0, m)
    scatters["q", 1].join(True)
    ffn(0)
    scatters["u", 1].second()
    scatters["d", 1].second()
    backward_mid(0, m)
    scatters["q", 1].second()
    scatters["u", 0].join(True)
    scatters["d", 0].join(False)
    backward_attention(0, m)
    scatters["u", 1].third()
    scatters["d", 1].third()
    attention_grads(0)
    scatters["q", 1].third()
    backward_in(0, m, g)
    results.append(swap(g, grad, 3))
    vec_state[0] = sums[...]
    scatters["q", 0].join(False)
    for kind in "udq":
        scatters[kind, 1].finish()
    vectors = VectorSum(m)
    vectors.begin()
    scatters["u", 0].second()
    scatters["d", 0].second()
    vectors.turn()
    scatters["q", 0].second()
    scatters["u", 0].third()
    scatters["d", 0].third()
    vectors.turn()
    scatters["q", 0].third()
    vectors.turn()
    for kind in "udq":
        scatters[kind, 0].finish()

    for layer in range(LAYERS):
        for owner in range(8):
            for group, total in enumerate((sum_q, sum_u)):
                start = 16 * group + 8 * layer
                send_f[owner, start : start + 6, :] = total[layer, 6 * owner : 6 * owner + 6, :]
        for owner in range(2):
            send_df[owner, 24 * layer : 24 * layer + 24, :] = sum_d[
                layer, 24 * owner : 24 * owner + 24, :
            ]
    last = group_sends(send_f, recv_f)
    last.append(links.send(send_df.at[1 - me["c"]], recv_df.at[me["c"]], sibling))
    recv_f[mine] = send_f[mine]
    recv_df[me["c"]] = send_df[me["c"]]
    sums[...] = vectors.end()
    own_entries(index, sums, vec_out)
    for copy in last:
        copy.wait_recv()
    for owner in range(8):
        columns = slice(384 * (owner % 2), 384 * (owner % 2) + 384)
        for layer in range(LAYERS):
            for row in range(6):
                spot = 8 * layer + row
                value = recv_f[owner, spot : spot + 1, :]
                if owner < 6:
                    g_qkv[row, layer : layer + 1, 384 * owner : 384 * owner + 384] = value
                else:
                    g_out[row, layer : layer + 1, columns] = value
                value = recv_f[owner, 16 + spot : 17 + spot, :]
                g_up[row, layer : layer + 1, 384 * owner : 384 * owner + 384] = value
    for layer in range(LAYERS):
        for half in range(2):
            g_down[layer, :, 384 * half : 384 * half + 384] = recv_df[
                half, 24 * layer : 24 * layer + 24, :
            ]
    for remote, copy in results:
        remote.wait_recv()
        copy.wait()
    links.drain()


def shards(
    hidden, cotangent, remaining, order,
    norm1_gain, norm1_bias, w_qkv, bias_qv, w_out, bias_out,
    norm2_gain, norm2_bias, w_up, bias_up, w_down, bias_down,
):
    vmem, hbm = pl.BlockSpec(memory_space=pltpu.VMEM), pl.BlockSpec(memory_space=pl.ANY)
    half = hidden.shape[1]
    swapped = [jnp.transpose(weight, (1, 0, 2)) for weight in (w_qkv, w_out, w_up)]
    wide, deep = (LAYERS, 4, 2, 4, 4, 48, 384), (LAYERS, 2, 4, 4, 4, 48, 384)
    sizes = [rows.stop - rows.start for kind in KINDS for rows, _ in STREAMS[kind]]
    out, grad, g_qkv, g_out, g_up, g_down, vecs = pl.pallas_call(
        kernel,
        out_shape=(
            jax.ShapeDtypeStruct((2, half, D), BF16),
            jax.ShapeDtypeStruct((2, half, D), F32),
            jax.ShapeDtypeStruct((6, LAYERS, 3 * D), F32),
            jax.ShapeDtypeStruct((6, LAYERS, D), F32),
            jax.ShapeDtypeStruct((6, LAYERS, FF), F32),
            jax.ShapeDtypeStruct((LAYERS, 24, D), F32),
            jax.ShapeDtypeStruct((LAYERS, 8, 128), F32),
        ),
        in_specs=[hbm, hbm] + [vmem] * 14,
        out_specs=(hbm, hbm) + (vmem,) * 5,
        scratch_shapes=[
            pltpu.VMEM(wide, BF16),
            pltpu.VMEM(wide, BF16),
            pltpu.VMEM(deep, BF16),
            pltpu.VMEM((4, 4, 4, 48, 384), BF16),
            pltpu.VMEM((4, 4, 4, 48, 384), BF16),
            *[pltpu.VMEM((3, 4, 4, size, 384), BF16) for size in sizes],
            *[pltpu.VMEM((LAYERS, 3, 4, size, 384), BF16) for size in sizes],
            *[pltpu.VMEM((LAYERS, 3, size, 384), BF16) for size in sizes],
            *[pltpu.VMEM((LAYERS, 48, 384), F32) for _ in range(3)],
            pltpu.VMEM((T, D), BF16),
            pltpu.VMEM((T, D), F32),
            pltpu.VMEM((LAYERS, T, D), BF16),
            pltpu.VMEM((LAYERS, 3, T, D), BF16),
            pltpu.VMEM((LAYERS, HEADS, T, T), BF16),
            pltpu.VMEM((LAYERS, T, D), BF16),
            pltpu.VMEM((LAYERS, T, D), F32),
            pltpu.VMEM((LAYERS, T, D), BF16),
            pltpu.VMEM((LAYERS, 4, T, D), BF16),
            pltpu.VMEM((4, T, D), BF16),
            pltpu.VMEM((T, D), F32),
            pltpu.VMEM((T, D), F32),
            pltpu.VMEM((T, D), BF16),
            pltpu.VMEM((T, D), BF16),
            pltpu.VMEM((T, D), BF16),
            pltpu.VMEM((LAYERS, 16, D), F32),
            pltpu.VMEM((LAYERS, 16, D), F32),
            pltpu.VMEM((4, LAYERS, 16, D), F32),
            pltpu.VMEM((10, LAYERS, 16, D), F32),
            pltpu.VMEM((3, LAYERS, 16, 128), F32),
            pltpu.VMEM((8, 32, 384), BF16),
            pltpu.VMEM((8, 32, 384), BF16),
            pltpu.VMEM((2, 48, 384), BF16),
            pltpu.VMEM((2, 48, 384), BF16),
            pltpu.VMEM((8, 48, 384), F32),
            pltpu.VMEM((8, 32, 384), F32),
            pltpu.VMEM((8, 32, 384), F32),
            pltpu.VMEM((2, 48, 384), F32),
            pltpu.VMEM((2, 48, 384), F32),
            pltpu.SemaphoreType.DMA((400,)),
            pltpu.SemaphoreType.DMA((400,)),
            pltpu.SemaphoreType.DMA((4,)),
            pltpu.SemaphoreType.REGULAR((8,)),
        ],
        compiler_params=pltpu.CompilerParams(
            collective_id=0, has_side_effects=True, vmem_limit_bytes=(63 << 20) + (1 << 19)
        ),
        name="layers",
    )(
        hidden, cotangent, order[:, None, :],
        jnp.broadcast_to(remaining[:, None, None], (2, 1, T)),
        *swapped, w_down,
        norm1_gain, norm1_bias, bias_qv, bias_out, norm2_gain, norm2_bias, bias_up, bias_down,
    )
    g_qkv, g_out, g_up = (jnp.transpose(part, (1, 0, 2)) for part in (g_qkv, g_out, g_up))
    gain1, off1, out_bias, gain2, off2, down = (vecs[:, row, 0:6] for row in range(6))
    return (
        out, grad, gain1, off1, g_qkv, vecs[:, 6, 0:12], g_out, out_bias,
        gain2, off2, g_up, vecs[:, 7, 0:24], g_down, down,
    )


def solution(mesh):
    tokens, rows = P("dp", "fsdp", None), P(None, ("dp", "fsdp"), None)
    vector = P(None, ("dp", "fsdp"))
    weights = (
        vector, vector, rows, vector, rows, vector, vector, vector, rows, vector, rows, vector
    )
    return jax.shard_map(
        shards,
        mesh=mesh,
        in_specs=(tokens, tokens, P("dp"), P("dp", None), *weights),
        out_specs=(tokens, tokens, *weights),
        check_vma=False,
    )
```

time: 1920 us -> 249 us (0.13); the launches traced: 1890 us -> 249 us
  blocking collectives: 501 us -> 0 us
  starting transfers between devices: 495 us -> 0 us
  waiting for transfers between devices: 388 us -> 0 us
  local copies, waits for them, and re-layouts: 297 us -> 11.7 us
  Pallas kernels: 0 us -> 236 us
  matrix products: 155 us -> 0 us
  other arithmetic: 37.7 us -> 0 us
  between operations: 19.9 us -> 0.69 us
    unnamed x197 -> x0, starting transfers between devices: 494 us -> none
    unnamed x2 -> x0, blocking collectives: 491 us -> none
    all_gather x8 -> x0, waiting for transfers between devices: 377 us -> none  [the longest x2 137 us: fetch(): lax.all_gather(w_up[layer_index], ('dp', 'fsdp'), axis=0, tiled=True)]
    unnamed x588 -> x20, local copies, waits for them, and re-layouts: 259 us -> 6.41 us
    pallas_call x0 -> x1, Pallas kernels: none -> 236 us  [shards(): pl.pallas_call(kernel, out_shape=(jax.ShapeDtypeStruct((2, half, D), BF16...]
    dot_general x36 -> x0, matrix products: 155 us -> none  [the longest x2 16.8 us: layer_forward(): jnp.einsum('shqk,skhe->sqhe', probs_low, values, preferred_element_type=j...]
  transfers between devices with their start and end apart: 207 -> 0, of which waited for: 11 -> 0; matrix products, arithmetic and copies ran while one was open for 43% -> 0% of each run, Pallas kernels for 0% -> 0%
where the time goes in v2:
time: 249 us
  Pallas kernels  236 us (95%)
  local copies, waits for them, and re-layouts  11.7 us (5%)
    pallas_call x1, Pallas kernels, shards(): pl.pallas_call(kernel, out_shape=(jax.ShapeDtypeStruct((2, half, D), BF16...  236 us
    unnamed x20, local copies, waits for them, and re-layouts  6.41 us

profile of v2, /device:TPU:1, one launch (start us, length us, event | category | flops | bytes accessed | tf_op | source)
XLA Modules:
  0.0 248.9 jit_solution(7267748139098253515)
XLA Ops:
  0.6 0.0 copy-start.6
  0.7 0.0 copy-start.5
  0.7 0.6 copy-done.6
  1.3 0.6 broadcast_in_dim.10.remaining
  1.9 0.0 copy-done.5
  2.0 0.6 broadcast_in_dim.4.order
  2.5 236.5 %layers.1 = (bf16[2,128,768]{2,1,0:T(8,128)(2,1)}, f32[2,128,768]{2,1,0:T(8,128)}, f32[6,2,2304]{2,1,0:T(2,128)}, f32[6,2,768]{2,1,0:T(2,128)}, f32[6,2,3072]{2,...) custom-call(bf16[2,128,768]{2,1,0:T(8,128)(2,1)} %hidden.1, bf16[2,128,768]{2,1,0:T(8,128)(2,1)} %cot.1, ...), custom_call_target="tpu_custom_call" | custom-call | tf_op jit(solution)/shard_map/layers/pallas_call | solution.py:861
  239.0 0.0 copy-start
  239.0 1.3 slice.26
  240.4 1.3 slice.30
  241.6 1.5 fusion
  243.1 1.8 copy.36
  244.9 0.0 copy-done
  244.9 0.0 copy-start.3
  244.9 0.9 copy.37
  245.8 0.1 copy-done.3
  245.9 0.0 copy-start.4
  245.9 0.0 copy-start.2
  245.9 0.6 copy.38
  246.6 0.1 copy-done.4
  246.7 0.6 copy.39
  247.3 0.0 copy-done.2
  247.3 0.0 copy-start.1
  247.3 0.7 copy.40
  248.0 0.3 copy-done.1
  248.3 0.7 copy.41
Async XLA Ops:
  0.6 0.7 copy-start.6
  0.7 1.3 copy-start.5
  239.0 5.9 %copy-start = (f32[2,128,768]{2,1,0:T(8,128)S(1)}, f32[2,128,768]{2,1,0:T(8,128)}, u32[]{:S(2)}) copy-start(f32[2,128,768]{2,1,0:T(8,128)} %get-tuple-element.49) | copy-start | bytes 2359300
  244.9 1.0 copy-start.3
  245.9 0.8 copy-start.4
  245.9 1.4 copy-start.2
  247.3 1.0 copy-start.1

commit v3 on v2

--- a/solution.py
+++ b/solution.py
@@ -16,16 +16,7 @@
 BF16, F32 = jnp.bfloat16, jnp.float32
 
 AXES = {"q": "yczx", "u": "yczx", "d": "czxy"}
-STREAMS = {
-    "q": ((slice(0, 32), "xyz"), (slice(32, 48), "xzy")),
-    "u": ((slice(0, 32), "xyz"), (slice(32, 48), "xzy")),
-    "d": ((slice(0, 32), "xzy"), (slice(32, 48), "yzx")),
-}
-FIRST = {
-    "q": ((slice(0, 48), "x"),),
-    "u": ((slice(0, 48), "x"),),
-    "d": ((slice(0, 32), "x"), (slice(32, 48), "y")),
-}
+STREAMS = ((slice(0, 16), "xyz"), (slice(16, 32), "yzx"), (slice(32, 48), "zxy"))
 KINDS = "qud"
 ALL = slice(None)
 STEPS = (1, 3, 2)
@@ -324,8 +315,7 @@
 
 class Gather:
     def __init__(self, kind, layer, m):
-        self.kind, self.layer, self.m = kind, layer, m
-        self.streams, self.handed = STREAMS[kind], []
+        self.kind, self.layer, self.m, self.handed = kind, layer, m, []
 
     def part(self, rows, at):
         index = tuple(at[axis] for axis in AXES[self.kind])
@@ -341,32 +331,29 @@
 
     def first(self):
         me = self.m.me
-        self.copies = [self.out(rows, me, axis, STEPS) for rows, axis in FIRST[self.kind]]
+        self.copies = [self.out(rows, me, axes[0], STEPS) for rows, axes in STREAMS]
 
     def second(self):
-        me = self.m.me
-        for (rows, axis), copies in zip(FIRST[self.kind], self.copies):
+        me, before = self.m.me, self.copies
+        self.copies = []
+        for (rows, axes), copies in zip(STREAMS, before):
             for step in STEPS:
                 copies[step].wait_recv()
-            self.hand_over(rows, {**me, axis: ALL})
-        self.copies = [
-            self.out(rows, {**me, axes[0]: ALL}, axes[1], STEPS) for rows, axes in self.streams
-        ]
+            self.copies.append(self.out(rows, {**me, axes[0]: ALL}, axes[1], STEPS))
 
     def third(self):
-        me = self.m.me
-        for (rows, axes), copies in zip(self.streams, self.copies):
+        me, before = self.m.me, self.copies
+        self.copies = []
+        for (rows, axes), copies in zip(STREAMS, before):
             for step in STEPS:
                 copies[step].wait_recv()
-                self.hand_over(rows, {**moved(me, axes[1], -step), axes[0]: ALL})
-        self.copies = [
-            self.out(rows, {**me, axes[0]: ALL, axes[1]: ALL}, axes[2], (1, 3))
-            for rows, axes in self.streams
-        ]
+            plane = {**me, axes[0]: ALL, axes[1]: ALL}
+            self.copies.append(self.out(rows, plane, axes[2], (1, 3)))
+            self.hand_over(rows, plane)
 
     def relay(self):
         me, self.halves = self.m.me, []
-        for (rows, axes), copies in zip(self.streams, self.copies):
+        for (rows, axes), copies in zip(STREAMS, self.copies):
             for step, start in ((1, 0), (3, 2)):
                 copies[step].wait_recv()
                 came = {**moved(me, axes[2], -step), axes[1]: ALL}
@@ -377,7 +364,7 @@
     def finish(self):
         for copy in self.halves:
             copy.wait_recv()
-        for rows, axes in self.streams:
+        for rows, axes in STREAMS:
             self.hand_over(rows, {**moved(self.m.me, axes[2], 2), axes[0]: ALL, axes[1]: ALL})
 
     def arrive(self):
@@ -388,13 +375,20 @@
 class Scatter:
     def __init__(self, kind, layer, m):
         self.kind, self.layer, self.m = kind, layer, m
-        self.streams = [(rows, axes[::-1]) for rows, axes in STREAMS[kind]]
+        number = KINDS.index(kind)
+        self.streams = [
+            (
+                rows,
+                axes[::-1],
+                m.first.at[number, stream],
+                m.second.at[layer, number, stream],
+                m.third.at[layer, number, stream],
+                m.free.at[3 * number + stream],
+            )
+            for stream, (rows, axes) in enumerate(STREAMS)
+        ]
         self.base = m.links.take(4)
-        self.slots = [m.first[kind, number] for number in range(2)]
-        self.later = [m.second[kind, number].at[layer] for number in range(2)]
-        self.last = [m.third[kind, number].at[layer] for number in range(2)]
-        self.free = [m.free.at[2 * KINDS.index(kind) + number] for number in range(2)]
-        self.room, self.got = (m.free.at[6], m.got_d) if kind == "d" else (m.free.at[7], m.got_qu)
+        self.room, self.got = (m.free.at[9], m.got_d) if kind == "d" else (m.free.at[10], m.got_qu)
 
     def part(self, rows, at):
         index = tuple(at.get(axis, ALL) for axis in AXES[self.kind])
@@ -410,7 +404,7 @@
 
     def join(self, more):
         m, me = self.m, self.m.me
-        axis, others = ("z", "xy") if self.kind == "d" else ("y", "zx")
+        axis, other = ("z", "x") if self.kind == "d" else ("y", "z")
         for index in range(4):
             copy = self.between(index)
             copy.wait_recv()
@@ -418,17 +412,15 @@
 
         @pl.loop(0, 16)
         def _(spot):
-            for third in range(4):
-                at = {axis: spot // 4, others[0]: spot % 4, others[1]: third, "c": me["c"]}
-                own = self.part(ALL, at)
-                own[...] += self.got[spot // 4, spot % 4, third]
+            own = self.part(ALL, {axis: spot // 4, other: spot % 4, "c": me["c"]})
+            own[...] += self.got[spot // 4, spot % 4]
 
         if more:
             pl.semaphore_signal(
                 self.room, inc=1, device_id=device(moved(me, "c", 1)), device_id_type=MESH
             )
         self.copies = []
-        for (rows, axes), slots, free in zip(self.streams, self.slots, self.free):
+        for rows, axes, slots, _, _, free in self.streams:
             if self.layer == 0:
                 pl.semaphore_wait(free, 3)
             for step in STEPS:
@@ -436,9 +428,6 @@
                 src = self.part(rows, {"c": me["c"], axes[0]: target[axes[0]]})
                 self.copies.append(m.links.send(src, slots.at[step - 1], target))
 
-    def rest(self, done):
-        return [axis for axis in AXES[self.kind] if axis != "c" and axis not in done]
-
     def add(self, target, slots):
         value = target[...].astype(F32)
         for slot in slots:
@@ -446,22 +435,19 @@
         return value
 
     def second(self):
-        m, me = self.m, self.m.me
-        for copy in self.copies:
-            copy.wait_recv()
+        m, me, before = self.m, self.m.me, self.copies
         self.copies = []
-        for (rows, axes), slots, later, free in zip(
-            self.streams, self.slots, self.later, self.free
-        ):
+        for number, (rows, axes, slots, later, _, free) in enumerate(self.streams):
+            for copy in before[3 * number : 3 * number + 3]:
+                copy.wait_recv()
             here = {"c": me["c"], axes[0]: me[axes[0]]}
-            others = self.rest(here)
+            other = [axis for axis in AXES[self.kind] if axis not in here][0]
 
             @pl.loop(0, 4)
-            def _(one):
-                for two in range(4):
-                    target = self.part(rows, {**here, others[0]: one, others[1]: two})
-                    total = self.add(target, [slots.at[step, one, two] for step in range(3)])
-                    target[...] = total.astype(BF16)
+            def _(index):
+                target = self.part(rows, {**here, other: index})
+                total = self.add(target, [slots.at[step, index] for step in range(3)])
+                target[...] = total.astype(BF16)
 
             if self.layer == 1:
                 for step in STEPS:
@@ -473,15 +459,14 @@
                 self.copies.append(m.links.send(src, later.at[step - 1], target))
 
     def third(self):
-        m, me = self.m, self.m.me
-        for copy in self.copies:
-            copy.wait_recv()
+        m, me, before = self.m, self.m.me, self.copies
         self.copies = []
-        for (rows, axes), later, last in zip(self.streams, self.later, self.last):
+        for number, (rows, axes, _, later, last, _) in enumerate(self.streams):
+            for copy in before[3 * number : 3 * number + 3]:
+                copy.wait_recv()
             here = {"c": me["c"], axes[0]: me[axes[0]], axes[1]: me[axes[1]]}
-            for one in range(4):
-                target = self.part(rows, {**here, axes[2]: one})
-                target[...] = self.add(target, [later.at[step, one] for step in range(3)]).astype(BF16)
+            target = self.part(rows, here)
+            target[...] = self.add(target, [later.at[step] for step in range(3)]).astype(BF16)
             for step in STEPS:
                 target = moved(me, axes[2], step)
                 src = self.part(rows, {**here, axes[2]: target[axes[2]]})
@@ -490,7 +475,7 @@
     def finish(self):
         for copy in self.copies:
             copy.wait_recv()
-        for (rows, _), last in zip(self.streams, self.last):
+        for rows, _, _, _, last, _ in self.streams:
             total = self.add(self.part(rows, self.m.me), [last.at[step] for step in range(3)])
             self.m.totals[self.kind][self.layer, rows, :] = total
 
@@ -524,7 +509,7 @@
         total = jnp.zeros((16, D), F32)
         for number, matrix in enumerate(spot_matrices(index)):
             total += dot(stage[number, layer].astype(BF16), matrix)
-        out[layer] = total
+        out[layer] = total.astype(BF16)
 
 
 def spot_matrices(index):
@@ -543,42 +528,42 @@
         for matrix in spot_matrices(index):
             found.append(dot_nt(high, matrix) + (dot_nt(middle, matrix) + dot_nt(low, matrix)))
         for place_out, row in enumerate(NARROW_ROWS):
-            out[layer, place_out : place_out + 1, :] = found[0][row : row + 1]
-        out[layer, 6:7, :] = found[1][BIAS_Q : BIAS_Q + 1] * flag(index < 64) + found[1][
-            BIAS_Q + 2 : BIAS_Q + 3
-        ] * flag(index >= 64)
+            out[place_out][layer : layer + 1, :] = found[0][row : row + 1, 0:6]
+        pair = found[1][BIAS_Q : BIAS_Q + 1] * flag(index < 64)
+        pair += found[1][BIAS_Q + 2 : BIAS_Q + 3] * flag(index >= 64)
+        out[6][layer : layer + 1, :] = pair[:, 0:12]
         up = jnp.zeros((1, 128), F32)
         for row in range(4):
             up += found[2][BIAS_UP + row : BIAS_UP + row + 1] * flag(index // 32 == row)
-        out[layer, 7:8, :] = up
+        out[7][layer : layer + 1, :] = up[:, 0:24]
 
 
 class VectorSum:
     ORDER = "xyzc"
 
-    def __init__(self, m):
-        self.m, self.number = m, 0
+    def __init__(self, m, state, recv):
+        self.m, self.state, self.recv, self.number = m, state, recv, 0
 
     def begin(self):
         m, axis = self.m, self.ORDER[self.number]
         self.copies = [
             m.links.send(
-                m.vec_state.at[self.number],
-                m.vec_recv.at[3 * self.number + step - 1],
+                self.state.at[self.number],
+                self.recv.at[3 * self.number + step - 1],
                 moved(m.me, axis, step),
             )
             for step in range(1, 2 if axis == "c" else 4)
         ]
 
     def end(self):
-        m, total = self.m, self.m.vec_state[self.number]
+        total = self.state[self.number].astype(F32)
         for copy in self.copies:
             copy.wait_recv()
         for step in range(len(self.copies)):
-            total += m.vec_recv[3 * self.number + step]
+            total += self.recv[3 * self.number + step].astype(F32)
         self.number += 1
         if self.number < 4:
-            m.vec_state[self.number] = total
+            self.state[self.number] = total.astype(self.state.dtype)
         return total
 
     def turn(self):
@@ -586,16 +571,27 @@
         self.begin()
 
 
-def kernel(
-    hidden, cot, order, remaining, w_qkv, w_out, w_up, w_down,
-    gain1, off1, bias_qv, bias_out, gain2, off2, bias_up, bias_down,
-    out, grad, g_qkv, g_out, g_up, g_down, vec_out,
-    wq, wu, wd, got_qu, got_d, q_a, q_b, u_a, u_b, d_a, d_b, q_a2, q_b2, u_a2, u_b2, d_a2, d_b2,
-    q_a3, q_b3, u_a3, u_b3, d_a3, d_b3, sum_q, sum_u, sum_d,
-    x0, x1, h, qkv, probs, o, mid, h2, u, tmp, g, gh, gz, cots, outs, vec, sums,
-    vec_state, vec_recv, stage, send_a, recv_a, send_d, recv_d, asm, send_f, recv_f, send_df, recv_df,
-    send_sems, recv_sems, local_sems, free,
-):
+def kernel(*refs):
+    inputs, refs = refs[:16], refs[16:]
+    outputs, refs = refs[:14], refs[14:]
+    staged, refs = refs[:14], refs[14:]
+    ready, refs = refs[:12], refs[12:]
+    (
+        wq, wu, wd, got_qu, got_d, first, second, third, sum_q, sum_u, sum_d,
+        x0, x1, h, qkv, probs, o, mid, h2, u, tmp, g, gh, gz, cots, outs, vec, sums,
+        low_state, low_recv, vec_state, vec_recv, stage,
+        send_a, recv_a, send_d, recv_d, asm, send_f, recv_f, send_df, recv_df,
+        send_sems, recv_sems, local_sems, free,
+    ) = refs
+    hidden, cot = inputs[:2]
+    out, grad = outputs[:2]
+    order, remaining, w_qkv, w_out, w_up, w_down, *vectors_in = staged
+    gain1, off1, bias_qv, bias_out, gain2, off2, bias_up, bias_down = vectors_in
+    g_qkv, g_out, g_up, g_down, *vectors_out = ready
+    loads = []
+    for number, (src, dst) in enumerate(zip(inputs[2:], staged)):
+        loads.append(pltpu.make_async_copy(src, dst, local_sems.at[4 + number]))
+        loads[-1].start()
     me = place()
     sibling = moved(me, "c", 1)
     mine = 2 * me["y"] + me["c"]
@@ -604,19 +600,14 @@
     m = types.SimpleNamespace(
         me=me, links=links, weights={"q": wq, "u": wu, "d": wd}, wq=wq, wu=wu, wd=wd,
         got_qu=got_qu, got_d=got_d, free=free, totals={"q": sum_q, "u": sum_u, "d": sum_d},
-        first={("q", 0): q_a, ("q", 1): q_b, ("u", 0): u_a, ("u", 1): u_b, ("d", 0): d_a, ("d", 1): d_b},
-        second={
-            ("q", 0): q_a2, ("q", 1): q_b2, ("u", 0): u_a2, ("u", 1): u_b2, ("d", 0): d_a2, ("d", 1): d_b2
-        },
-        third={
-            ("q", 0): q_a3, ("q", 1): q_b3, ("u", 0): u_a3, ("u", 1): u_b3, ("d", 0): d_a3, ("d", 1): d_b3
-        },
+        first=first, second=second, third=third,
         x=[x0, x1, g], h=h, qkv=qkv, probs=probs, o=o, mid=mid, h2=h2, u=u, a=tmp, g=g, gh=gh, gz=gz,
-        gu=tmp.at[1], go=tmp.at[3], gqkv=tmp, vec=vec, sums=sums, vec_state=vec_state, vec_recv=vec_recv,
+        gu=tmp.at[1], go=tmp.at[3], gqkv=tmp, vec=vec, sums=sums,
     )
-
-    asm[...] = jnp.zeros(asm.shape, F32)
     send_f[...] = jnp.zeros(send_f.shape, F32)
+    for copy in loads:
+        copy.wait()
+
     for owner in range(8):
         columns = slice(384 * (owner % 2), 384 * (owner % 2) + 384)
         for layer in range(LAYERS):
@@ -625,18 +616,18 @@
                     part = w_qkv[row, layer : layer + 1, 384 * owner : 384 * owner + 384]
                 else:
                     part = w_out[row, layer : layer + 1, columns]
-                asm[owner, 8 * layer + row : 8 * layer + row + 1, :] = part.astype(F32)
+                send_f[owner, 8 * layer + row : 8 * layer + row + 1, :] = part.astype(F32)
                 part = w_up[row, layer : layer + 1, 384 * owner : 384 * owner + 384]
-                asm[owner, 16 + 8 * layer + row : 17 + 8 * layer + row, :] = part.astype(F32)
+                send_f[owner, 16 + 8 * layer + row : 17 + 8 * layer + row, :] = part.astype(F32)
     for owner in range(8):
-        send_a[owner] = asm[owner, 0:32, :].astype(BF16)
+        send_a[owner] = send_f[owner].astype(BF16)
     for half in range(2):
         for layer in range(LAYERS):
             part = w_down[layer, :, 384 * half : 384 * half + 384]
             send_df[half, 24 * layer : 24 * layer + 24, :] = part.astype(F32)
         send_d[half] = send_df[half].astype(BF16)
     narrow = (gain1, off1, bias_out, gain2, off2, bias_down)
-    spread_vectors(index, narrow, bias_qv, bias_up, stage, vec_state.at[0])
+    spread_vectors(index, narrow, bias_qv, bias_up, stage, low_state.at[0])
 
     greet(me)
 
@@ -662,41 +653,47 @@
         copy = pltpu.make_async_copy(src.at[me["c"]], dst.at[here, :], local_sems.at[number])
         copy.start()
         halves.append(copy)
-    vectors = VectorSum(m)
-    vectors.begin()
     for copy in arrivals:
         copy.wait_recv()
     gathers = [Gather(kind, layer, m) for layer in range(LAYERS) for kind in KINDS]
     own = (me["y"], me["c"], me["z"], me["x"])
+    vectors = VectorSum(m, low_state, low_recv)
     for layer in range(LAYERS):
         for group, target in enumerate((wq, wu)):
             for source in range(8):
                 rows = slice(16 * group + 8 * layer, 16 * group + 8 * layer + 6)
                 asm[group, 6 * source : 6 * source + 6, :] = recv_a[source].astype(F32)[rows]
             target[(layer, *own)] = asm[group].astype(BF16)
+            if layer == 0:
+                gathers[group].first()
         for half in range(2):
             asm[2, 24 * half : 24 * half + 24, :] = recv_d[half].astype(F32)[
                 24 * layer : 24 * layer + 24
             ]
         wd[layer, me["c"], me["z"], me["x"], me["y"]] = asm[2].astype(BF16)
-        for gather in gathers[3 * layer : 3 * layer + 3]:
-            gather.first()
+        if layer == 0:
+            vectors.begin()
+            gathers[2].first()
+    gathers[0].second()
+    gathers[1].second()
     vectors.turn()
-    gathers[0].second()
-    vectors.turn()
-    gathers[1].second()
     gathers[0].third()
     gathers[2].second()
+    gathers[3].first()
     gathers[1].third()
-    for gather in gathers[3:]:
-        gather.second()
     vectors.turn()
+    gathers[4].first()
+    gathers[5].first()
     gathers[0].relay()
+    vectors.turn()
     gathers[2].third()
+    gathers[3].second()
     gathers[0].finish()
+    gathers[4].second()
+    vec[...] = vectors.end()
     gathers[1].relay()
     gathers[3].third()
-    vec[...] = vectors.end()
+    gathers[5].second()
     halves[0].wait_recv()
     halves[1].wait()
     gathers[0].arrive()
@@ -739,7 +736,7 @@
         return remote, copy
 
     results = [swap(outs, out, 2)]
-    upstream(order[me["c"]], remaining[me["c"]], cots, m)
+    upstream(order[pl.ds(me["c"], 1), :], remaining[me["c"]], cots, m)
     sums[...] = jnp.zeros(sums.shape, F32)
     scatters = {(kind, layer): Scatter(kind, layer, m) for layer in (1, 0) for kind in KINDS}
 
@@ -794,7 +791,7 @@
     scatters["q", 0].join(False)
     for kind in "udq":
         scatters[kind, 1].finish()
-    vectors = VectorSum(m)
+    vectors = VectorSum(m, vec_state, vec_recv)
     vectors.begin()
     scatters["u", 0].second()
     scatters["d", 0].second()
@@ -822,7 +819,7 @@
     recv_f[mine] = send_f[mine]
     recv_df[me["c"]] = send_df[me["c"]]
     sums[...] = vectors.end()
-    own_entries(index, sums, vec_out)
+    own_entries(index, sums, vectors_out)
     for copy in last:
         copy.wait_recv()
     for owner in range(8):
@@ -842,10 +839,51 @@
             g_down[layer, :, 384 * half : 384 * half + 384] = recv_df[
                 half, 24 * layer : 24 * layer + 24, :
             ]
+    stores = []
+    for number, (src, dst) in enumerate(zip(ready, outputs[2:])):
+        stores.append(pltpu.make_async_copy(src, dst, local_sems.at[4 + number]))
+        stores[-1].start()
     for remote, copy in results:
         remote.wait_recv()
         copy.wait()
     links.drain()
+    for copy in stores:
+        copy.wait()
+
+
+def deliver_kernel(*refs):
+    count = len(refs) // 3
+    sources, results, held, sems = refs[:count], refs[count : 2 * count], refs[2 * count : -1], refs[-1]
+    loads = [
+        pltpu.make_async_copy(src, dst, sems.at[0, number])
+        for number, (src, dst) in enumerate(zip(sources, held))
+    ]
+    stores = [
+        pltpu.make_async_copy(src, dst, sems.at[1, number])
+        for number, (src, dst) in enumerate(zip(held, results))
+    ]
+    for copy in loads:
+        copy.start()
+    for load, store in zip(loads, stores):
+        load.wait()
+        store.start()
+    for copy in stores:
+        copy.wait()
+
+
+def deliver(values):
+    hbm = pl.BlockSpec(memory_space=pl.ANY)
+    return pl.pallas_call(
+        deliver_kernel,
+        out_shape=[jax.ShapeDtypeStruct(value.shape, value.dtype) for value in values],
+        in_specs=[hbm] * len(values),
+        out_specs=[hbm] * len(values),
+        scratch_shapes=[
+            *[pltpu.VMEM(value.shape, value.dtype) for value in values],
+            pltpu.SemaphoreType.DMA((2, len(values))),
+        ],
+        name="deliver",
+    )(*values)
 
 
 def shards(
@@ -853,33 +891,39 @@
     norm1_gain, norm1_bias, w_qkv, bias_qv, w_out, bias_out,
     norm2_gain, norm2_bias, w_up, bias_up, w_down, bias_down,
 ):
-    vmem, hbm = pl.BlockSpec(memory_space=pltpu.VMEM), pl.BlockSpec(memory_space=pl.ANY)
     half = hidden.shape[1]
+    hbm = pl.BlockSpec(memory_space=pl.ANY)
     swapped = [jnp.transpose(weight, (1, 0, 2)) for weight in (w_qkv, w_out, w_up)]
     wide, deep = (LAYERS, 4, 2, 4, 4, 48, 384), (LAYERS, 2, 4, 4, 4, 48, 384)
-    sizes = [rows.stop - rows.start for kind in KINDS for rows, _ in STREAMS[kind]]
-    out, grad, g_qkv, g_out, g_up, g_down, vecs = pl.pallas_call(
+    inputs = (
+        hidden, cotangent, order, remaining, *swapped, w_down,
+        norm1_gain, norm1_bias, bias_qv, bias_out, norm2_gain, norm2_bias, bias_up, bias_down,
+    )
+    results = [((2, half, D), BF16)] + [
+        (shape, F32)
+        for shape in (
+            (2, half, D), (6, LAYERS, 3 * D), (6, LAYERS, D), (6, LAYERS, FF), (LAYERS, 24, D),
+            *[(LAYERS, 6)] * 6, (LAYERS, 12), (LAYERS, 24),
+        )
+    ]
+    staged = [pltpu.VMEM(value.shape, value.dtype) for value in inputs[2:]]
+    staged[1] = pltpu.SMEM(remaining.shape, remaining.dtype)
+    values = pl.pallas_call(
         kernel,
-        out_shape=(
-            jax.ShapeDtypeStruct((2, half, D), BF16),
-            jax.ShapeDtypeStruct((2, half, D), F32),
-            jax.ShapeDtypeStruct((6, LAYERS, 3 * D), F32),
-            jax.ShapeDtypeStruct((6, LAYERS, D), F32),
-            jax.ShapeDtypeStruct((6, LAYERS, FF), F32),
-            jax.ShapeDtypeStruct((LAYERS, 24, D), F32),
-            jax.ShapeDtypeStruct((LAYERS, 8, 128), F32),
-        ),
-        in_specs=[hbm, hbm] + [vmem] * 14,
-        out_specs=(hbm, hbm) + (vmem,) * 5,
+        out_shape=[jax.ShapeDtypeStruct(*result) for result in results],
+        in_specs=[hbm] * len(inputs),
+        out_specs=[hbm] * len(results),
         scratch_shapes=[
+            *staged,
+            *[pltpu.VMEM(*result) for result in results[2:]],
             pltpu.VMEM(wide, BF16),
             pltpu.VMEM(wide, BF16),
             pltpu.VMEM(deep, BF16),
             pltpu.VMEM((4, 4, 4, 48, 384), BF16),
             pltpu.VMEM((4, 4, 4, 48, 384), BF16),
-            *[pltpu.VMEM((3, 4, 4, size, 384), BF16) for size in sizes],
-            *[pltpu.VMEM((LAYERS, 3, 4, size, 384), BF16) for size in sizes],
-            *[pltpu.VMEM((LAYERS, 3, size, 384), BF16) for size in sizes],
+            pltpu.VMEM((3, 3, 3, 4, 4, 16, 384), BF16),
+            pltpu.VMEM((LAYERS, 3, 3, 3, 4, 16, 384), BF16),
+            pltpu.VMEM((LAYERS, 3, 3, 3, 16, 384), BF16),
             *[pltpu.VMEM((LAYERS, 48, 384), F32) for _ in range(3)],
             pltpu.VMEM((T, D), BF16),
             pltpu.VMEM((T, D), F32),
@@ -898,6 +942,8 @@
             pltpu.VMEM((T, D), BF16),
             pltpu.VMEM((LAYERS, 16, D), F32),
             pltpu.VMEM((LAYERS, 16, D), F32),
+            pltpu.VMEM((4, LAYERS, 16, D), BF16),
+            pltpu.VMEM((10, LAYERS, 16, D), BF16),
             pltpu.VMEM((4, LAYERS, 16, D), F32),
             pltpu.VMEM((10, LAYERS, 16, D), F32),
             pltpu.VMEM((3, LAYERS, 16, 128), F32),
@@ -905,32 +951,25 @@
             pltpu.VMEM((8, 32, 384), BF16),
             pltpu.VMEM((2, 48, 384), BF16),
             pltpu.VMEM((2, 48, 384), BF16),
-            pltpu.VMEM((8, 48, 384), F32),
+            pltpu.VMEM((3, 48, 384), F32),
             pltpu.VMEM((8, 32, 384), F32),
             pltpu.VMEM((8, 32, 384), F32),
             pltpu.VMEM((2, 48, 384), F32),
             pltpu.VMEM((2, 48, 384), F32),
-            pltpu.SemaphoreType.DMA((400,)),
-            pltpu.SemaphoreType.DMA((400,)),
-            pltpu.SemaphoreType.DMA((4,)),
-            pltpu.SemaphoreType.REGULAR((8,)),
+            pltpu.SemaphoreType.DMA((600,)),
+            pltpu.SemaphoreType.DMA((600,)),
+            pltpu.SemaphoreType.DMA((18,)),
+            pltpu.SemaphoreType.REGULAR((11,)),
         ],
         compiler_params=pltpu.CompilerParams(
             collective_id=0, has_side_effects=True, vmem_limit_bytes=(63 << 20) + (1 << 19)
         ),
         name="layers",
-    )(
-        hidden, cotangent, order[:, None, :],
-        jnp.broadcast_to(remaining[:, None, None], (2, 1, T)),
-        *swapped, w_down,
-        norm1_gain, norm1_bias, bias_qv, bias_out, norm2_gain, norm2_bias, bias_up, bias_down,
-    )
+    )(*inputs)
+    values = deliver(values)
+    out, grad, g_qkv, g_out, g_up, g_down, gain1, off1, b_out, gain2, off2, b_down, b_qv, b_up = values
     g_qkv, g_out, g_up = (jnp.transpose(part, (1, 0, 2)) for part in (g_qkv, g_out, g_up))
-    gain1, off1, out_bias, gain2, off2, down = (vecs[:, row, 0:6] for row in range(6))
-    return (
-        out, grad, gain1, off1, g_qkv, vecs[:, 6, 0:12], g_out, out_bias,
-        gain2, off2, g_up, vecs[:, 7, 0:24], g_down, down,
-    )
+    return out, grad, gain1, off1, g_qkv, b_qv, g_out, b_out, gain2, off2, g_up, b_up, g_down, b_down
 
 
 def solution(mesh):

time: 249 us -> 196 us (0.79)
  Pallas kernels: 236 us -> 195 us
  local copies, waits for them, and re-layouts: 11.7 us -> 0 us
    pallas_call x1 -> x2, Pallas kernels: 236 us -> 195 us  [the longest x1 193 us: shards(): pl.pallas_call(kernel, out_shape=[jax.ShapeDtypeStruct(*result) for resul...]
    unnamed x20 -> x0, local copies, waits for them, and re-layouts: 6.41 us -> none
    slice x3 -> x0, local copies, waits for them, and re-layouts: 4.1 us -> none  [the longest x1 1.5 us: shards(): vecs[:, row, 0:6]]
where the time goes in v3:
time: 196 us
  Pallas kernels  195 us (99%)
    pallas_call x1, Pallas kernels, shards(): pl.pallas_call(kernel, out_shape=[jax.ShapeDtypeStruct(*result) for resul...  193 us

profile of v3, /device:TPU:1, one launch (start us, length us, event | category | flops | bytes accessed | tf_op | source)
XLA Modules:
  0.0 196.1 jit_solution(768952033103806558)
XLA Ops:
  0.7 192.7 %layers.1 = (bf16[2,128,768]{2,1,0:T(8,128)(2,1)}, f32[2,128,768]{2,1,0:T(8,128)}, f32[6,2,2304]{2,1,0:T(2,128)}, f32[6,2,768]{2,1,0:T(2,128)}, f32[6,2,3072]{2,...) custom-call(bf16[2,128,768]{2,1,0:T(8,128)(2,1)} %refs_0_.1, ...), custom_call_target="tpu_custom_call" | custom-call | tf_op jit(solution)/shard_map/layers/pallas_call | solution.py:911
  193.4 2.5 %deliver.1 = (bf16[2,128,768]{2,1,0:T(8,128)(2,1)}, f32[2,128,768]{2,1,0:T(8,128)}, f32[6,2,2304]{2,1,0:T(2,128)}, f32[6,2,768]{2,1,0:T(2,128)}, f32[6,2,3072]{2...) custom-call(bf16[2,128,768]{2,1,0:T(8,128)(2,1)} %get-tuple-element., ...), custom_call_target="tpu_custom_call" | custom-call | tf_op jit(solution)/shard_map/deliver/pallas_call | solution.py:876

commit v4 on v3

--- a/solution.py
+++ b/solution.py
@@ -36,33 +36,46 @@
     return {**at, axis: (at[axis] + step) % size}
 
 
-class Links:
-    def __init__(self, send_sems, recv_sems):
-        self.send_sems, self.recv_sems, self.used, self.open = send_sems, recv_sems, 0, []
-
-    def copy(self, src, dst, target, number):
+class Batch:
+    def __init__(self, links, whole):
+        self.links, self.whole = links, whole
+        self.number = links.batches
+        links.batches += 1
+        links.open.append(self)
+
+    def copy(self, src, dst, target):
         return pltpu.make_async_remote_copy(
             src_ref=src,
             dst_ref=dst,
-            send_sem=self.send_sems.at[number],
-            recv_sem=self.recv_sems.at[number],
+            send_sem=self.links.send_sems.at[self.number],
+            recv_sem=self.links.recv_sems.at[self.number],
             device_id=device(target),
             device_id_type=MESH,
         )
 
-    def take(self, count):
-        self.used += count
-        return self.used - count
-
     def send(self, src, dst, target):
-        copy = self.copy(src, dst, target, self.take(1))
-        copy.start()
-        self.open.append(copy)
-        return copy
+        self.copy(src, dst, target).start()
+
+    def all(self):
+        return self.copy(self.whole, self.whole, self.links.sibling)
+
+    def wait(self):
+        self.all().wait_recv()
+
+
+class Links:
+    def __init__(self, me, send_sems, recv_sems):
+        self.sibling = moved(me, "c", 1)
+        self.send_sems, self.recv_sems, self.open, self.batches = send_sems, recv_sems, [], 0
+
+    def send(self, src, dst, target):
+        batch = Batch(self, src)
+        batch.send(src, dst, target)
+        return batch
 
     def drain(self):
-        for copy in self.open:
-            copy.wait_send()
+        for batch in self.open:
+            batch.all().wait_send()
         self.open = []
 
 
@@ -315,7 +328,13 @@
 
 class Gather:
     def __init__(self, kind, layer, m):
-        self.kind, self.layer, self.m, self.handed = kind, layer, m, []
+        self.kind, self.layer, self.m = kind, layer, m
+        sizes = m.wq.at[0]
+        self.handed = Batch(m.links, sizes.at[:, 0])
+        self.one = Batch(m.links, sizes.at[0, 0, 0, pl.ds(0, 3)])
+        self.two = Batch(m.links, sizes.at[0, 0, pl.ds(0, 3)])
+        self.three = Batch(m.links, sizes.at[pl.ds(0, 2), 0])
+        self.halves = Batch(m.links, sizes.at[0, 0])
 
     def part(self, rows, at):
         index = tuple(at[axis] for axis in AXES[self.kind])
@@ -323,110 +342,128 @@
 
     def hand_over(self, rows, at):
         part = self.part(rows, at)
-        self.handed.append(self.m.links.send(part, part, moved(self.m.me, "c", 1)))
-
-    def out(self, rows, at, axis, steps):
-        part, me = self.part(rows, at), self.m.me
-        return {step: self.m.links.send(part, part, moved(me, axis, step)) for step in steps}
+        self.handed.send(part, part, self.m.links.sibling)
+
+    def out(self, batch, rows, at, axis, steps):
+        part = self.part(rows, at)
+        for step in steps:
+            batch.send(part, part, moved(self.m.me, axis, step))
 
     def first(self):
-        me = self.m.me
-        self.copies = [self.out(rows, me, axes[0], STEPS) for rows, axes in STREAMS]
+        for rows, axes in STREAMS:
+            self.out(self.one, rows, self.m.me, axes[0], STEPS)
 
     def second(self):
-        me, before = self.m.me, self.copies
-        self.copies = []
-        for (rows, axes), copies in zip(STREAMS, before):
-            for step in STEPS:
-                copies[step].wait_recv()
-            self.copies.append(self.out(rows, {**me, axes[0]: ALL}, axes[1], STEPS))
+        self.one.wait()
+        for rows, axes in STREAMS:
+            self.out(self.two, rows, {**self.m.me, axes[0]: ALL}, axes[1], STEPS)
 
     def third(self):
-        me, before = self.m.me, self.copies
-        self.copies = []
-        for (rows, axes), copies in zip(STREAMS, before):
-            for step in STEPS:
-                copies[step].wait_recv()
-            plane = {**me, axes[0]: ALL, axes[1]: ALL}
-            self.copies.append(self.out(rows, plane, axes[2], (1, 3)))
+        self.two.wait()
+        planes = [
+            (rows, axes, {**self.m.me, axes[0]: ALL, axes[1]: ALL}) for rows, axes in STREAMS
+        ]
+        for rows, axes, plane in planes:
+            self.out(self.three, rows, plane, axes[2], (1, 3))
+        for rows, axes, plane in planes:
             self.hand_over(rows, plane)
 
     def relay(self):
-        me, self.halves = self.m.me, []
-        for (rows, axes), copies in zip(STREAMS, self.copies):
-            for step, start in ((1, 0), (3, 2)):
-                copies[step].wait_recv()
-                came = {**moved(me, axes[2], -step), axes[1]: ALL}
-                half = self.part(rows, {**came, axes[0]: pl.ds(start, 2)})
-                self.halves.append(self.m.links.send(half, half, moved(me, axes[2], step)))
-                self.hand_over(rows, {**came, axes[0]: ALL})
+        self.three.wait()
+        came = [
+            (rows, axes, step, {**moved(self.m.me, axes[2], -step), axes[0]: ALL, axes[1]: ALL})
+            for rows, axes in STREAMS
+            for step in (1, 3)
+        ]
+        for rows, axes, step, at in came:
+            self.out(self.halves, rows, {**at, axes[0]: pl.ds(step - 1, 2)}, axes[2], (step,))
+        for rows, axes, step, at in came:
+            self.hand_over(rows, at)
 
     def finish(self):
-        for copy in self.halves:
-            copy.wait_recv()
+        self.halves.wait()
         for rows, axes in STREAMS:
             self.hand_over(rows, {**moved(self.m.me, axes[2], 2), axes[0]: ALL, axes[1]: ALL})
 
     def arrive(self):
-        for copy in self.handed:
-            copy.wait_recv()
+        self.handed.wait()
 
 
 class Scatter:
     def __init__(self, kind, layer, m):
         self.kind, self.layer, self.m = kind, layer, m
+        self.slow = "z" if kind == "d" else "y"
         number = KINDS.index(kind)
-        self.streams = [
-            (
-                rows,
-                axes[::-1],
-                m.first.at[number, stream],
-                m.second.at[layer, number, stream],
-                m.third.at[layer, number, stream],
-                m.free.at[3 * number + stream],
-            )
-            for stream, (rows, axes) in enumerate(STREAMS)
-        ]
-        self.base = m.links.take(4)
+        self.streams = []
+        for stream, (rows, axes) in enumerate(STREAMS):
+            others = [axis for axis in AXES[kind] if axis not in ("c", axes[2])]
+            slots = m.first.at[number, stream]
+            later = (m.second.at[layer, number, stream], m.third.at[layer, number, stream])
+            free = m.free.at[3 * number + stream]
+            self.streams.append((rows, axes[::-1], others, slots, *later, free))
+        sizes = m.wq.at[0]
+        self.shared = [Batch(m.links, sizes.at[pl.ds(0, 2), 0]) for _ in range(2)]
+        self.passing, self.direct, self.passed = (Batch(m.links, sizes.at[0, 0]) for _ in range(3))
+        self.two = Batch(m.links, sizes.at[0, 0, pl.ds(0, 3)])
+        self.one = Batch(m.links, sizes.at[0, 0, 0, pl.ds(0, 3)])
         self.room, self.got = (m.free.at[9], m.got_d) if kind == "d" else (m.free.at[10], m.got_qu)
 
     def part(self, rows, at):
         index = tuple(at.get(axis, ALL) for axis in AXES[self.kind])
         return self.m.weights[self.kind].at[(self.layer, *index, rows, ALL)]
 
-    def between(self, index):
-        axis, sibling = ("z" if self.kind == "d" else "y"), moved(self.m.me, "c", 1)
-        src = self.part(ALL, {axis: index, "c": sibling["c"]})
-        return self.m.links.copy(src, self.got.at[index], sibling, self.base + index)
+    def share(self, index, half):
+        sibling = self.m.links.sibling
+        src = self.part(ALL, {self.slow: index, "c": sibling["c"]})
+        self.shared[half].send(src, self.got.at[index], sibling)
 
     def wait_room(self):
         pl.semaphore_wait(self.room, 1)
 
-    def join(self, more):
+    def give_room(self):
+        sibling = device(self.m.links.sibling)
+        pl.semaphore_signal(self.room, inc=1, device_id=sibling, device_id_type=MESH)
+
+    def join(self, half):
         m, me = self.m, self.m.me
-        axis, other = ("z", "x") if self.kind == "d" else ("y", "z")
-        for index in range(4):
-            copy = self.between(index)
-            copy.wait_recv()
-            m.links.open.append(copy)
-
-        @pl.loop(0, 16)
+        other = "x" if self.kind == "d" else "z"
+        self.shared[half].wait()
+
+        @pl.loop(8 * half, 8 * half + 8)
         def _(spot):
-            own = self.part(ALL, {axis: spot // 4, other: spot % 4, "c": me["c"]})
+            own = self.part(ALL, {self.slow: spot // 4, other: spot % 4, "c": me["c"]})
             own[...] += self.got[spot // 4, spot % 4]
 
-        if more:
-            pl.semaphore_signal(
-                self.room, inc=1, device_id=device(moved(me, "c", 1)), device_id_type=MESH
-            )
-        self.copies = []
-        for rows, axes, slots, _, _, free in self.streams:
-            if self.layer == 0:
-                pl.semaphore_wait(free, 3)
-            for step in STEPS:
-                target = moved(me, axes[0], step)
-                src = self.part(rows, {"c": me["c"], axes[0]: target[axes[0]]})
-                self.copies.append(m.links.send(src, slots.at[step - 1], target))
+        for rows, axes, others, slots, _, _, free in self.streams:
+            split = others[0] == self.slow
+            if self.layer == 0 and half == (0 if split else 1):
+                pl.semaphore_wait(free, 2)
+            for now in (half,) if split else (0, 1) if half else ():
+                self.leave(rows, axes[0], others[0], slots, now)
+
+    def leave(self, rows, axis, split, slots, half):
+        me, step, back = self.m.me, 1 + 2 * half, 3 - 2 * half
+        halves = pl.ds(2 * half, 2)
+        spot = {"c": me["c"], split: halves}
+        src = self.part(rows, {**spot, axis: moved(me, axis, 2)[axis]})
+        self.passing.send(src, slots.at[2, halves], moved(me, axis, step))
+        target = moved(me, axis, back)
+        src = self.part(rows, {**spot, axis: target[axis]})
+        self.direct.send(src, slots.at[1 - half, halves], target)
+
+    def relay(self):
+        me = self.m.me
+        self.passing.wait()
+        for rows, axes, others, slots, _, _, _ in self.streams:
+            for half in range(2):
+                target = moved(me, axes[0], 1 + 2 * half)
+                spot = {"c": me["c"], axes[0]: target[axes[0]]}
+                for index in (2 * half, 2 * half + 1):
+                    own = self.part(rows, {**spot, others[0]: index})
+                    own[...] += slots[2, index]
+                halves = pl.ds(2 * half, 2)
+                src = self.part(rows, {**spot, others[0]: halves})
+                self.passed.send(src, slots.at[half, halves], target)
 
     def add(self, target, slots):
         value = target[...].astype(F32)
@@ -435,47 +472,42 @@
         return value
 
     def second(self):
-        m, me, before = self.m, self.m.me, self.copies
-        self.copies = []
-        for number, (rows, axes, slots, later, _, free) in enumerate(self.streams):
-            for copy in before[3 * number : 3 * number + 3]:
-                copy.wait_recv()
+        m, me = self.m, self.m.me
+        self.direct.wait()
+        self.passed.wait()
+        for rows, axes, others, slots, later, _, free in self.streams:
             here = {"c": me["c"], axes[0]: me[axes[0]]}
-            other = [axis for axis in AXES[self.kind] if axis not in here][0]
 
             @pl.loop(0, 4)
             def _(index):
-                target = self.part(rows, {**here, other: index})
-                total = self.add(target, [slots.at[step, index] for step in range(3)])
+                target = self.part(rows, {**here, others[0]: index})
+                total = self.add(target, [slots.at[side, index] for side in range(2)])
                 target[...] = total.astype(BF16)
 
             if self.layer == 1:
-                for step in STEPS:
+                for step in (1, 3):
                     peer = device(moved(me, axes[0], step))
                     pl.semaphore_signal(free, inc=1, device_id=peer, device_id_type=MESH)
             for step in STEPS:
                 target = moved(me, axes[1], step)
                 src = self.part(rows, {**here, axes[1]: target[axes[1]]})
-                self.copies.append(m.links.send(src, later.at[step - 1], target))
+                self.two.send(src, later.at[step - 1], target)
 
     def third(self):
-        m, me, before = self.m, self.m.me, self.copies
-        self.copies = []
-        for number, (rows, axes, _, later, last, _) in enumerate(self.streams):
-            for copy in before[3 * number : 3 * number + 3]:
-                copy.wait_recv()
+        m, me = self.m, self.m.me
+        self.two.wait()
+        for rows, axes, _, _, later, last, _ in self.streams:
             here = {"c": me["c"], axes[0]: me[axes[0]], axes[1]: me[axes[1]]}
             target = self.part(rows, here)
             target[...] = self.add(target, [later.at[step] for step in range(3)]).astype(BF16)
             for step in STEPS:
                 target = moved(me, axes[2], step)
                 src = self.part(rows, {**here, axes[2]: target[axes[2]]})
-                self.copies.append(m.links.send(src, last.at[step - 1], target))
+                self.one.send(src, last.at[step - 1], target)
 
     def finish(self):
-        for copy in self.copies:
-            copy.wait_recv()
-        for rows, _, _, _, last, _ in self.streams:
+        self.one.wait()
+        for rows, _, _, _, _, last, _ in self.streams:
             total = self.add(self.part(rows, self.m.me), [last.at[step] for step in range(3)])
             self.m.totals[self.kind][self.layer, rows, :] = total
 
@@ -546,28 +578,23 @@
 
     def begin(self):
         m, axis = self.m, self.ORDER[self.number]
-        self.copies = [
-            m.links.send(
-                self.state.at[self.number],
-                self.recv.at[3 * self.number + step - 1],
-                moved(m.me, axis, step),
-            )
-            for step in range(1, 2 if axis == "c" else 4)
-        ]
-
-    def end(self):
-        total = self.state[self.number].astype(F32)
-        for copy in self.copies:
-            copy.wait_recv()
-        for step in range(len(self.copies)):
-            total += self.recv[3 * self.number + step].astype(F32)
+        self.steps = range(1, 2 if axis == "c" else 4)
+        self.batch = Batch(m.links, self.recv.at[pl.ds(0, len(self.steps))])
+        for step in self.steps:
+            slot = self.recv.at[3 * self.number + step - 1]
+            self.batch.send(self.state.at[self.number], slot, moved(m.me, axis, step))
+
+    def end(self, total):
+        self.batch.wait()
+        for step in self.steps:
+            total += self.recv[3 * self.number + step - 1].astype(F32)
         self.number += 1
         if self.number < 4:
             self.state[self.number] = total.astype(self.state.dtype)
         return total
 
     def turn(self):
-        self.end()
+        self.end(self.state[self.number].astype(F32))
         self.begin()
 
 
@@ -579,7 +606,7 @@
     (
         wq, wu, wd, got_qu, got_d, first, second, third, sum_q, sum_u, sum_d,
         x0, x1, h, qkv, probs, o, mid, h2, u, tmp, g, gh, gz, cots, outs, vec, sums,
-        low_state, low_recv, vec_state, vec_recv, stage,
+        low_state, low_recv, stage,
         send_a, recv_a, send_d, recv_d, asm, send_f, recv_f, send_df, recv_df,
         send_sems, recv_sems, local_sems, free,
     ) = refs
@@ -596,7 +623,7 @@
     sibling = moved(me, "c", 1)
     mine = 2 * me["y"] + me["c"]
     index = ((me["z"] * 4 + me["x"]) * 4 + me["y"]) * 2 + me["c"]
-    links = Links(send_sems, recv_sems)
+    links = Links(me, send_sems, recv_sems)
     m = types.SimpleNamespace(
         me=me, links=links, weights={"q": wq, "u": wu, "d": wd}, wq=wq, wu=wu, wd=wd,
         got_qu=got_qu, got_d=got_d, free=free, totals={"q": sum_q, "u": sum_u, "d": sum_d},
@@ -631,17 +658,17 @@
 
     greet(me)
 
-    def group_sends(src, dst):
-        copies = []
+    def group_sends(src, dst, rows=ALL):
+        batch = Batch(links, dst.at[pl.ds(0, 7), rows])
         for dy in range(4):
             for dc in range(2):
                 if dy or dc:
                     target = moved(moved(me, "y", dy), "c", dc)
-                    spot = src.at[2 * target["y"] + target["c"]]
-                    copies.append(links.send(spot, dst.at[mine], target))
-        return copies
-
-    arrivals = group_sends(send_a, recv_a)
+                    spot = src.at[2 * target["y"] + target["c"], rows]
+                    batch.send(spot, dst.at[mine, rows], target)
+        return batch
+
+    arrivals = [group_sends(send_a, recv_a)]
     arrivals.append(links.send(send_d.at[1 - me["c"]], recv_d.at[me["c"]], sibling))
     recv_a[mine] = send_a[mine]
     recv_d[me["c"]] = send_d[me["c"]]
@@ -653,8 +680,8 @@
         copy = pltpu.make_async_copy(src.at[me["c"]], dst.at[here, :], local_sems.at[number])
         copy.start()
         halves.append(copy)
-    for copy in arrivals:
-        copy.wait_recv()
+    for batch in arrivals:
+        batch.wait()
     gathers = [Gather(kind, layer, m) for layer in range(LAYERS) for kind in KINDS]
     own = (me["y"], me["c"], me["z"], me["x"])
     vectors = VectorSum(m, low_state, low_recv)
@@ -690,11 +717,11 @@
     gathers[3].second()
     gathers[0].finish()
     gathers[4].second()
-    vec[...] = vectors.end()
+    vec[...] = vectors.end(low_state[3].astype(F32))
     gathers[1].relay()
     gathers[3].third()
     gathers[5].second()
-    halves[0].wait_recv()
+    halves[0].wait()
     halves[1].wait()
     gathers[0].arrive()
 
@@ -726,7 +753,7 @@
     forward_down(1, m)
     outs[...] = g[...].astype(BF16)
     links.drain()
-    halves[2].wait_recv()
+    halves[2].wait()
     halves[3].wait()
 
     def swap(src, dst, number):
@@ -741,87 +768,123 @@
     scatters = {(kind, layer): Scatter(kind, layer, m) for layer in (1, 0) for kind in KINDS}
 
     def ffn(layer):
-        ups, downs = scatters["u", layer], scatters["d", layer]
+        groups = [scatters[kind, layer] for kind in "ud"]
         if layer == 0:
-            ups.wait_room()
-            downs.wait_room()
-
-        @pl.loop(0, 4)
-        def _(part):
-            backward_ffn(layer, m, part)
-            ups.between(part).start()
-            downs.between(part).start()
+            for group in groups:
+                group.wait_room()
+
+        @pl.loop(0, 2)
+        def _(half):
+            @pl.loop(0, 2)
+            def _(part):
+                backward_ffn(layer, m, 2 * half + part)
+
+                @pl.when(half == 0)
+                def _():
+                    for group in groups:
+                        group.share(part, 0)
+
+                @pl.when(half == 1)
+                def _():
+                    for group in groups:
+                        group.share(2 + part, 1)
+
+                    if layer == 1:
+
+                        @pl.when(part == 0)
+                        def _():
+                            for group in groups:
+                                group.join(0)
 
     def attention_grads(layer):
         scatter = scatters["q", layer]
         scatter.wait_room()
-        scatter.between(3).start()
+        scatter.share(3, 1)
         m.gh[...] = jnp.zeros((T, D), F32)
 
         @pl.loop(0, 3)
         def _(part):
             backward_qkv(layer, m, part)
-            scatter.between(part).start()
+
+            @pl.when(part < 2)
+            def _():
+                scatter.share(part, 0)
+
+            @pl.when(part == 2)
+            def _():
+                scatter.share(2, 1)
+
+    def steps(step, kinds, layer, *given):
+        for kind in kinds:
+            getattr(scatters[kind, layer], step)(*given)
 
     top(1, m)
     ffn(1)
     backward_mid(1, m)
-    scatters["u", 1].join(True)
-    scatters["d", 1].join(True)
+    steps("join", "ud", 1, 1)
+    steps("give_room", "ud", 1)
     backward_attention(1, m)
+    steps("relay", "ud", 1)
     attention_grads(1)
     backward_in(1, m, g)
     top(0, m)
-    scatters["q", 1].join(True)
+    steps("join", "q", 1, 0)
+    steps("join", "q", 1, 1)
+    steps("give_room", "q", 1)
     ffn(0)
-    scatters["u", 1].second()
-    scatters["d", 1].second()
+    steps("second", "ud", 1)
+    steps("relay", "q", 1)
+    for half in range(2):
+        steps("join", "ud", 0, half)
+    steps("give_room", "u", 0)
     backward_mid(0, m)
-    scatters["q", 1].second()
-    scatters["u", 0].join(True)
-    scatters["d", 0].join(False)
+    steps("third", "ud", 1)
+    steps("second", "q", 1)
     backward_attention(0, m)
-    scatters["u", 1].third()
-    scatters["d", 1].third()
+    steps("relay", "ud", 0)
     attention_grads(0)
-    scatters["q", 1].third()
+    steps("third", "q", 1)
     backward_in(0, m, g)
     results.append(swap(g, grad, 3))
-    vec_state[0] = sums[...]
-    scatters["q", 0].join(False)
-    for kind in "udq":
-        scatters[kind, 1].finish()
-    vectors = VectorSum(m, vec_state, vec_recv)
+    low_state[0] = sums[...].astype(BF16)
+    for half in range(2):
+        steps("join", "q", 0, half)
+    vectors = VectorSum(m, low_state, low_recv)
     vectors.begin()
-    scatters["u", 0].second()
-    scatters["d", 0].second()
+    steps("second", "ud", 0)
+    steps("finish", "udq", 1)
+    steps("relay", "q", 0)
     vectors.turn()
-    scatters["q", 0].second()
-    scatters["u", 0].third()
-    scatters["d", 0].third()
+    steps("third", "ud", 0)
+    steps("second", "q", 0)
     vectors.turn()
-    scatters["q", 0].third()
-    vectors.turn()
-    for kind in "udq":
-        scatters[kind, 0].finish()
-
+    steps("finish", "ud", 0)
+
+    def owned(total, layer, start):
+        for owner in range(8):
+            send_f[owner, start : start + 6, :] = total[layer, 6 * owner : 6 * owner + 6, :]
+
+    owned(sum_q, 1, 8)
+    owned(sum_u, 0, 16)
+    owned(sum_u, 1, 24)
     for layer in range(LAYERS):
-        for owner in range(8):
-            for group, total in enumerate((sum_q, sum_u)):
-                start = 16 * group + 8 * layer
-                send_f[owner, start : start + 6, :] = total[layer, 6 * owner : 6 * owner + 6, :]
         for owner in range(2):
             send_df[owner, 24 * layer : 24 * layer + 24, :] = sum_d[
                 layer, 24 * owner : 24 * owner + 24, :
             ]
-    last = group_sends(send_f, recv_f)
+    last = [group_sends(send_f, recv_f, slice(8, 32))]
     last.append(links.send(send_df.at[1 - me["c"]], recv_df.at[me["c"]], sibling))
+    recv_df[me["c"]] = send_df[me["c"]]
+    steps("third", "q", 0)
+    vectors.turn()
+    steps("finish", "q", 0)
+    owned(sum_q, 0, 0)
+    last.append(group_sends(send_f, recv_f, slice(0, 8)))
     recv_f[mine] = send_f[mine]
-    recv_df[me["c"]] = send_df[me["c"]]
-    sums[...] = vectors.end()
+    sums[...] = vectors.end(low_state[3].astype(F32))
     own_entries(index, sums, vectors_out)
-    for copy in last:
-        copy.wait_recv()
+    for batch in last:
+        batch.wait()
     for owner in range(8):
         columns = slice(384 * (owner % 2), 384 * (owner % 2) + 384)
         for layer in range(LAYERS):
@@ -844,7 +907,7 @@
         stores.append(pltpu.make_async_copy(src, dst, local_sems.at[4 + number]))
         stores[-1].start()
     for remote, copy in results:
-        remote.wait_recv()
+        remote.wait()
         copy.wait()
     links.drain()
     for copy in stores:
@@ -944,8 +1007,6 @@
             pltpu.VMEM((LAYERS, 16, D), F32),
             pltpu.VMEM((4, LAYERS, 16, D), BF16),
             pltpu.VMEM((10, LAYERS, 16, D), BF16),
-            pltpu.VMEM((4, LAYERS, 16, D), F32),
-            pltpu.VMEM((10, LAYERS, 16, D), F32),
             pltpu.VMEM((3, LAYERS, 16, 128), F32),
             pltpu.VMEM((8, 32, 384), BF16),
             pltpu.VMEM((8, 32, 384), BF16),
@@ -956,8 +1017,8 @@
             pltpu.VMEM((8, 32, 384), F32),
             pltpu.VMEM((2, 48, 384), F32),
             pltpu.VMEM((2, 48, 384), F32),
-            pltpu.SemaphoreType.DMA((600,)),
-            pltpu.SemaphoreType.DMA((600,)),
+            pltpu.SemaphoreType.DMA((89,)),
+            pltpu.SemaphoreType.DMA((89,)),
             pltpu.SemaphoreType.DMA((18,)),
             pltpu.SemaphoreType.REGULAR((11,)),
         ],

time: 196 us -> 178 us (0.908)
  Pallas kernels: 195 us -> 177 us
    pallas_call x1, Pallas kernels: 193 us -> 174 us  [shards(): pl.pallas_call(kernel, out_shape=[jax.ShapeDtypeStruct(*result) for resul...]
where the time goes in v4:
time: 178 us
  Pallas kernels  177 us (99%)
    pallas_call x1, Pallas kernels, shards(): pl.pallas_call(kernel, out_shape=[jax.ShapeDtypeStruct(*result) for resul...  174 us

profile of v4, /device:TPU:1, one launch (start us, length us, event | category | flops | bytes accessed | tf_op | source)
XLA Modules:
  0.0 177.5 jit_solution(108210397508583901)
XLA Ops:
  0.7 174.2 %layers.1 = (bf16[2,128,768]{2,1,0:T(8,128)(2,1)}, f32[2,128,768]{2,1,0:T(8,128)}, f32[6,2,2304]{2,1,0:T(2,128)}, f32[6,2,768]{2,1,0:T(2,128)}, f32[6,2,3072]{2,...) custom-call(bf16[2,128,768]{2,1,0:T(8,128)(2,1)} %refs_0_.1, ...), custom_call_target="tpu_custom_call" | custom-call | tf_op jit(solution)/shard_map/layers/pallas_call | solution.py:974
  174.8 2.5 %deliver.1 = (bf16[2,128,768]{2,1,0:T(8,128)(2,1)}, f32[2,128,768]{2,1,0:T(8,128)}, f32[6,2,2304]{2,1,0:T(2,128)}, f32[6,2,768]{2,1,0:T(2,128)}, f32[6,2,3072]{2...) custom-call(bf16[2,128,768]{2,1,0:T(8,128)(2,1)} %get-tuple-element., ...), custom_call_target="tpu_custom_call" | custom-call | tf_op jit(solution)/shard_map/deliver/pallas_call | solution.py:939

commit v5 on v4

--- a/solution.py
+++ b/solution.py
@@ -434,21 +434,27 @@
             own = self.part(ALL, {self.slow: spot // 4, other: spot % 4, "c": me["c"]})
             own[...] += self.got[spot // 4, spot % 4]
 
+        ready = []
         for rows, axes, others, slots, _, _, free in self.streams:
             split = others[0] == self.slow
             if self.layer == 0 and half == (0 if split else 1):
                 pl.semaphore_wait(free, 2)
             for now in (half,) if split else (0, 1) if half else ():
-                self.leave(rows, axes[0], others[0], slots, now)
+                ready.append((rows, axes[0], others[0], slots, now))
+        for now in ready:
+            self.pass_on(*now)
+        for now in ready:
+            self.leave(*now)
+
+    def pass_on(self, rows, axis, split, slots, half):
+        me, halves = self.m.me, pl.ds(2 * half, 2)
+        src = self.part(rows, {"c": me["c"], split: halves, axis: moved(me, axis, 2)[axis]})
+        self.passing.send(src, slots.at[2, halves], moved(me, axis, 1 + 2 * half))
 
     def leave(self, rows, axis, split, slots, half):
-        me, step, back = self.m.me, 1 + 2 * half, 3 - 2 * half
-        halves = pl.ds(2 * half, 2)
-        spot = {"c": me["c"], split: halves}
-        src = self.part(rows, {**spot, axis: moved(me, axis, 2)[axis]})
-        self.passing.send(src, slots.at[2, halves], moved(me, axis, step))
-        target = moved(me, axis, back)
-        src = self.part(rows, {**spot, axis: target[axis]})
+        me, halves = self.m.me, pl.ds(2 * half, 2)
+        target = moved(me, axis, 3 - 2 * half)
+        src = self.part(rows, {"c": me["c"], split: halves, axis: target[axis]})
         self.direct.send(src, slots.at[1 - half, halves], target)
 
     def relay(self):
@@ -512,90 +518,108 @@
             self.m.totals[self.kind][self.layer, rows, :] = total
 
 
+TILE_PAIRS = ((GAIN1, OFF1), (BIAS_OUT, GAIN2), (OFF2, BIAS_DOWN))
+NARROW_ROWS = tuple(row for pair in TILE_PAIRS for row in pair)
+
+
 def spot_matrix(base, width):
-    row = lax.broadcasted_iota(jnp.int32, (128, D), 0)
-    lane = lax.broadcasted_iota(jnp.int32, (128, D), 1)
+    row = lax.broadcasted_iota(jnp.int32, (128, 128), 0)
+    lane = lax.broadcasted_iota(jnp.int32, (128, 128), 1)
     return jnp.where((lane == base + row) & (row < width), 1.0, 0.0).astype(BF16)
+
+
+def spot_matrices(member):
+    return (
+        spot_matrix(6 * member, 6), spot_matrix(48 + 6 * member, 6),
+        spot_matrix(12 * member, 12), spot_matrix(24 * (member % 4), 24),
+    )
 
 
 def flag(condition):
     return jnp.where(condition, 1.0, 0.0).astype(F32)
 
 
-NARROW_ROWS = (GAIN1, OFF1, BIAS_OUT, GAIN2, OFF2, BIAS_DOWN)
-
-
-def spread_vectors(index, narrow, wide_qv, wide_up, stage, out):
+def vector_tile(member, narrow, wide_qv, wide_up, stage):
     stage[...] = jnp.zeros(stage.shape, F32)
     for layer in range(LAYERS):
         rows = slice(layer, layer + 1)
-        for row, vector in zip(NARROW_ROWS, narrow):
-            stage[0, layer, row : row + 1, 0:6] = vector[rows, :].astype(F32)
-        pair = wide_qv[rows, :].astype(F32)
-        stage[1, layer, BIAS_Q : BIAS_Q + 1, 0:12] = pair * flag(index < 64)
-        stage[1, layer, BIAS_Q + 2 : BIAS_Q + 3, 0:12] = pair * flag(index >= 64)
-        for row in range(4):
-            up = wide_up[rows, :].astype(F32) * flag(index // 32 == row)
-            stage[2, layer, BIAS_UP + row : BIAS_UP + row + 1, 0:24] = up
+        for number, vector in enumerate(narrow):
+            row = 8 * layer + number // 2
+            stage[number % 2, row : row + 1, 0:6] = vector[rows, :].astype(F32)
+        row = 8 * layer + 3
+        stage[2, row : row + 1, 0:12] = wide_qv[rows, :].astype(F32)
+        for half in range(2):
+            up = wide_up[rows, :].astype(F32) * flag(member // 4 == half)
+            stage[3, row + 1 + half : row + 2 + half, 0:24] = up
+    total = jnp.zeros((16, 128), F32)
+    for number, matrix in enumerate(spot_matrices(member)):
+        total += dot(stage[number].astype(BF16), matrix)
+    return total.astype(BF16)
+
+
+def whole_vectors(tiles, vec):
+    tiles = [tiles[index // 4, index % 4].astype(F32) for index in range(16)]
+
+    def joined(row, first, last, groups):
+        return jnp.concatenate([tiles[group][row : row + 1, first:last] for group in groups], axis=1)
+
     for layer in range(LAYERS):
-        total = jnp.zeros((16, D), F32)
-        for number, matrix in enumerate(spot_matrices(index)):
-            total += dot(stage[number, layer].astype(BF16), matrix)
-        out[layer] = total.astype(BF16)
-
-
-def spot_matrices(index):
-    return (
-        spot_matrix(6 * index, 6), spot_matrix(12 * (index % 64), 12), spot_matrix(24 * (index % 32), 24)
-    )
-
-
-def own_entries(index, total, out):
+        vec[layer] = jnp.zeros((16, D), F32)
+        for number, pair in enumerate(TILE_PAIRS):
+            for side, row in enumerate(pair):
+                value = joined(8 * layer + number, 48 * side, 48 * side + 48, range(16))
+                vec[layer, row : row + 1, :] = value
+        for side in range(2):
+            value = joined(8 * layer + 3, 0, 96, range(8 * side, 8 * side + 8))
+            vec[layer, BIAS_Q + 2 * side : BIAS_Q + 2 * side + 1, :] = value
+        for part in range(4):
+            pieces = []
+            for group in range(4 * part, 4 * part + 4):
+                for half in range(2):
+                    row = 8 * layer + 4 + half
+                    pieces.append(tiles[group][row : row + 1, 0:96])
+            value = jnp.concatenate(pieces, axis=1)
+            vec[layer, BIAS_UP + part : BIAS_UP + part + 1, :] = value
+
+
+def vector_tiles(sums, tiles):
+    tiles[...] = jnp.zeros(tiles.shape, F32)
     for layer in range(LAYERS):
-        value = total[layer]
-        high = value.astype(BF16)
-        middle = (value - high.astype(F32)).astype(BF16)
-        low = (value - high.astype(F32) - middle.astype(F32)).astype(BF16)
-        found = []
-        for matrix in spot_matrices(index):
-            found.append(dot_nt(high, matrix) + (dot_nt(middle, matrix) + dot_nt(low, matrix)))
-        for place_out, row in enumerate(NARROW_ROWS):
-            out[place_out][layer : layer + 1, :] = found[0][row : row + 1, 0:6]
-        pair = found[1][BIAS_Q : BIAS_Q + 1] * flag(index < 64)
-        pair += found[1][BIAS_Q + 2 : BIAS_Q + 3] * flag(index >= 64)
-        out[6][layer : layer + 1, :] = pair[:, 0:12]
-        up = jnp.zeros((1, 128), F32)
-        for row in range(4):
-            up += found[2][BIAS_UP + row : BIAS_UP + row + 1] * flag(index // 32 == row)
-        out[7][layer : layer + 1, :] = up[:, 0:24]
-
-
-class VectorSum:
-    ORDER = "xyzc"
-
-    def __init__(self, m, state, recv):
-        self.m, self.state, self.recv, self.number = m, state, recv, 0
-
-    def begin(self):
-        m, axis = self.m, self.ORDER[self.number]
-        self.steps = range(1, 2 if axis == "c" else 4)
-        self.batch = Batch(m.links, self.recv.at[pl.ds(0, len(self.steps))])
-        for step in self.steps:
-            slot = self.recv.at[3 * self.number + step - 1]
-            self.batch.send(self.state.at[self.number], slot, moved(m.me, axis, step))
-
-    def end(self, total):
-        self.batch.wait()
-        for step in self.steps:
-            total += self.recv[3 * self.number + step - 1].astype(F32)
-        self.number += 1
-        if self.number < 4:
-            self.state[self.number] = total.astype(self.state.dtype)
-        return total
-
-    def turn(self):
-        self.end(self.state[self.number].astype(F32))
-        self.begin()
+        for group in range(16):
+            spot = tiles.at[group // 4, group % 4]
+            for number, pair in enumerate(TILE_PAIRS):
+                for side, row in enumerate(pair):
+                    value = sums[layer, row : row + 1, 48 * group : 48 * group + 48]
+                    at = 8 * layer + number
+                    spot[at : at + 1, 48 * side : 48 * side + 48] = value
+            row, start = BIAS_Q + 2 * (group // 8), 96 * (group % 8)
+            at = 8 * layer + 3
+            spot[at : at + 1, 0:96] = sums[layer, row : row + 1, start : start + 96]
+            row, start = BIAS_UP + group // 4, 192 * (group % 4)
+            for half in range(2):
+                first = start + 96 * half
+                value = sums[layer, row : row + 1, first : first + 96]
+                spot[at + 1 + half : at + 2 + half, 0:96] = value
+
+
+def own_entries(member, value, out):
+    high = value.astype(BF16)
+    middle = (value - high.astype(F32)).astype(BF16)
+    low = (value - high.astype(F32) - middle.astype(F32)).astype(BF16)
+    found = [
+        dot_nt(high, matrix) + (dot_nt(middle, matrix) + dot_nt(low, matrix))
+        for matrix in spot_matrices(member)
+    ]
+    for layer in range(LAYERS):
+        rows = slice(layer, layer + 1)
+        for number in range(6):
+            row = 8 * layer + number // 2
+            out[number][rows, :] = found[number % 2][row : row + 1, 0:6]
+        row = 8 * layer + 3
+        out[6][rows, :] = found[2][row : row + 1, 0:12]
+        up = found[3][row + 1 : row + 2] * flag(member // 4 == 0)
+        up += found[3][row + 2 : row + 3] * flag(member // 4 == 1)
+        out[7][rows, :] = up[:, 0:24]
 
 
 def kernel(*refs):
@@ -605,8 +629,8 @@
     ready, refs = refs[:12], refs[12:]
     (
         wq, wu, wd, got_qu, got_d, first, second, third, sum_q, sum_u, sum_d,
-        x0, x1, h, qkv, probs, o, mid, h2, u, tmp, g, gh, gz, cots, outs, vec, sums,
-        low_state, low_recv, stage,
+        x0, x1, x2, h, qkv, probs, o, mid, h2, u, tmp, g, gh, gz, cots, outs, vec, sums,
+        vec_out, vec_in, vec_all, stage, sum_all, sum_in, sum_next, sum_out, sum_got,
         send_a, recv_a, send_d, recv_d, asm, send_f, recv_f, send_df, recv_df,
         send_sems, recv_sems, local_sems, free,
     ) = refs
@@ -622,13 +646,12 @@
     me = place()
     sibling = moved(me, "c", 1)
     mine = 2 * me["y"] + me["c"]
-    index = ((me["z"] * 4 + me["x"]) * 4 + me["y"]) * 2 + me["c"]
     links = Links(me, send_sems, recv_sems)
     m = types.SimpleNamespace(
         me=me, links=links, weights={"q": wq, "u": wu, "d": wd}, wq=wq, wu=wu, wd=wd,
         got_qu=got_qu, got_d=got_d, free=free, totals={"q": sum_q, "u": sum_u, "d": sum_d},
         first=first, second=second, third=third,
-        x=[x0, x1, g], h=h, qkv=qkv, probs=probs, o=o, mid=mid, h2=h2, u=u, a=tmp, g=g, gh=gh, gz=gz,
+        x=[x0, x1, x2], h=h, qkv=qkv, probs=probs, o=o, mid=mid, h2=h2, u=u, a=tmp, g=g, gh=gh, gz=gz,
         gu=tmp.at[1], go=tmp.at[3], gqkv=tmp, vec=vec, sums=sums,
     )
     send_f[...] = jnp.zeros(send_f.shape, F32)
@@ -654,7 +677,7 @@
             send_df[half, 24 * layer : 24 * layer + 24, :] = part.astype(F32)
         send_d[half] = send_df[half].astype(BF16)
     narrow = (gain1, off1, bias_out, gain2, off2, bias_down)
-    spread_vectors(index, narrow, bias_qv, bias_up, stage, low_state.at[0])
+    vec_out[...] = vector_tile(mine, narrow, bias_qv, bias_up, stage)
 
     greet(me)
 
@@ -668,10 +691,19 @@
                     batch.send(spot, dst.at[mine, rows], target)
         return batch
 
-    arrivals = [group_sends(send_a, recv_a)]
+    def group_tiles(src, dst):
+        batch = Batch(links, dst.at[pl.ds(0, 7)])
+        for dy in range(4):
+            for dc in range(2):
+                if dy or dc:
+                    batch.send(src, dst.at[mine], moved(moved(me, "y", dy), "c", dc))
+        return batch
+
+    arrivals = [group_tiles(vec_out, vec_in), group_sends(send_a, recv_a)]
     arrivals.append(links.send(send_d.at[1 - me["c"]], recv_d.at[me["c"]], sibling))
     recv_a[mine] = send_a[mine]
     recv_d[me["c"]] = send_d[me["c"]]
+    vec_in[mine] = vec_out[...]
     here = pl.ds(pl.multiple_of(128 * me["c"], 128), 128)
     there = pl.ds(pl.multiple_of(128 * (1 - me["c"]), 128), 128)
     halves = []
@@ -684,77 +716,85 @@
         batch.wait()
     gathers = [Gather(kind, layer, m) for layer in range(LAYERS) for kind in KINDS]
     own = (me["y"], me["c"], me["z"], me["x"])
-    vectors = VectorSum(m, low_state, low_recv)
+    tile = jnp.zeros((16, 128), F32)
+    for source in range(8):
+        tile += vec_in[source].astype(F32)
+    vec_all[me["z"], me["x"]] = tile.astype(BF16)
+    spot = vec_all.at[me["z"], me["x"]]
+    along_z = Batch(links, vec_all.at[0, pl.ds(0, 3)])
+    for step in STEPS:
+        along_z.send(spot, spot, moved(me, "z", step))
     for layer in range(LAYERS):
         for group, target in enumerate((wq, wu)):
             for source in range(8):
                 rows = slice(16 * group + 8 * layer, 16 * group + 8 * layer + 6)
                 asm[group, 6 * source : 6 * source + 6, :] = recv_a[source].astype(F32)[rows]
             target[(layer, *own)] = asm[group].astype(BF16)
-            if layer == 0:
-                gathers[group].first()
+            gathers[3 * layer + group].first()
         for half in range(2):
             asm[2, 24 * half : 24 * half + 24, :] = recv_d[half].astype(F32)[
                 24 * layer : 24 * layer + 24
             ]
         wd[layer, me["c"], me["z"], me["x"], me["y"]] = asm[2].astype(BF16)
-        if layer == 0:
-            vectors.begin()
-            gathers[2].first()
-    gathers[0].second()
-    gathers[1].second()
-    vectors.turn()
-    gathers[0].third()
-    gathers[2].second()
-    gathers[3].first()
-    gathers[1].third()
-    vectors.turn()
-    gathers[4].first()
-    gathers[5].first()
-    gathers[0].relay()
-    vectors.turn()
-    gathers[2].third()
-    gathers[3].second()
-    gathers[0].finish()
-    gathers[4].second()
-    vec[...] = vectors.end(low_state[3].astype(F32))
-    gathers[1].relay()
-    gathers[3].third()
-    gathers[5].second()
+        gathers[3 * layer + 2].first()
+    q0, u0, d0, q1, u1, d1 = gathers
+    q0.second()
+    along_z.wait()
+    column = vec_all.at[:, me["x"]]
+    along_x = Batch(links, vec_all.at[pl.ds(0, 3)])
+    for step in STEPS:
+        along_x.send(column, column, moved(me, "x", step))
+    u0.second()
+    q0.third()
+    d0.second()
+    u0.third()
+    along_x.wait()
+    whole_vectors(vec_all, vec)
+    q1.second()
+    q0.relay()
+    d0.third()
+    u1.second()
+    d1.second()
+    q0.finish()
+    u0.relay()
+    q1.third()
     halves[0].wait()
     halves[1].wait()
-    gathers[0].arrive()
+    q0.arrive()
 
     forward_qkv(0, m)
-    gathers[1].finish()
-    gathers[2].relay()
-    gathers[4].third()
+    u0.finish()
+    d0.relay()
+    u1.third()
     forward_attention(0, m)
+    u0.arrive()
+    d0.finish()
+    q1.relay()
+    d1.third()
     forward_out(0, m)
-    gathers[2].finish()
-    gathers[3].relay()
-    gathers[5].third()
-    gathers[1].arrive()
     forward_up(0, m)
-    gathers[3].finish()
-    gathers[4].relay()
-    gathers[2].arrive()
+    d0.arrive()
     forward_down(0, m)
-    gathers[4].finish()
-    gathers[5].relay()
-    gathers[3].arrive()
-    forward_qkv(1, m)
-    gathers[5].finish()
-    forward_attention(1, m)
-    forward_out(1, m)
-    gathers[4].arrive()
-    forward_up(1, m)
-    gathers[5].arrive()
-    forward_down(1, m)
-    outs[...] = g[...].astype(BF16)
-    links.drain()
+    q1.finish()
+    u1.relay()
     halves[2].wait()
     halves[3].wait()
+    upstream(order[pl.ds(me["c"], 1), :], remaining[me["c"]], cots, m)
+    sums[...] = jnp.zeros(sums.shape, F32)
+    top(1, m)
+    q1.arrive()
+    forward_qkv(1, m)
+    u1.finish()
+    forward_attention(1, m)
+    d1.relay()
+    forward_out(1, m)
+    u1.arrive()
+    forward_up(1, m)
+    d1.finish()
+    d1.arrive()
+    forward_down(1, m)
+    outs[...] = x2[...].astype(BF16)
+    links.drain()
 
     def swap(src, dst, number):
         remote = links.send(src.at[there, :], dst.at[me["c"]], sibling)
@@ -763,8 +803,6 @@
         return remote, copy
 
     results = [swap(outs, out, 2)]
-    upstream(order[pl.ds(me["c"], 1), :], remaining[me["c"]], cots, m)
-    sums[...] = jnp.zeros(sums.shape, F32)
     scatters = {(kind, layer): Scatter(kind, layer, m) for layer in (1, 0) for kind in KINDS}
 
     def ffn(layer):
@@ -784,17 +822,21 @@
                     for group in groups:
                         group.share(part, 0)
 
+                    if layer == 0:
+
+                        @pl.when(part == 1)
+                        def _():
+                            scatters["q", 1].relay()
+
                 @pl.when(half == 1)
                 def _():
                     for group in groups:
                         group.share(2 + part, 1)
 
-                    if layer == 1:
-
-                        @pl.when(part == 0)
-                        def _():
-                            for group in groups:
-                                group.join(0)
+                    @pl.when(part == 0)
+                    def _():
+                        for group in groups:
+                            group.join(0)
 
     def attention_grads(layer):
         scatter = scatters["q", layer]
@@ -818,7 +860,6 @@
         for kind in kinds:
             getattr(scatters[kind, layer], step)(*given)
 
-    top(1, m)
     ffn(1)
     backward_mid(1, m)
     steps("join", "ud", 1, 1)
@@ -831,33 +872,49 @@
     steps("join", "q", 1, 0)
     steps("join", "q", 1, 1)
     steps("give_room", "q", 1)
+    steps("second", "ud", 1)
     ffn(0)
-    steps("second", "ud", 1)
-    steps("relay", "q", 1)
-    for half in range(2):
-        steps("join", "ud", 0, half)
+    backward_mid(0, m)
+    for kind in "ud":
+        steps("join", kind, 0, 1)
     steps("give_room", "u", 0)
-    backward_mid(0, m)
+    steps("second", "q", 1)
     steps("third", "ud", 1)
-    steps("second", "q", 1)
     backward_attention(0, m)
     steps("relay", "ud", 0)
+    steps("third", "q", 1)
     attention_grads(0)
-    steps("third", "q", 1)
     backward_in(0, m, g)
+    vector_tiles(sums, sum_all)
+    along_z = Batch(links, sum_in)
+    for step in STEPS:
+        target = moved(me, "z", step)
+        along_z.send(sum_all.at[target["z"]], sum_in.at[step - 1], target)
     results.append(swap(g, grad, 3))
-    low_state[0] = sums[...].astype(BF16)
-    for half in range(2):
-        steps("join", "q", 0, half)
-    vectors = VectorSum(m, low_state, low_recv)
-    vectors.begin()
+    steps("join", "q", 0, 0)
+    steps("join", "q", 0, 1)
     steps("second", "ud", 0)
     steps("finish", "udq", 1)
+    along_z.wait()
+    for index in range(4):
+        row = sum_all[me["z"], index]
+        for step in range(3):
+            row += sum_in[step, index]
+        sum_all[me["z"], index] = row
+    along_x = Batch(links, sum_next)
+    for step in STEPS:
+        target = moved(me, "x", step)
+        along_x.send(sum_all.at[me["z"], target["x"]], sum_next.at[step - 1], target)
     steps("relay", "q", 0)
-    vectors.turn()
     steps("third", "ud", 0)
+    along_x.wait()
+    tile = sum_all[me["z"], me["x"]]
+    for step in range(3):
+        tile += sum_next[step]
+    sum_out[...] = tile
+    last = [group_tiles(sum_out, sum_got)]
+    sum_got[mine] = tile
     steps("second", "q", 0)
-    vectors.turn()
     steps("finish", "ud", 0)
 
     def owned(total, layer, start):
@@ -872,18 +929,20 @@
             send_df[owner, 24 * layer : 24 * layer + 24, :] = sum_d[
                 layer, 24 * owner : 24 * owner + 24, :
             ]
-    last = [group_sends(send_f, recv_f, slice(8, 32))]
+    last.append(group_sends(send_f, recv_f, slice(8, 32)))
     last.append(links.send(send_df.at[1 - me["c"]], recv_df.at[me["c"]], sibling))
     recv_df[me["c"]] = send_df[me["c"]]
     steps("third", "q", 0)
-    vectors.turn()
     steps("finish", "q", 0)
     owned(sum_q, 0, 0)
     last.append(group_sends(send_f, recv_f, slice(0, 8)))
     recv_f[mine] = send_f[mine]
-    sums[...] = vectors.end(low_state[3].astype(F32))
-    own_entries(index, sums, vectors_out)
-    for batch in last:
+    last[0].wait()
+    tile = sum_got[0]
+    for source in range(1, 8):
+        tile += sum_got[source]
+    own_entries(mine, tile, vectors_out)
+    for batch in last[1:]:
         batch.wait()
     for owner in range(8):
         columns = slice(384 * (owner % 2), 384 * (owner % 2) + 384)
@@ -990,6 +1049,7 @@
             *[pltpu.VMEM((LAYERS, 48, 384), F32) for _ in range(3)],
             pltpu.VMEM((T, D), BF16),
             pltpu.VMEM((T, D), F32),
+            pltpu.VMEM((T, D), F32),
             pltpu.VMEM((LAYERS, T, D), BF16),
             pltpu.VMEM((LAYERS, 3, T, D), BF16),
             pltpu.VMEM((LAYERS, HEADS, T, T), BF16),
@@ -1005,9 +1065,15 @@
             pltpu.VMEM((T, D), BF16),
             pltpu.VMEM((LAYERS, 16, D), F32),
             pltpu.VMEM((LAYERS, 16, D), F32),
-            pltpu.VMEM((4, LAYERS, 16, D), BF16),
-            pltpu.VMEM((10, LAYERS, 16, D), BF16),
-            pltpu.VMEM((3, LAYERS, 16, 128), F32),
+            pltpu.VMEM((16, 128), BF16),
+            pltpu.VMEM((8, 16, 128), BF16),
+            pltpu.VMEM((4, 4, 16, 128), BF16),
+            pltpu.VMEM((4, 16, 128), F32),
+            pltpu.VMEM((4, 4, 16, 128), F32),
+            pltpu.VMEM((3, 4, 16, 128), F32),
+            pltpu.VMEM((3, 16, 128), F32),
+            pltpu.VMEM((16, 128), F32),
+            pltpu.VMEM((8, 16, 128), F32),
             pltpu.VMEM((8, 32, 384), BF16),
             pltpu.VMEM((8, 32, 384), BF16),
             pltpu.VMEM((2, 48, 384), BF16),
@@ -1017,8 +1083,8 @@
             pltpu.VMEM((8, 32, 384), F32),
             pltpu.VMEM((2, 48, 384), F32),
             pltpu.VMEM((2, 48, 384), F32),
-            pltpu.SemaphoreType.DMA((89,)),
-            pltpu.SemaphoreType.DMA((89,)),
+            pltpu.SemaphoreType.DMA((87,)),
+            pltpu.SemaphoreType.DMA((87,)),
             pltpu.SemaphoreType.DMA((18,)),
             pltpu.SemaphoreType.REGULAR((11,)),
         ],

time: 178 us -> 167 us (0.938)
  Pallas kernels: 177 us -> 166 us
    pallas_call x1, Pallas kernels: 174 us -> 164 us  [shards(): pl.pallas_call(kernel, out_shape=[jax.ShapeDtypeStruct(*result) for resul...]
where the time goes in v5:
time: 167 us
  Pallas kernels  166 us (99%)
    pallas_call x1, Pallas kernels, shards(): pl.pallas_call(kernel, out_shape=[jax.ShapeDtypeStruct(*result) for resul...  164 us

profile of v5, /device:TPU:1, one launch (start us, length us, event | category | flops | bytes accessed | tf_op | source)
XLA Modules:
  0.0 167.0 jit_solution(3633426498988694355)
XLA Ops:
  0.7 163.7 %layers.1 = (bf16[2,128,768]{2,1,0:T(8,128)(2,1)}, f32[2,128,768]{2,1,0:T(8,128)}, f32[6,2,2304]{2,1,0:T(2,128)}, f32[6,2,768]{2,1,0:T(2,128)}, f32[6,2,3072]{2,...) custom-call(bf16[2,128,768]{2,1,0:T(8,128)(2,1)} %refs_0_.1, ...), custom_call_target="tpu_custom_call" | custom-call | tf_op jit(solution)/shard_map/layers/pallas_call | solution.py:1033
  164.3 2.5 %deliver.1 = (bf16[2,128,768]{2,1,0:T(8,128)(2,1)}, f32[2,128,768]{2,1,0:T(8,128)}, f32[6,2,2304]{2,1,0:T(2,128)}, f32[6,2,768]{2,1,0:T(2,128)}, f32[6,2,3072]{2...) custom-call(bf16[2,128,768]{2,1,0:T(8,128)(2,1)} %get-tuple-element., ...), custom_call_target="tpu_custom_call" | custom-call | tf_op jit(solution)/shard_map/deliver/pallas_call | solution.py:998

commit v6 on v5

--- a/solution.py
+++ b/solution.py
@@ -73,10 +73,13 @@
         batch.send(src, dst, target)
         return batch
 
-    def drain(self):
-        for batch in self.open:
+    def so_far(self):
+        batches, self.open = self.open, []
+        return batches
+
+    def drain(self, batches):
+        for batch in batches:
             batch.all().wait_send()
-        self.open = []
 
 
 def greet(me):
@@ -85,7 +88,7 @@
     barrier = pltpu.get_barrier_semaphore()
     for partner in partners:
         pl.semaphore_signal(barrier, inc=1, device_id=device(partner), device_id_type=MESH)
-    pl.semaphore_wait(barrier, len(partners))
+    return len(partners)
 
 
 T = 256
@@ -247,16 +250,34 @@
         out[...] += dot(m.a[index], chunk(m.wd, layer, index))
 
 
+def forward_last(layer, m, out):
+    for core in range(2):
+        columns = slice(384 * core, 384 * core + 384)
+        value = m.mid[layer, :, columns] + m.vec[layer, BIAS_DOWN : BIAS_DOWN + 1, columns]
+        for index in range(4):
+            value += dot(m.a[index], m.wd[layer, core, index].reshape(D, 384))
+        out[:, columns] = value.astype(BF16)
+
+
+def backward_down(layer, m, index):
+    for core, ref in ((m.me["c"], m.top_down), (1 - m.me["c"], m.got_qu)):
+        columns = pl.ds(pl.multiple_of(384 * core, 128), 384)
+        value = dot_tn(m.a[index], m.gz[:, columns])
+        ref[index] = value.astype(BF16).reshape(4, 4, 48, 384)
+
+
 def backward_ffn(layer, m, index):
     grad_active = dot_nt(m.gz[...], chunk(m.wd, layer, index))
     active, slope = gelu_parts(m.u[layer, index].astype(F32))
     pre = (grad_active * slope).astype(BF16)
-    m.gu[...] = pre
-    m.a[0] = active.astype(BF16)
+    gu = m.gu[layer]
+    gu[...] = pre
     m.sums[layer, pl.ds(BIAS_UP + index, 1), :] = total(pre.astype(F32))
-    m.gh[...] += dot_nt(m.gu[...], slab(m.wu, layer, index))
-    put_chunk(m.wd, layer, index, dot_tn(m.a[0], m.gz[...]).astype(BF16))
-    put_slab(m.wu, layer, index, dot_tn(m.h2[layer], m.gu[...]).astype(BF16))
+    m.gh[...] += dot_nt(gu[...], slab(m.wu, layer, index))
+    if layer == 0:
+        m.a[0] = active.astype(BF16)
+        put_chunk(m.wd, layer, index, dot_tn(m.a[0], m.gz[...]).astype(BF16))
+    put_slab(m.wu, layer, index, dot_tn(m.h2[layer], gu[...]).astype(BF16))
 
 
 def backward_mid(layer, m):
@@ -332,7 +353,9 @@
         sizes = m.wq.at[0]
         self.handed = Batch(m.links, sizes.at[:, 0])
         self.one = Batch(m.links, sizes.at[0, 0, 0, pl.ds(0, 3)])
-        self.two = Batch(m.links, sizes.at[0, 0, pl.ds(0, 3)])
+        self.ring = (kind, layer) != ("q", 0)
+        self.two = Batch(m.links, sizes.at[0, 0, pl.ds(0, 2 if self.ring else 3)])
+        self.two_halves = Batch(m.links, sizes.at[0, 0, 0]) if self.ring else None
         self.three = Batch(m.links, sizes.at[pl.ds(0, 2), 0])
         self.halves = Batch(m.links, sizes.at[0, 0])
 
@@ -356,10 +379,18 @@
     def second(self):
         self.one.wait()
         for rows, axes in STREAMS:
-            self.out(self.two, rows, {**self.m.me, axes[0]: ALL}, axes[1], STEPS)
+            steps = (1, 3) if self.ring else STEPS
+            self.out(self.two, rows, {**self.m.me, axes[0]: ALL}, axes[1], steps)
+
+    def relay_two(self):
+        self.two.wait()
+        for rows, axes in STREAMS:
+            for step in (1, 3):
+                came = {**moved(self.m.me, axes[1], -step), axes[0]: pl.ds(step - 1, 2)}
+                self.out(self.two_halves, rows, came, axes[1], (step,))
 
     def third(self):
-        self.two.wait()
+        (self.two_halves if self.ring else self.two).wait()
         planes = [
             (rows, axes, {**self.m.me, axes[0]: ALL, axes[1]: ALL}) for rows, axes in STREAMS
         ]
@@ -409,12 +440,17 @@
         self.room, self.got = (m.free.at[9], m.got_d) if kind == "d" else (m.free.at[10], m.got_qu)
 
     def part(self, rows, at):
+        if self.kind == "d" and self.layer == 1:
+            return self.m.top_down.at[(*(at.get(axis, ALL) for axis in "zxy"), rows, ALL)]
         index = tuple(at.get(axis, ALL) for axis in AXES[self.kind])
         return self.m.weights[self.kind].at[(self.layer, *index, rows, ALL)]
 
     def share(self, index, half):
         sibling = self.m.links.sibling
-        src = self.part(ALL, {self.slow: index, "c": sibling["c"]})
+        if self.kind == "d" and self.layer == 1:
+            src = self.m.got_qu.at[index]
+        else:
+            src = self.part(ALL, {self.slow: index, "c": sibling["c"]})
         self.shared[half].send(src, self.got.at[index], sibling)
 
     def wait_room(self):
@@ -425,15 +461,15 @@
         pl.semaphore_signal(self.room, inc=1, device_id=sibling, device_id_type=MESH)
 
     def join(self, half):
-        m, me = self.m, self.m.me
         other = "x" if self.kind == "d" else "z"
         self.shared[half].wait()
 
         @pl.loop(8 * half, 8 * half + 8)
         def _(spot):
-            own = self.part(ALL, {self.slow: spot // 4, other: spot % 4, "c": me["c"]})
+            own = self.part(ALL, {self.slow: spot // 4, other: spot % 4, "c": self.m.me["c"]})
             own[...] += self.got[spot // 4, spot % 4]
 
+    def leave(self, half):
         ready = []
         for rows, axes, others, slots, _, _, free in self.streams:
             split = others[0] == self.slow
@@ -444,14 +480,14 @@
         for now in ready:
             self.pass_on(*now)
         for now in ready:
-            self.leave(*now)
+            self.go(*now)
 
     def pass_on(self, rows, axis, split, slots, half):
         me, halves = self.m.me, pl.ds(2 * half, 2)
         src = self.part(rows, {"c": me["c"], split: halves, axis: moved(me, axis, 2)[axis]})
         self.passing.send(src, slots.at[2, halves], moved(me, axis, 1 + 2 * half))
 
-    def leave(self, rows, axis, split, slots, half):
+    def go(self, rows, axis, split, slots, half):
         me, halves = self.m.me, pl.ds(2 * half, 2)
         target = moved(me, axis, 3 - 2 * half)
         src = self.part(rows, {"c": me["c"], split: halves, axis: target[axis]})
@@ -628,10 +664,10 @@
     staged, refs = refs[:14], refs[14:]
     ready, refs = refs[:12], refs[12:]
     (
-        wq, wu, wd, got_qu, got_d, first, second, third, sum_q, sum_u, sum_d,
-        x0, x1, x2, h, qkv, probs, o, mid, h2, u, tmp, g, gh, gz, cots, outs, vec, sums,
+        wq, wu, wd, got_qu, got_d, top_down, first, second, third, sum_q, sum_u, sum_d,
+        x0, x1, h, qkv, probs, o, mid, h2, u, tmp, g, gh, gz, cots, vec, sums,
         vec_out, vec_in, vec_all, stage, sum_all, sum_in, sum_next, sum_out, sum_got,
-        send_a, recv_a, send_d, recv_d, asm, send_f, recv_f, send_df, recv_df,
+        send_a, recv_a, send_d, recv_d, send_f, recv_f, send_df, recv_df,
         send_sems, recv_sems, local_sems, free,
     ) = refs
     hidden, cot = inputs[:2]
@@ -639,11 +675,12 @@
     order, remaining, w_qkv, w_out, w_up, w_down, *vectors_in = staged
     gain1, off1, bias_qv, bias_out, gain2, off2, bias_up, bias_down = vectors_in
     g_qkv, g_out, g_up, g_down, *vectors_out = ready
+    me = place()
+    partners = greet(me)
     loads = []
     for number, (src, dst) in enumerate(zip(inputs[2:], staged)):
         loads.append(pltpu.make_async_copy(src, dst, local_sems.at[4 + number]))
         loads[-1].start()
-    me = place()
     sibling = moved(me, "c", 1)
     mine = 2 * me["y"] + me["c"]
     links = Links(me, send_sems, recv_sems)
@@ -651,8 +688,8 @@
         me=me, links=links, weights={"q": wq, "u": wu, "d": wd}, wq=wq, wu=wu, wd=wd,
         got_qu=got_qu, got_d=got_d, free=free, totals={"q": sum_q, "u": sum_u, "d": sum_d},
         first=first, second=second, third=third,
-        x=[x0, x1, x2], h=h, qkv=qkv, probs=probs, o=o, mid=mid, h2=h2, u=u, a=tmp, g=g, gh=gh, gz=gz,
-        gu=tmp.at[1], go=tmp.at[3], gqkv=tmp, vec=vec, sums=sums,
+        x=[x0, x1], h=h, qkv=qkv, probs=probs, o=o, mid=mid, h2=h2, u=u, a=tmp, g=g, gh=gh, gz=gz,
+        gu=[tmp.at[1], cots], top_down=top_down, go=tmp.at[3], gqkv=tmp, vec=vec, sums=sums,
     )
     send_f[...] = jnp.zeros(send_f.shape, F32)
     for copy in loads:
@@ -679,7 +716,7 @@
     narrow = (gain1, off1, bias_out, gain2, off2, bias_down)
     vec_out[...] = vector_tile(mine, narrow, bias_qv, bias_up, stage)
 
-    greet(me)
+    pl.semaphore_wait(pltpu.get_barrier_semaphore(), partners)
 
     def group_sends(src, dst, rows=ALL):
         batch = Batch(links, dst.at[pl.ds(0, 7), rows])
@@ -724,19 +761,22 @@
     along_z = Batch(links, vec_all.at[0, pl.ds(0, 3)])
     for step in STEPS:
         along_z.send(spot, spot, moved(me, "z", step))
-    for layer in range(LAYERS):
+
+    def prepare(layer):
         for group, target in enumerate((wq, wu)):
             for source in range(8):
                 rows = slice(16 * group + 8 * layer, 16 * group + 8 * layer + 6)
-                asm[group, 6 * source : 6 * source + 6, :] = recv_a[source].astype(F32)[rows]
-            target[(layer, *own)] = asm[group].astype(BF16)
+                sum_q[group, 6 * source : 6 * source + 6, :] = recv_a[source].astype(F32)[rows]
+            target[(layer, *own)] = sum_q[group].astype(BF16)
             gathers[3 * layer + group].first()
         for half in range(2):
-            asm[2, 24 * half : 24 * half + 24, :] = recv_d[half].astype(F32)[
+            sum_d[0, 24 * half : 24 * half + 24, :] = recv_d[half].astype(F32)[
                 24 * layer : 24 * layer + 24
             ]
-        wd[layer, me["c"], me["z"], me["x"], me["y"]] = asm[2].astype(BF16)
+        wd[layer, me["c"], me["z"], me["x"], me["y"]] = sum_d[0].astype(BF16)
         gathers[3 * layer + 2].first()
+
+    prepare(0)
     q0, u0, d0, q1, u1, d1 = gathers
     q0.second()
     along_z.wait()
@@ -746,13 +786,17 @@
         along_x.send(column, column, moved(me, "x", step))
     u0.second()
     q0.third()
+    u0.relay_two()
     d0.second()
+    prepare(1)
     u0.third()
     along_x.wait()
     whole_vectors(vec_all, vec)
+    d0.relay_two()
     q1.second()
     q0.relay()
     d0.third()
+    q1.relay_two()
     u1.second()
     d1.second()
     q0.finish()
@@ -763,6 +807,8 @@
     q0.arrive()
 
     forward_qkv(0, m)
+    u1.relay_two()
+    d1.relay_two()
     u0.finish()
     d0.relay()
     u1.third()
@@ -790,11 +836,29 @@
     forward_out(1, m)
     u1.arrive()
     forward_up(1, m)
+    gathered = links.so_far()
+    scatters = {(kind, layer): Scatter(kind, layer, m) for layer in (1, 0) for kind in KINDS}
+
+    def steps(*plan):
+        for word in plan:
+            name, step, *given = word.split(".")
+            getattr(scatters[name[0], int(name[1])], step)(*map(int, given))
+
+    @pl.loop(0, 4)
+    def _(part):
+        backward_down(1, m, part)
+        for now in range(4):
+
+            @pl.when(part == now)
+            def _():
+                scatters["d", 1].share(now, now // 2)
+
     d1.finish()
+    steps("d1.join.0", "d1.leave.0", "d1.join.1", "d1.leave.1")
+    links.drain(scatters["d", 1].shared)
+    steps("u1.give_room")
     d1.arrive()
-    forward_down(1, m)
-    outs[...] = x2[...].astype(BF16)
-    links.drain()
+    links.drain(gathered)
 
     def swap(src, dst, number):
         remote = links.send(src.at[there, :], dst.at[me["c"]], sibling)
@@ -802,41 +866,21 @@
         copy.start()
         return remote, copy
 
-    results = [swap(outs, out, 2)]
-    scatters = {(kind, layer): Scatter(kind, layer, m) for layer in (1, 0) for kind in KINDS}
-
-    def ffn(layer):
-        groups = [scatters[kind, layer] for kind in "ud"]
-        if layer == 0:
-            for group in groups:
-                group.wait_room()
-
-        @pl.loop(0, 2)
-        def _(half):
-            @pl.loop(0, 2)
-            def _(part):
-                backward_ffn(layer, m, 2 * half + part)
-
-                @pl.when(half == 0)
+    def ffn(layer, *plans):
+        groups = [scatters[kind, layer] for kind in ("u" if layer else "ud")]
+        for group in groups:
+            group.wait_room()
+
+        @pl.loop(0, 4)
+        def _(part):
+            backward_ffn(layer, m, part)
+            for now in range(4):
+
+                @pl.when(part == now)
                 def _():
                     for group in groups:
-                        group.share(part, 0)
-
-                    if layer == 0:
-
-                        @pl.when(part == 1)
-                        def _():
-                            scatters["q", 1].relay()
-
-                @pl.when(half == 1)
-                def _():
-                    for group in groups:
-                        group.share(2 + part, 1)
-
-                    @pl.when(part == 0)
-                    def _():
-                        for group in groups:
-                            group.join(0)
+                        group.share(now, now // 2)
+                    steps(*plans[now])
 
     def attention_grads(layer):
         scatter = scatters["q", layer]
@@ -855,35 +899,30 @@
             @pl.when(part == 2)
             def _():
                 scatter.share(2, 1)
-
-    def steps(step, kinds, layer, *given):
-        for kind in kinds:
-            getattr(scatters[kind, layer], step)(*given)
-
-    ffn(1)
+                scatter.join(0)
+                scatter.leave(0)
+
+    ffn(1, (), (), ("u1.join.0", "u1.leave.0"), ())
+    forward_last(1, m, cots)
+    results = [swap(cots, out, 2)]
+    steps("u1.join.1", "u1.leave.1", "u1.give_room", "d1.give_room", "d1.relay")
     backward_mid(1, m)
-    steps("join", "ud", 1, 1)
-    steps("give_room", "ud", 1)
     backward_attention(1, m)
-    steps("relay", "ud", 1)
+    steps("u1.relay")
     attention_grads(1)
+    steps("d1.second")
     backward_in(1, m, g)
     top(0, m)
-    steps("join", "q", 1, 0)
-    steps("join", "q", 1, 1)
-    steps("give_room", "q", 1)
-    steps("second", "ud", 1)
-    ffn(0)
+    steps("q1.join.1", "q1.give_room", "q1.leave.1", "u1.second")
+    ffn(
+        0, (), ("d1.third",), ("q1.relay", "u0.join.0", "u0.leave.0"), ("d0.join.0", "d0.leave.0")
+    )
     backward_mid(0, m)
-    for kind in "ud":
-        steps("join", kind, 0, 1)
-    steps("give_room", "u", 0)
-    steps("second", "q", 1)
-    steps("third", "ud", 1)
+    steps("u0.join.1", "u0.leave.1", "u0.give_room", "d0.join.1", "d0.leave.1", "u1.third")
     backward_attention(0, m)
-    steps("relay", "ud", 0)
-    steps("third", "q", 1)
+    steps("q1.second", "u0.relay")
     attention_grads(0)
+    steps("d0.relay", "q0.join.1", "q0.leave.1")
     backward_in(0, m, g)
     vector_tiles(sums, sum_all)
     along_z = Batch(links, sum_in)
@@ -891,10 +930,7 @@
         target = moved(me, "z", step)
         along_z.send(sum_all.at[target["z"]], sum_in.at[step - 1], target)
     results.append(swap(g, grad, 3))
-    steps("join", "q", 0, 0)
-    steps("join", "q", 0, 1)
-    steps("second", "ud", 0)
-    steps("finish", "udq", 1)
+    steps("q1.third", "u0.second", "q0.relay", "d0.second")
     along_z.wait()
     for index in range(4):
         row = sum_all[me["z"], index]
@@ -905,62 +941,65 @@
     for step in STEPS:
         target = moved(me, "x", step)
         along_x.send(sum_all.at[me["z"], target["x"]], sum_next.at[step - 1], target)
-    steps("relay", "q", 0)
-    steps("third", "ud", 0)
+    steps("u1.finish", "d1.finish", "q1.finish")
+
+    spots = {("q", 1): 0, ("u", 1): 8, ("u", 0): 16, ("q", 0): 24}
+
+    def give_back(rows, *groups):
+        for kind, layer in groups:
+            start, total = spots[kind, layer], {"q": sum_q, "u": sum_u}[kind]
+            for owner in range(8):
+                send_f[owner, start : start + 6, :] = total[layer, 6 * owner : 6 * owner + 6, :]
+        return group_sends(send_f, recv_f, rows)
+
+    def give_back_down(layer):
+        rows = slice(24 * layer, 24 * layer + 24)
+        for owner in range(2):
+            send_df[owner, rows, :] = sum_d[layer, 24 * owner : 24 * owner + 24, :]
+        recv_df[me["c"], rows, :] = send_df[me["c"], rows, :]
+        return links.send(send_df.at[1 - me["c"], rows], recv_df.at[me["c"], rows], sibling)
+
+    def take_back(kind, layer):
+        start, wide_out = spots[kind, layer], g_up if kind == "u" else g_qkv
+        for owner in range(8):
+            columns = slice(384 * owner, 384 * owner + 384)
+            target = wide_out
+            if kind == "q" and owner >= 6:
+                columns, target = slice(384 * (owner - 6), 384 * (owner - 5)), g_out
+            for row in range(6):
+                value = recv_f[owner, start + row : start + row + 1, :]
+                target[row, layer : layer + 1, columns] = value
+
+    early = [give_back(slice(0, 16), ("q", 1), ("u", 1)), give_back_down(1)]
+    steps("q0.second", "u0.third", "d0.third")
     along_x.wait()
     tile = sum_all[me["z"], me["x"]]
     for step in range(3):
         tile += sum_next[step]
     sum_out[...] = tile
-    last = [group_tiles(sum_out, sum_got)]
+    tiles = group_tiles(sum_out, sum_got)
     sum_got[mine] = tile
-    steps("second", "q", 0)
-    steps("finish", "ud", 0)
-
-    def owned(total, layer, start):
-        for owner in range(8):
-            send_f[owner, start : start + 6, :] = total[layer, 6 * owner : 6 * owner + 6, :]
-
-    owned(sum_q, 1, 8)
-    owned(sum_u, 0, 16)
-    owned(sum_u, 1, 24)
-    for layer in range(LAYERS):
-        for owner in range(2):
-            send_df[owner, 24 * layer : 24 * layer + 24, :] = sum_d[
-                layer, 24 * owner : 24 * owner + 24, :
-            ]
-    last.append(group_sends(send_f, recv_f, slice(8, 32)))
-    last.append(links.send(send_df.at[1 - me["c"]], recv_df.at[me["c"]], sibling))
-    recv_df[me["c"]] = send_df[me["c"]]
-    steps("third", "q", 0)
-    steps("finish", "q", 0)
-    owned(sum_q, 0, 0)
-    last.append(group_sends(send_f, recv_f, slice(0, 8)))
+    steps("q0.third", "u0.finish", "d0.finish")
+    early += [give_back(slice(16, 24), ("u", 0)), give_back_down(0)]
+    steps("q0.finish")
+    last = give_back(slice(24, 32), ("q", 0))
     recv_f[mine] = send_f[mine]
-    last[0].wait()
+    tiles.wait()
     tile = sum_got[0]
     for source in range(1, 8):
         tile += sum_got[source]
     own_entries(mine, tile, vectors_out)
-    for batch in last[1:]:
+    for batch in early:
         batch.wait()
-    for owner in range(8):
-        columns = slice(384 * (owner % 2), 384 * (owner % 2) + 384)
+    for kind, layer in (("q", 1), ("u", 1), ("u", 0)):
+        take_back(kind, layer)
+    for half in range(2):
         for layer in range(LAYERS):
-            for row in range(6):
-                spot = 8 * layer + row
-                value = recv_f[owner, spot : spot + 1, :]
-                if owner < 6:
-                    g_qkv[row, layer : layer + 1, 384 * owner : 384 * owner + 384] = value
-                else:
-                    g_out[row, layer : layer + 1, columns] = value
-                value = recv_f[owner, 16 + spot : 17 + spot, :]
-                g_up[row, layer : layer + 1, 384 * owner : 384 * owner + 384] = value
-    for layer in range(LAYERS):
-        for half in range(2):
             g_down[layer, :, 384 * half : 384 * half + 384] = recv_df[
                 half, 24 * layer : 24 * layer + 24, :
             ]
+    last.wait()
+    take_back("q", 0)
     stores = []
     for number, (src, dst) in enumerate(zip(ready, outputs[2:])):
         stores.append(pltpu.make_async_copy(src, dst, local_sems.at[4 + number]))
@@ -968,7 +1007,8 @@
     for remote, copy in results:
         remote.wait()
         copy.wait()
-    links.drain()
+    links.drain([batch for batch in links.so_far() if batch not in scatters["d", 1].shared])
+    assert links.batches <= 96
     for copy in stores:
         copy.wait()
 
@@ -1043,12 +1083,12 @@
             pltpu.VMEM(deep, BF16),
             pltpu.VMEM((4, 4, 4, 48, 384), BF16),
             pltpu.VMEM((4, 4, 4, 48, 384), BF16),
+            pltpu.VMEM((4, 4, 4, 48, 384), BF16),
             pltpu.VMEM((3, 3, 3, 4, 4, 16, 384), BF16),
             pltpu.VMEM((LAYERS, 3, 3, 3, 4, 16, 384), BF16),
             pltpu.VMEM((LAYERS, 3, 3, 3, 16, 384), BF16),
             *[pltpu.VMEM((LAYERS, 48, 384), F32) for _ in range(3)],
             pltpu.VMEM((T, D), BF16),
-            pltpu.VMEM((T, D), F32),
             pltpu.VMEM((T, D), F32),
             pltpu.VMEM((LAYERS, T, D), BF16),
             pltpu.VMEM((LAYERS, 3, T, D), BF16),
@@ -1060,7 +1100,6 @@
             pltpu.VMEM((4, T, D), BF16),
             pltpu.VMEM((T, D), F32),
             pltpu.VMEM((T, D), F32),
-            pltpu.VMEM((T, D), BF16),
             pltpu.VMEM((T, D), BF16),
             pltpu.VMEM((T, D), BF16),
             pltpu.VMEM((LAYERS, 16, D), F32),
@@ -1078,13 +1117,12 @@
             pltpu.VMEM((8, 32, 384), BF16),
             pltpu.VMEM((2, 48, 384), BF16),
             pltpu.VMEM((2, 48, 384), BF16),
-            pltpu.VMEM((3, 48, 384), F32),
             pltpu.VMEM((8, 32, 384), F32),
             pltpu.VMEM((8, 32, 384), F32),
             pltpu.VMEM((2, 48, 384), F32),
             pltpu.VMEM((2, 48, 384), F32),
-            pltpu.SemaphoreType.DMA((87,)),
-            pltpu.SemaphoreType.DMA((87,)),
+            pltpu.SemaphoreType.DMA((96,)),
+            pltpu.SemaphoreType.DMA((96,)),
             pltpu.SemaphoreType.DMA((18,)),
             pltpu.SemaphoreType.REGULAR((11,)),
         ],

time: 167 us -> 158 us (0.946)
  Pallas kernels: 166 us -> 157 us
    pallas_call x1, Pallas kernels: 164 us -> 154 us  [shards(): pl.pallas_call(kernel, out_shape=[jax.ShapeDtypeStruct(*result) for resul...]
where the time goes in v6:
time: 158 us
  Pallas kernels  157 us (99%)
    pallas_call x1, Pallas kernels, shards(): pl.pallas_call(kernel, out_shape=[jax.ShapeDtypeStruct(*result) for resul...  154 us

profile of v6, /device:TPU:1, one launch (start us, length us, event | category | flops | bytes accessed | tf_op | source)
XLA Modules:
  0.0 157.5 jit_solution(13100360180156196933)
XLA Ops:
  0.7 154.1 %layers.1 = (bf16[2,128,768]{2,1,0:T(8,128)(2,1)}, f32[2,128,768]{2,1,0:T(8,128)}, f32[6,2,2304]{2,1,0:T(2,128)}, f32[6,2,768]{2,1,0:T(2,128)}, f32[6,2,3072]{2,...) custom-call(bf16[2,128,768]{2,1,0:T(8,128)(2,1)} %refs_0_.1, ...), custom_call_target="tpu_custom_call" | custom-call | tf_op jit(solution)/shard_map/layers/pallas_call | solution.py:1073
  154.8 2.5 %deliver.1 = (bf16[2,128,768]{2,1,0:T(8,128)(2,1)}, f32[2,128,768]{2,1,0:T(8,128)}, f32[6,2,2304]{2,1,0:T(2,128)}, f32[6,2,768]{2,1,0:T(2,128)}, f32[6,2,3072]{2...) custom-call(bf16[2,128,768]{2,1,0:T(8,128)(2,1)} %get-tuple-element., ...), custom_call_target="tpu_custom_call" | custom-call | tf_op jit(solution)/shard_map/deliver/pallas_call | solution.py:1038

commit v7 on v6

--- a/solution.py
+++ b/solution.py
@@ -208,7 +208,7 @@
 
 
 def forward_attention(layer, m):
-    @pl.loop(0, HEADS // 2)
+    @pl.loop(0, HEADS // 2, unroll=2)
     def _(pair):
         lanes = lanes_of(pair)
         query, keys, values = (m.qkv[layer, part, :, lanes] for part in range(3))
@@ -289,7 +289,7 @@
 
 
 def backward_attention(layer, m):
-    @pl.loop(0, HEADS // 2)
+    @pl.loop(0, HEADS // 2, unroll=2)
     def _(pair):
         lanes = lanes_of(pair)
         query, keys, values = (m.qkv[layer, part, :, lanes] for part in range(3))
@@ -695,27 +695,28 @@
     for copy in loads:
         copy.wait()
 
-    for owner in range(8):
-        columns = slice(384 * (owner % 2), 384 * (owner % 2) + 384)
-        for layer in range(LAYERS):
+    def build(layer):
+        start, rows = 16 * layer, slice(16 * layer, 16 * layer + 16)
+        for owner in range(8):
+            columns = slice(384 * (owner % 2), 384 * (owner % 2) + 384)
             for row in range(6):
                 if owner < 6:
                     part = w_qkv[row, layer : layer + 1, 384 * owner : 384 * owner + 384]
                 else:
                     part = w_out[row, layer : layer + 1, columns]
-                send_f[owner, 8 * layer + row : 8 * layer + row + 1, :] = part.astype(F32)
+                send_f[owner, start + row : start + row + 1, :] = part.astype(F32)
                 part = w_up[row, layer : layer + 1, 384 * owner : 384 * owner + 384]
-                send_f[owner, 16 + 8 * layer + row : 17 + 8 * layer + row, :] = part.astype(F32)
-    for owner in range(8):
-        send_a[owner] = send_f[owner].astype(BF16)
+                send_f[owner, start + 8 + row : start + 9 + row, :] = part.astype(F32)
+        for owner in range(8):
+            send_a[owner, rows, :] = send_f[owner, rows, :].astype(BF16)
+        recv_a[mine, rows, :] = send_a[mine, rows, :]
+
+    build(0)
     for half in range(2):
         for layer in range(LAYERS):
             part = w_down[layer, :, 384 * half : 384 * half + 384]
             send_df[half, 24 * layer : 24 * layer + 24, :] = part.astype(F32)
         send_d[half] = send_df[half].astype(BF16)
-    narrow = (gain1, off1, bias_out, gain2, off2, bias_down)
-    vec_out[...] = vector_tile(mine, narrow, bias_qv, bias_up, stage)
-
     pl.semaphore_wait(pltpu.get_barrier_semaphore(), partners)
 
     def group_sends(src, dst, rows=ALL):
@@ -736,11 +737,15 @@
                     batch.send(src, dst.at[mine], moved(moved(me, "y", dy), "c", dc))
         return batch
 
-    arrivals = [group_tiles(vec_out, vec_in), group_sends(send_a, recv_a)]
+    arrivals = [group_sends(send_a, recv_a, slice(0, 16))]
     arrivals.append(links.send(send_d.at[1 - me["c"]], recv_d.at[me["c"]], sibling))
-    recv_a[mine] = send_a[mine]
     recv_d[me["c"]] = send_d[me["c"]]
+    narrow = (gain1, off1, bias_out, gain2, off2, bias_down)
+    vec_out[...] = vector_tile(mine, narrow, bias_qv, bias_up, stage)
     vec_in[mine] = vec_out[...]
+    tiles = group_tiles(vec_out, vec_in)
+    build(1)
+    second_layer = group_sends(send_a, recv_a, slice(16, 32))
     here = pl.ds(pl.multiple_of(128 * me["c"], 128), 128)
     there = pl.ds(pl.multiple_of(128 * (1 - me["c"]), 128), 128)
     halves = []
@@ -753,6 +758,23 @@
         batch.wait()
     gathers = [Gather(kind, layer, m) for layer in range(LAYERS) for kind in KINDS]
     own = (me["y"], me["c"], me["z"], me["x"])
+
+    def prepare(layer):
+        for group, target in enumerate((wq, wu)):
+            for source in range(8):
+                rows = recv_a[source, 16 * layer : 16 * layer + 16, :].astype(F32)
+                sum_q[group, 6 * source : 6 * source + 6, :] = rows[8 * group : 8 * group + 6]
+            target[(layer, *own)] = sum_q[group].astype(BF16)
+            gathers[3 * layer + group].first()
+        for half in range(2):
+            sum_d[0, 24 * half : 24 * half + 24, :] = recv_d[half].astype(F32)[
+                24 * layer : 24 * layer + 24
+            ]
+        wd[layer, me["c"], me["z"], me["x"], me["y"]] = sum_d[0].astype(BF16)
+        gathers[3 * layer + 2].first()
+
+    prepare(0)
+    tiles.wait()
     tile = jnp.zeros((16, 128), F32)
     for source in range(8):
         tile += vec_in[source].astype(F32)
@@ -761,22 +783,6 @@
     along_z = Batch(links, vec_all.at[0, pl.ds(0, 3)])
     for step in STEPS:
         along_z.send(spot, spot, moved(me, "z", step))
-
-    def prepare(layer):
-        for group, target in enumerate((wq, wu)):
-            for source in range(8):
-                rows = slice(16 * group + 8 * layer, 16 * group + 8 * layer + 6)
-                sum_q[group, 6 * source : 6 * source + 6, :] = recv_a[source].astype(F32)[rows]
-            target[(layer, *own)] = sum_q[group].astype(BF16)
-            gathers[3 * layer + group].first()
-        for half in range(2):
-            sum_d[0, 24 * half : 24 * half + 24, :] = recv_d[half].astype(F32)[
-                24 * layer : 24 * layer + 24
-            ]
-        wd[layer, me["c"], me["z"], me["x"], me["y"]] = sum_d[0].astype(BF16)
-        gathers[3 * layer + 2].first()
-
-    prepare(0)
     q0, u0, d0, q1, u1, d1 = gathers
     q0.second()
     along_z.wait()
@@ -788,6 +794,7 @@
     q0.third()
     u0.relay_two()
     d0.second()
+    second_layer.wait()
     prepare(1)
     u0.third()
     along_x.wait()

time: 158 us -> 157 us (level)
  no operation moved by 1% of the time
where the time goes in v7:
time: 157 us
  Pallas kernels  156 us (99%)
    pallas_call x1, Pallas kernels, shards(): pl.pallas_call(kernel, out_shape=[jax.ShapeDtypeStruct(*result) for resul...  153 us

profile of v7, /device:TPU:1, one launch (start us, length us, event | category | flops | bytes accessed | tf_op | source)
XLA Modules:
  0.0 156.6 jit_solution(8828069567947639625)
XLA Ops:
  0.7 153.2 %layers.1 = (bf16[2,128,768]{2,1,0:T(8,128)(2,1)}, f32[2,128,768]{2,1,0:T(8,128)}, f32[6,2,2304]{2,1,0:T(2,128)}, f32[6,2,768]{2,1,0:T(2,128)}, f32[6,2,3072]{2,...) custom-call(bf16[2,128,768]{2,1,0:T(8,128)(2,1)} %refs_0_.1, ...), custom_call_target="tpu_custom_call" | custom-call | tf_op jit(solution)/shard_map/layers/pallas_call | solution.py:1080
  153.9 2.5 %deliver.1 = (bf16[2,128,768]{2,1,0:T(8,128)(2,1)}, f32[2,128,768]{2,1,0:T(8,128)}, f32[6,2,2304]{2,1,0:T(2,128)}, f32[6,2,768]{2,1,0:T(2,128)}, f32[6,2,3072]{2...) custom-call(bf16[2,128,768]{2,1,0:T(8,128)(2,1)} %get-tuple-element., ...), custom_call_target="tpu_custom_call" | custom-call | tf_op jit(solution)/shard_map/deliver/pallas_call | solution.py:1045
